TPU v7x, 32 devices: a whole 2x2x4 slice. The times are simulated.
32 devices in a mesh: row: 8 (over y, x, core), col: 4 (over z).
Axes of the slice: x: 2, y: 2, z: 4, core: 2. Of those that a mesh axis runs over, the one named last changes fastest.
Arguments:
- features: bfloat16 [2048, 256], P(('row', 'col')), may hold values from -6 to 6
- grad_out: bfloat16 [2048, 256], P(('row', 'col')), may hold values from -6 to 6
- relu_mask: int32 [2048, 256], P(('row', 'col')), may hold values 0 or 1
- degree: int32 [2048], P(('row', 'col')), may hold values from 1 to 16
- weight: bfloat16 [256, 256], replicated, may hold values from -0.375 to 0.375
- adjacency: bfloat16 [8, 4, 6, 128, 128], P('row', 'col'), may hold values from -0.25 to 0.25
- block_slot: int32 [8, 4, 6], P('row', 'col'), may hold values from 0 to 7, as said below
- block_count: int32 [8, 4], P('row', 'col'), may hold values from 1 to 6, as said below
Outputs:
- grad_features: float32 [2048, 256], P(('row', 'col'))
- weight_grad: float32 [256, 256], replicated
Inputs may be any that keep to these rules, and one draw needn't show every extreme that they name: `block_slot`: within one tile the positions are distinct. `block_count`: some tile uses all 6 entries.
All inputs are finite; a program needn't handle non-finite values. No bound on the sum of `relu_mask` on one device may be relied on, other than what follows from the above.
Results may differ from a plain program's by a relative error of at most 0.0075.
Values may be sent and summed in bfloat16 or wider, within the bound.
No kernel may reach another device: no remote copies, remote signals or barrier semaphores. Data moves between devices by JAX's collectives and lax.ppermute only.
A program may use at most 64 MiB of HBM per device.

v0:
```python
import math

import jax
import jax.numpy as jnp
from jax import lax
from jax.sharding import PartitionSpec as P


def block_pass(tile_blocks, source_ids, target_ids, live_count, source, target_count, transpose):
    slot_count = tile_blocks.shape[0]
    block_size = tile_blocks.shape[-1]
    feature_width = source.shape[1]
    per_turn = math.gcd(slot_count, 16)
    turn_count = slot_count // per_turn
    pieces = source.reshape(-1, block_size, feature_width)
    einsum_form = "gab,gaf->gbf" if transpose else "gab,gbf->gaf"

    def advance(running, turn_index):
        offset = turn_index * per_turn
        group_blocks = lax.dynamic_slice_in_dim(tile_blocks, offset, per_turn, 0)
        group_source = lax.dynamic_slice_in_dim(source_ids, offset, per_turn, 0)
        group_target = lax.dynamic_slice_in_dim(target_ids, offset, per_turn, 0)
        live_mask = (offset + jnp.arange(per_turn) < live_count).astype(jnp.float32)
        picked = pieces[group_source]
        products = jnp.einsum(einsum_form, group_blocks, picked, preferred_element_type=jnp.float32)
        products = products * live_mask[:, None, None]
        running = running.at[group_target].add(products)
        return (running, None)

    running, unused = lax.scan(
        advance,
        jnp.zeros((target_count, block_size, feature_width), jnp.float32),
        jnp.arange(turn_count),
    )
    return running.reshape(target_count * block_size, feature_width)


def local(features, grad_out, relu_mask, degree, weight, adjacency, block_slot, block_count):
    own_rows = features.shape[0]
    row_devices = lax.axis_size("row")
    col_devices = lax.axis_size("col")
    block_size = adjacency.shape[-1]
    row_blocks = own_rows * col_devices // block_size
    col_blocks = own_rows * row_devices // block_size
    node_scale = lax.rsqrt(degree.astype(jnp.float32))[:, None]
    masked = grad_out * relu_mask.astype(jnp.bfloat16)
    scaled_grad = (masked.astype(jnp.float32) * node_scale).astype(jnp.bfloat16)
    tile_blocks = adjacency[0, 0]
    slots = block_slot[0, 0]
    live_count = block_count[0, 0]
    block_row = slots // col_blocks
    block_col = slots % col_blocks
    grad_rows = lax.all_gather(scaled_grad, "col", axis=0, tiled=True)
    partial_value = block_pass(
        tile_blocks, block_row, block_col, live_count, grad_rows, col_blocks, True
    )
    summed = lax.psum_scatter(partial_value, "row", scatter_dimension=0, tiled=True)
    pulled = summed * node_scale
    grad_features = jnp.dot(pulled, weight.astype(jnp.float32).T, precision=lax.Precision.HIGHEST)
    scaled_feat = (features.astype(jnp.float32) * node_scale).astype(jnp.bfloat16)
    feat_cols = lax.all_gather(scaled_feat, "row", axis=0, tiled=True)
    forward = block_pass(
        tile_blocks, block_col, block_row, live_count, feat_cols, row_blocks, False
    )
    aggregated = lax.psum_scatter(forward, "col", scatter_dimension=0, tiled=True) * node_scale
    local_grad = jnp.dot(aggregated.T, masked.astype(jnp.float32), precision=lax.Precision.HIGHEST)
    node_total = own_rows * row_devices * col_devices
    weight_grad = lax.psum(local_grad, ("row", "col")) * node_total ** (-0.5)
    return (grad_features, weight_grad)


def solution(mesh):
    placed = (
        P(("row", "col"), None),
        P(("row", "col"), None),
        P(("row", "col"), None),
        P(("row", "col")),
        P(),
        P("row", "col", None, None, None),
        P("row", "col", None),
        P("row", "col"),
    )
    return jax.shard_map(
        local, mesh=mesh, in_specs=placed, out_specs=(P(("row", "col"), None), P()), check_vma=False
    )
```

profile of v0, /device:TPU:0, one launch (start us, length us, event | category | flops | bytes accessed | tf_op | source)
XLA Modules:
  0.0 193.3 jit_solution(17788219946523666126)
XLA Ops:
  8.1 0.7 and_select_fusion
  8.7 1.0 multiply_convert_fusion
  9.7 10.8 %all_gather.7 = bf16[512,256]{1,0:T(8,128)(2,1)S(1)} all-gather(bf16[64,256]{1,0:T(8,128)(2,1)S(1)} %get-tuple-element.132), channel_id=1, replica_groups=mesh['row'=8,'col'=4] {'row'}, dimensions={0}, use_global_device_ids=true | all-gather | bytes 294912 | tf_op jit(solution)/shard_map/all_gather | solution.py:61
  20.5 0.9 copy-done.3
  21.4 10.3 %while.21 = (s32[]{:T(128)}, f32[2,128,256]{2,1,0:T(8,128)S(1)}, s32[3]{0:T(128)S(1)}, s32[6]{0:T(128)S(1)}, bf16[6,128,128]{2,1,0:T(8,128)(2,1)S(1)}, /*index=5...) while((s32[]{:T(128)}, f32[2,128,256]{2,1,0:T(8,128)S(1)}, ...), condition=%wide.region_6.7_spmd, body=%wide.region_4.6_spmd.sunk | while | flops 16909336 | bytes 1512199 | solution.py:30
  21.4 0.6 dynamic_slice.44
  22.6 0.1 compare_select_fusion.10
  22.7 0.6 gather_fusion.1
  23.3 0.7 compare_convert_fusion.5
  24.0 0.2 convolution_multiply_fusion.5
  24.1 0.7 scatter_fusion.1
  24.8 0.6 dynamic_slice.44
  26.1 0.1 compare_select_fusion.10
  26.2 0.6 gather_fusion.1
  26.7 0.7 compare_convert_fusion.5
  27.4 0.2 convolution_multiply_fusion.5
  27.6 0.7 scatter_fusion.1
  28.3 0.6 dynamic_slice.44
  29.6 0.6 gather_fusion.1
  30.2 0.7 compare_convert_fusion.5
  30.8 0.2 convolution_multiply_fusion.5
  31.0 0.7 scatter_fusion.1
  31.7 0.7 copy-done.1
  32.5 14.1 %all_gather.6 = bf16[256,256]{1,0:T(8,128)(2,1)S(1)} all-gather(bf16[64,256]{1,0:T(8,128)(2,1)S(1)} %get-tuple-element.133), channel_id=1, replica_groups=mesh['row'=8,'col'=4] {'col'}, dimensions={0}, use_global_device_ids=true | all-gather | bytes 163840 | tf_op jit(solution)/shard_map/all_gather | solution.py:53
  46.6 6.7 %reduce-scatter.5.cloned.1.call-done = f32[64,256]{1,0:T(8,128)} async-done(((f32[256,256]{1,0:T(8,128)}), f32[64,256]{1,0:T(8,128)}) %reduce-scatter.5.cloned.1.call-update) | async-done | bytes 65552 | tf_op jit(solution)/shard_map/reduce_scatter | solution.py:65
  53.3 1.9 fusion.4
  55.4 10.3 %while.20 = (s32[]{:T(128)}, f32[4,128,256]{2,1,0:T(8,128)S(1)}, s32[3]{0:T(128)S(1)}, s32[6]{0:T(128)S(1)}, bf16[6,128,128]{2,1,0:T(8,128)(2,1)S(1)}, /*index=5...) while((s32[]{:T(128)}, f32[4,128,256]{2,1,0:T(8,128)S(1)}, ...), condition=%wide.region_2.3_spmd, body=%wide.region_0.2_spmd.sunk | while | flops 16909336 | bytes 1512199 | solution.py:30
  55.4 0.6 dynamic_slice.41
  56.6 0.6 gather_fusion
  57.2 0.7 compare_convert_fusion.4
  57.8 0.2 convolution_multiply_fusion.4
  58.1 0.7 scatter_fusion
  58.8 0.6 dynamic_slice.41
  60.0 0.1 compare_select_fusion.9
  60.0 0.6 gather_fusion
  60.6 0.7 compare_convert_fusion.4
  61.3 0.2 convolution_multiply_fusion.4
  61.5 0.7 scatter_fusion
  62.2 0.6 dynamic_slice.41
  63.4 0.1 compare_select_fusion.9
  63.5 0.6 gather_fusion
  64.0 0.7 compare_convert_fusion.4
  64.7 0.2 convolution_multiply_fusion.4
  64.9 0.7 scatter_fusion
  65.6 0.8 copy-done.2
  66.4 116.0 %all-reduce.2.cloned.1.call-done = f32[256,256]{1,0:T(8,128)} async-done(((f32[256,256]{1,0:T(8,128)}), f32[256,256]{1,0:T(8,128)}) %all-reduce.2.cloned.1.call-update) | async-done | bytes 262160 | tf_op jit(solution)/shard_map/psum | solution.py:68
  182.4 1.7 broadcast_multiply_fusion
  184.1 1.8 fusion.6
  (31 shorter events, 0.5 us)
Async XLA Ops:
  8.0 176.1 %copy-start = (bf16[256,256]{1,0:T(8,128)(2,1)S(1)}, bf16[256,256]{1,0:T(8,128)(2,1)}, u32[]{:S(2)}) copy-start(bf16[256,256]{1,0:T(8,128)(2,1)} %param.16) | copy-start | bytes 393220
  8.0 0.7 copy-start.6
  8.0 45.3 %reduce-scatter.5.cloned.1.call-start = ((), (), s32[]{:S(2)}) async-start(), calls=%async_computation.3 | async-start | bytes 327680 | tf_op jit(solution)/shard_map/reduce_scatter | solution.py:65
  20.5 0.9 copy-start.3
  31.7 0.7 copy-start.1
  32.5 149.9 %all-reduce.2.cloned.1.call-start = ((), (), s32[]{:S(2)}) async-start(), calls=%async_computation.4 | async-start | bytes 524288 | tf_op jit(solution)/shard_map/psum | solution.py:68
  32.5 20.8 %copy-start.4 = (s32[64,256]{1,0:T(8,128)S(1)}, s32[64,256]{1,0:T(8,128)}, u32[]{:S(2)}) copy-start(s32[64,256]{1,0:T(8,128)} %param.14) | copy-start | bytes 196612
  32.5 20.8 %copy-start.5 = (bf16[64,256]{1,0:T(8,128)(2,1)S(1)}, bf16[64,256]{1,0:T(8,128)(2,1)}, u32[]{:S(2)}) copy-start(bf16[64,256]{1,0:T(8,128)(2,1)} %param.13) | copy-start | bytes 98308
  55.3 128.8 %reduce-scatter.3.cloned.1.call-start = ((), (), s32[]{:S(2)}) async-start(), calls=%async_computation.2 | async-start | bytes 589824 | tf_op jit(solution)/shard_map/reduce_scatter | solution.py:57
  65.6 0.8 copy-start.2
Sparse Core Ops, SparseCore 0:
  32.6 20.6 reduce-scatter.4
  59.4 122.9 all-reduce.1
Sparse Core Ops, SparseCore 1:
  66.5 32.1 reduce-scatter.2
where the time goes:
time: 194 us; the launch traced here: 193 us
  waiting for transfers between devices  123 us (63%)
  blocking collectives  24.8 us (13%)
  between operations  15.6 us (8%)
  other arithmetic  11.9 us (6%)
  local copies, waits for them, and re-layouts  9.29 us (5%)
  matrix products  4.9 us (3%)
  loops' own time  3.95 us (2%)
    psum x1, waiting for transfers between devices, local(): weight_grad = lax.psum(local_grad, ('row', 'col')) * node_total ** (-0.5)  116 us
    all_gather x1, blocking collectives, local(): grad_rows = lax.all_gather(scaled_grad, 'col', axis=0, tiled=True)  14.1 us
    all_gather x1, blocking collectives, local(): feat_cols = lax.all_gather(scaled_feat, 'row', axis=0, tiled=True)  10.8 us
    reduce_scatter x1, waiting for transfers between devices, local(): lax.psum_scatter(forward, 'col', scatter_dimension=0, tiled=True)  6.71 us
    scatter-add x6, other arithmetic, advance(): running = running.at[group_target].add(products)  4.15 us
    another operation x2, loops' own time, block_pass(): lax.scan(advance, jnp.zeros((target_count, block_size, feature_width), jn...  3.95 us
    convert_element_type x6, other arithmetic, advance(): live_mask = (offset + jnp.arange(per_turn) < live_count).astype(jnp.float32)  3.91 us
  transfers between devices with their start and end apart: 3, of which 2 were waited for; matrix products, arithmetic and copies ran while one was open for 5% of the time, Pallas kernels for 0%

commit v1 on v0

v1 whole, which is shorter than its diff:
```python
import functools

import jax
import jax.numpy as jnp
from jax import lax
from jax.experimental import pallas as pl
from jax.experimental.pallas import tpu as pltpu
from jax.sharding import PartitionSpec as P

VMEM = pltpu.VMEM
SMEM = pltpu.SMEM
CORES = 2


def positions():
    row = lax.axis_index("row")
    return row // CORES, row % CORES, lax.axis_index("col")


def call(body, outs, ins, spaces=None, limit=8 * 2**20, flops=0):
    spaces = spaces or [VMEM] * len(ins)
    moved = sum(x.size * x.dtype.itemsize for x in list(ins) + list(outs))
    return pl.pallas_call(
        body,
        out_shape=outs,
        in_specs=[pl.BlockSpec(memory_space=s) for s in spaces],
        out_specs=[pl.BlockSpec(memory_space=VMEM) for _ in outs],
        compiler_params=pltpu.CompilerParams(vmem_limit_bytes=limit),
        cost_estimate=pl.CostEstimate(flops=flops, bytes_accessed=moved, transcendentals=0),
    )(*ins)


def pair_up(sg, sf, other, gpair, xpair):
    nodes, width = sg.shape
    half = width // CORES
    core = positions()[1]
    columns = pl.ds(pl.multiple_of(core * half, half), half)
    gpair[:nodes] = sg[...]
    gpair[nodes:] = other[:nodes]
    xpair[:nodes] = sf[:, columns]
    xpair[nodes:] = other[nodes:, columns]


def lay_out(nodes, own, theirs, own_slot, their_slot, own_count, their_count, dense):
    block = own.shape[-1]
    per_block = block // nodes
    chip, core, col = positions()
    col_blocks = dense.shape[0] // block
    dense[...] = jnp.zeros_like(dense)
    for p, (blocks, slots, count) in enumerate(
        ((own, own_slot, own_count), (theirs, their_slot, their_count))
    ):
        @pl.loop(0, count[0, 0])
        def place(b):
            slot = slots[0, 0, b]
            source = (slot // col_blocks) ^ (col // per_block)
            target = (slot % col_blocks) ^ chip
            value = blocks[0, 0, b]
            swapped = jnp.concatenate([value[nodes:], value[:nodes]], axis=0)
            value = jnp.where(col % per_block == 1, swapped, value).T
            swapped = jnp.concatenate([value[nodes:], value[:nodes]], axis=0)
            value = jnp.where(core == 1, swapped, value)
            rows = pl.ds(pl.multiple_of(target * block, block), block)
            columns = pl.ds(pl.multiple_of((source * CORES + p) * block, block), block)
            dense[rows, columns] = value


def multiply(nodes, chips, cols, refs):
    dense = refs[0]
    grads = refs[1 : 1 + cols]
    feats = refs[1 + cols : 1 + cols + chips]
    pulled = refs[1 + cols + chips]
    weighted = refs[2 + cols + chips]
    sends = refs[3 + cols + chips :]
    per_block = 2
    order = [
        grads[per_block * kh + kl][p * nodes : (p + 1) * nodes]
        for kh in range(cols // per_block)
        for p in range(CORES)
        for kl in range(per_block)
    ]
    gathered = jnp.concatenate(order, axis=0)
    total = jnp.dot(dense[...], gathered, preferred_element_type=jnp.float32)
    features = jnp.concatenate([f[...] for f in feats], axis=0)
    high = total.astype(jnp.bfloat16)
    low = (total - high.astype(jnp.float32)).astype(jnp.bfloat16)
    rows = (((0,), (0,)), ((), ()))
    part = lax.dot_general(features, high, rows, preferred_element_type=jnp.float32)
    part = part + lax.dot_general(features, low, rows, preferred_element_type=jnp.float32)
    part = part.astype(jnp.bfloat16)
    pulled[...] = total[:nodes]
    weighted[...] = part
    for k, send in enumerate(sends, 1):
        at = k * CORES * nodes
        send[:nodes] = high[at : at + nodes]
        send[nodes:] = part


def tree(terms):
    while len(terms) > 1:
        terms = [a + b for a, b in zip(terms[::2], terms[1::2])]
    return terms[0]


def sum_chips(nodes, weighted, *refs):
    received, out = refs[:-1], refs[-1]
    terms = [weighted[...].astype(jnp.float32)]
    terms += [r[nodes:].astype(jnp.float32) for r in received]
    out[...] = tree(terms).astype(jnp.bfloat16)


def finish_features(nodes, pulled, scale, weight, *refs):
    received, out = refs[:-1], refs[-1]
    total = tree([pulled[...]] + [r[:nodes].astype(jnp.float32) for r in received])
    total = total * scale[...]
    high = total.astype(jnp.bfloat16)
    low = (total - high.astype(jnp.float32)).astype(jnp.bfloat16)
    last = (((1,), (1,)), ((), ()))
    w = weight[...]
    out[...] = lax.dot_general(high, w, last, preferred_element_type=jnp.float32)
    out[...] += lax.dot_general(low, w, last, preferred_element_type=jnp.float32)


def sum_cols(factor, *refs):
    terms, out = refs[:-1], refs[-1]
    out[...] = tree([t[...].astype(jnp.float32) for t in terms]) * factor


def join(own, other, out):
    half = own.shape[0]
    core = positions()[1]
    out[pl.ds(pl.multiple_of(core * half, half), half)] = own[...]
    out[pl.ds(pl.multiple_of((1 - core) * half, half), half)] = other[...]


def local(features, grad_out, relu_mask, degree, weight, adjacency, block_slot, block_count):
    nodes, width = features.shape
    rows = lax.axis_size("row")
    cols = lax.axis_size("col")
    chips = rows // CORES
    block = adjacency.shape[-1]
    half = width // CORES
    bf16, f32 = jnp.bfloat16, jnp.float32
    shape = jax.ShapeDtypeStruct

    def swap(x, axis, size, k):
        return lax.ppermute(x, axis, [(d, d ^ k) for d in range(size)])

    their_blocks = swap(adjacency, "row", rows, 1)
    their_slot = swap(block_slot, "row", rows, 1)
    their_count = swap(block_count, "row", rows, 1)
    scale = lax.rsqrt(degree.astype(f32))[:, None]
    masked = grad_out * relu_mask.astype(bf16)
    scaled_grad = (masked.astype(f32) * scale).astype(bf16)
    scaled_feat = (features.astype(f32) * scale).astype(bf16)
    other = swap(jnp.concatenate([scaled_grad, scaled_feat], axis=0), "row", rows, 1)
    gpair, xpair = call(
        pair_up,
        [shape((CORES * nodes, width), bf16), shape((CORES * nodes, half), bf16)],
        [scaled_grad, scaled_feat, other],
    )
    grads = [gpair] + [swap(gpair, "col", cols, k) for k in range(1, cols)]
    feats = [xpair] + [swap(xpair, "row", rows, CORES * k) for k in range(1, chips)]

    targets, sources = rows * nodes, CORES * cols * nodes
    size = targets * sources * 2
    (dense,) = call(
        functools.partial(lay_out, nodes),
        [shape((targets, sources), bf16)],
        [adjacency, their_blocks, block_slot, their_slot, block_count, their_count],
        [VMEM, VMEM, SMEM, SMEM, SMEM, SMEM],
        limit=8 * 2**20 + 3 * size,
    )
    out = call(
        lambda *refs: multiply(nodes, chips, cols, refs),
        [shape((nodes, width), f32), shape((half, width), bf16)]
        + [shape((nodes + half, width), bf16)] * (chips - 1),
        [dense] + grads + feats,
        limit=8 * 2**20 + 3 * size,
        flops=2 * targets * sources * width + 4 * targets * half * width,
    )
    pulled, weighted, sends = out[0], out[1], out[2:]
    received = [swap(s, "row", rows, CORES * k) for k, s in enumerate(sends, 1)]
    (plane,) = call(
        functools.partial(sum_chips, nodes), [shape((half, width), bf16)], [weighted] + received
    )
    planes = [plane] + [swap(plane, "col", cols, k) for k in range(1, cols)]
    (grad_features,) = call(
        functools.partial(finish_features, nodes),
        [shape((nodes, width), f32)],
        [pulled, scale, weight] + received,
        flops=4 * nodes * width * width,
    )
    factor = (nodes * rows * cols) ** (-0.5)
    (own_half,) = call(functools.partial(sum_cols, factor), [shape((half, width), f32)], planes)
    other_half = swap(own_half, "row", rows, 1)
    (weight_grad,) = call(join, [shape((width, width), f32)], [own_half, other_half])
    return grad_features, weight_grad


def solution(mesh):
    placed = (
        P(("row", "col"), None),
        P(("row", "col"), None),
        P(("row", "col"), None),
        P(("row", "col")),
        P(),
        P("row", "col", None, None, None),
        P("row", "col", None),
        P("row", "col"),
    )
    return jax.shard_map(
        local, mesh=mesh, in_specs=placed, out_specs=(P(("row", "col"), None), P()), check_vma=False
    )
```

time: 194 us -> 37.6 us (0.19)
  waiting for transfers between devices: 123 us -> 11.8 us
  blocking collectives: 24.8 us -> 0 us
  starting transfers between devices: 0.12 us -> 18.2 us
  between operations: 15.6 us -> 1.38 us
  other arithmetic: 11.9 us -> 1.66 us
  local copies, waits for them, and re-layouts: 9.29 us -> 0.62 us
  matrix products: 4.9 us -> 0 us
  loops' own time: 3.95 us -> 0 us
  Pallas kernels: 0 us -> 3.82 us
    psum x1 -> x0, waiting for transfers between devices: 116 us -> none  [local(): weight_grad = lax.psum(local_grad, ('row', 'col')) * node_total ** (-0.5)]
    all_gather x2 -> x0, blocking collectives: 24.8 us -> none  [the longest x1 14.1 us: local(): grad_rows = lax.all_gather(scaled_grad, 'col', axis=0, tiled=True)]
    ppermute x0 -> x17, starting transfers between devices: none -> 18.2 us  [swap(): return lax.ppermute(x, axis, [(d, d ^ k) for d in range(size)])]
    ppermute x0 -> x17, waiting for transfers between devices: none -> 11.8 us  [swap(): return lax.ppermute(x, axis, [(d, d ^ k) for d in range(size)])]
    reduce_scatter x2 -> x0, waiting for transfers between devices: 6.71 us -> none  [the longest x1 6.71 us: local(): lax.psum_scatter(forward, 'col', scatter_dimension=0, tiled=True)]
    dot_general x8 -> x0, matrix products: 4.9 us -> none  [the longest x1 1.93 us: local(): jnp.dot(aggregated.T, masked.astype(jnp.float32), precision=lax.Precision...]
    scatter-add x6 -> x0, other arithmetic: 4.15 us -> none  [advance(): running = running.at[group_target].add(products)]
    another operation x2 -> x0, loops' own time: 3.95 us -> none  [block_pass(): lax.scan(advance, jnp.zeros((target_count, block_size, feature_width), jn...]
  transfers between devices with their start and end apart: 3 -> 17, of which waited for: 2 -> 8; matrix products, arithmetic and copies ran while one was open for 5% -> 5% of each run, Pallas kernels for 0% -> 6%
where the time goes in v1:
time: 37.6 us; the launch traced here: 37.5 us
  starting transfers between devices  18.2 us (48%)
  waiting for transfers between devices  11.8 us (31%)
  Pallas kernels  3.82 us (10%)
  other arithmetic  1.66 us (4%)
  between operations  1.38 us (4%)
  local copies, waits for them, and re-layouts  0.62 us (2%)
    ppermute x17, starting transfers between devices, swap(): return lax.ppermute(x, axis, [(d, d ^ k) for d in range(size)])  18.2 us
    ppermute x17, waiting for transfers between devices, swap(): return lax.ppermute(x, axis, [(d, d ^ k) for d in range(size)])  11.8 us
    pallas_call x7, Pallas kernels, call(): pl.pallas_call(body, out_shape=outs, in_specs=[pl.BlockSpec(memory_space=...  3.82 us
    convert_element_type x1, other arithmetic, local(): scaled_feat = (features.astype(f32) * scale).astype(bf16)  1 us
  transfers between devices with their start and end apart: 17, of which 8 were waited for; matrix products, arithmetic and copies ran while one was open for 5% of the time, Pallas kernels for 6%

profile of v1, /device:TPU:0, one launch (start us, length us, event | category | flops | bytes accessed | tf_op | source)
XLA Modules:
  0.0 37.5 jit_solution(10318036305006737885)
XLA Ops:
  0.6 0.5 %collective-permute-start = (bf16[1,1,6,128,128]{4,3,2,1,0:T(8,128)(2,1)}, bf16[1,1,6,128,128]{4,3,2,1,0:T(8,128)(2,1)S(1)}, u32[]{:S(2)}, u32[]{:S(2)}) collective-permute-start(bf16[1,1,6,128,128]{4,3,2,1,0:T(8,128)(2,1)} %own.1), channel_id=1, source_target_pairs={{0,4},{4,0},{8,12},{12,8},{16,20},{20,16},{24,28},{28,24},{1,5},{5... | collective-permute-start | bytes 589832 | tf_op jit(solution)/shard_map/ppermute | solution.py:147
  1.1 0.7 %fusion = (f32[64,1]{0,1:T(1,128)S(1)}, f32[64]{0:T(128)S(1)}) fusion(s32[64]{0:T(128)} %param.11), kind=kLoop, calls=%fused_computation.4 | loop fusion | flops 64 | bytes 768 | tf_op jit(solution)/shard_map/broadcast_in_dim | solution.py:152
  1.8 0.0 copy-start
  1.8 1.0 %multiply_convert_fusion = (bf16[64,256]{1,0:T(8,128)(2,1)S(1)}, bf16[64,256]{1,0:T(8,128)(2,1)S(1)}) fusion(bf16[64,256]{1,0:T(8,128)(2,1)} %param.8, f32[64]{0:T(128)S(1)} %get-tuple-element.17, bf16[64,256]{1,0:T(8,128)(2,1)} %param.9, s32[64,256]{1,0:T(8,128)} %param.10), kind=kLoop, calls=%fused_computation.1 | loop fusion | flops 131072 | bytes 196864 | tf_op jit(solution)/shard_map/convert_element_type | solution.py:155
  2.8 0.0 copy-start.2
  2.8 0.1 collective-permute-start.3
  3.0 0.5 %copy-done.2 = s32[1,1,6]{2,1,0:T(1,128)S(1)} copy-done((s32[1,1,6]{2,1,0:T(1,128)S(1)}, s32[1,1,6]{2,1,0:T(1,128)}, u32[]{:S(2)}) %copy-start.2) | copy-done | bytes 48
  3.5 0.1 collective-permute-start.1
  3.5 0.5 %collective-permute-start.2 = (s32[1,1]{1,0:T(1,128)}, s32[1,1]{1,0:T(1,128)}, u32[]{:S(2)}, u32[]{:S(2)}) collective-permute-start(s32[1,1]{1,0:T(1,128)} %param.15), channel_id=1, source_target_pairs={{0,4},{4,0},{8,12},{12,8},{16,20},{20,16},{24,28},{28,24},{1,5},{5... | collective-permute-start | bytes 20 | tf_op jit(solution)/shard_map/ppermute | solution.py:147
  4.0 0.2 collective-permute-done.3.other
  4.2 2.7 %collective-permute-start.7 = (bf16[128,128]{1,0:T(8,128)(2,1)S(1)}, bf16[128,128]{1,0:T(8,128)(2,1)S(1)}, u32[]{:S(2)}, u32[]{:S(2)}) collective-permute-start(bf16[128,128]{1,0:T(8,128)(2,1)S(1)} %get-tuple-element.10.refs_5_), channel_id=1, source_target_pairs={{0,8},{4,12},{8,0},{12,4},{16,24},{20,28},{24,16},{28,20},{1,9},{5... | collective-permute-start | bytes 98312 | tf_op jit(solution)/shard_map/ppermute | solution.py:147
  6.9 1.6 %collective-permute-start.4 = (bf16[128,256]{1,0:T(8,128)(2,1)S(1)}, bf16[128,256]{1,0:T(8,128)(2,1)S(1)}, u32[]{:S(2)}, u32[]{:S(2)}) collective-permute-start(bf16[128,256]{1,0:T(8,128)(2,1)S(1)} %get-tuple-element.9.refs_1_), channel_id=1, source_target_pairs={{0,1},{1,0},{2,3},{3,2},{4,5},{5,4},{6,7},{7,6},{8,9},{9,8},{10,11... | collective-permute-start | bytes 196616 | tf_op jit(solution)/shard_map/ppermute | solution.py:147
  8.5 0.0 collective-permute-done.2.their_count
  8.5 2.6 %collective-permute-start.5 = (bf16[128,256]{1,0:T(8,128)(2,1)S(1)}, bf16[128,256]{1,0:T(8,128)(2,1)S(1)}, u32[]{:S(2)}, u32[]{:S(2)}) collective-permute-start(bf16[128,256]{1,0:T(8,128)(2,1)S(1)} %get-tuple-element.9.refs_1_), channel_id=1, source_target_pairs={{0,2},{1,3},{2,0},{3,1},{4,6},{5,7},{6,4},{7,5},{8,10},{9,11},{10,... | collective-permute-start | bytes 196616 | tf_op jit(solution)/shard_map/ppermute | solution.py:147
  11.1 0.0 collective-permute-done.1.their_slot
  11.1 0.2 collective-permute-start.6
  11.3 0.0 collective-permute-done.7.refs_6_
  11.3 1.5 %collective-permute-start.8 = (bf16[128,128]{1,0:T(8,128)(2,1)S(1)}, bf16[128,128]{1,0:T(8,128)(2,1)S(1)}, u32[]{:S(2)}, u32[]{:S(2)}) collective-permute-start(bf16[128,128]{1,0:T(8,128)(2,1)S(1)} %get-tuple-element.10.refs_5_), channel_id=1, source_target_pairs={{0,16},{4,20},{8,24},{12,28},{16,0},{20,4},{24,8},{28,12},{1,17},{... | collective-permute-start | bytes 98312 | tf_op jit(solution)/shard_map/ppermute | solution.py:147
  12.8 0.0 collective-permute-done.theirs
  12.8 0.3 collective-permute-start.9
  13.8 0.0 copy-done
  13.8 1.6 %shard_map.95.refs_0_ = bf16[512,512]{1,0:T(8,128)(2,1)S(1)} custom-call(bf16[1,1,6,128,128]{4,3,2,1,0:T(8,128)(2,1)S(1)} %copy-done, bf16[1,1,6,128,128]{4,3,2,1,0:T(8,128)(2,1)S(1)} %collective-permute-done.theirs, s32[1,1,6]{2,1,0:T(1,128)S(1)} %copy-done.2, s32[1,1,6]{2,1,0:T(1,128)S(1)} %collective-permute-done.1.their_slot, ...), custom_call_target="tpu_custom_call" | custom-call | bytes 917560 | tf_op jit(solution)/shard_map/pallas_call | solution.py:23
  15.4 0.0 collective-permute-done.8.refs_7_
  15.4 2.2 %collective-permute-done.9.refs_8_ = bf16[128,128]{1,0:T(8,128)(2,1)S(1)} collective-permute-done((bf16[128,128]{1,0:T(8,128)(2,1)S(1)}, bf16[128,128]{1,0:T(8,128)(2,1)S(1)}, u32[]{:S(2)}, u32[]{:S(2)}) %collective-permute-start.9) | collective-permute-done | bytes 32800 | tf_op jit(solution)/shard_map/ppermute | solution.py:147
  17.6 0.0 collective-permute-done.4.refs_2_
  17.6 0.0 collective-permute-done.5.refs_3_
  17.6 0.0 collective-permute-done.6.refs_4_
  17.6 0.6 %shard_map.97 = (f32[64,256]{1,0:T(8,128)S(1)}, bf16[128,256]{1,0:T(8,128)(2,1)S(1)}, bf16[192,256]{1,0:T(8,128)(2,1)S(1)}, bf16[192,256]{1,0:T(8,128)(2,1)S(1)}, bf16[192,256]{1,0:T(8,128)(2,1)S(1)}) custom-call(bf16[512,512]{1,0:T(8,128)(2,1)S(1)} %shard_map.95.refs_0_, bf16[128,256]{1,0:T(8,128)(2,1)S(1)} %get-tuple-element.9.refs_1_, ...), custom_call_target="tpu_custom_call" | custom-call | flops 201326592 | bytes 1343488 | tf_op jit(solution)/shard_map/pallas_call | solution.py:23
  18.2 0.6 %collective-permute-start.10 = (bf16[192,256]{1,0:T(8,128)(2,1)S(1)}, bf16[192,256]{1,0:T(8,128)(2,1)S(1)}, u32[]{:S(2)}, u32[]{:S(2)}) collective-permute-start(bf16[192,256]{1,0:T(8,128)(2,1)S(1)} %get-tuple-element.12), channel_id=1, source_target_pairs={{0,8},{4,12},{8,0},{12,4},{16,24},{20,28},{24,16},{28,20},{1,9},{5... | collective-permute-start | bytes 294920 | tf_op jit(solution)/shard_map/ppermute | solution.py:147
  18.8 1.1 %collective-permute-start.11 = (bf16[192,256]{1,0:T(8,128)(2,1)S(1)}, bf16[192,256]{1,0:T(8,128)(2,1)S(1)}, u32[]{:S(2)}, u32[]{:S(2)}) collective-permute-start(bf16[192,256]{1,0:T(8,128)(2,1)S(1)} %get-tuple-element.13), channel_id=1, source_target_pairs={{0,16},{4,20},{8,24},{12,28},{16,0},{20,4},{24,8},{28,12},{1,17},{... | collective-permute-start | bytes 294920 | tf_op jit(solution)/shard_map/ppermute | solution.py:147
  19.9 1.8 %collective-permute-start.12 = (bf16[192,256]{1,0:T(8,128)(2,1)S(1)}, bf16[192,256]{1,0:T(8,128)(2,1)S(1)}, u32[]{:S(2)}, u32[]{:S(2)}) collective-permute-start(bf16[192,256]{1,0:T(8,128)(2,1)S(1)} %get-tuple-element.14), channel_id=1, source_target_pairs={{0,24},{4,28},{8,16},{12,20},{16,8},{20,12},{24,0},{28,4},{1,25},{... | collective-permute-start | bytes 294920 | tf_op jit(solution)/shard_map/ppermute | solution.py:147
  21.8 1.1 %collective-permute-done.10.refs_0_ = bf16[192,256]{1,0:T(8,128)(2,1)S(1)} collective-permute-done((bf16[192,256]{1,0:T(8,128)(2,1)S(1)}, bf16[192,256]{1,0:T(8,128)(2,1)S(1)}, u32[]{:S(2)}, u32[]{:S(2)}) %collective-permute-start.10) | collective-permute-done | bytes 98336 | tf_op jit(solution)/shard_map/ppermute | solution.py:147
  22.9 0.5 %collective-permute-done.11.refs_1_ = bf16[192,256]{1,0:T(8,128)(2,1)S(1)} collective-permute-done((bf16[192,256]{1,0:T(8,128)(2,1)S(1)}, bf16[192,256]{1,0:T(8,128)(2,1)S(1)}, u32[]{:S(2)}, u32[]{:S(2)}) %collective-permute-start.11) | collective-permute-done | bytes 98336 | tf_op jit(solution)/shard_map/ppermute | solution.py:147
  23.5 2.0 %collective-permute-done.12.refs_2_ = bf16[192,256]{1,0:T(8,128)(2,1)S(1)} collective-permute-done((bf16[192,256]{1,0:T(8,128)(2,1)S(1)}, bf16[192,256]{1,0:T(8,128)(2,1)S(1)}, u32[]{:S(2)}, u32[]{:S(2)}) %collective-permute-start.12) | collective-permute-done | bytes 98336 | tf_op jit(solution)/shard_map/ppermute | solution.py:147
  25.5 0.0 copy-start.1
  25.5 0.8 %collective-permute-start.13 = (bf16[128,256]{1,0:T(8,128)(2,1)S(1)}, bf16[128,256]{1,0:T(8,128)(2,1)S(1)}, u32[]{:S(2)}, u32[]{:S(2)}) collective-permute-start(bf16[128,256]{1,0:T(8,128)(2,1)S(1)} %shard_map.99.refs_0_), channel_id=1, source_target_pairs={{0,1},{1,0},{2,3},{3,2},{4,5},{5,4},{6,7},{7,6},{8,9},{9,8},{10,11... | collective-permute-start | bytes 196616 | tf_op jit(solution)/shard_map/ppermute | solution.py:147
  26.3 2.9 %collective-permute-start.14 = (bf16[128,256]{1,0:T(8,128)(2,1)S(1)}, bf16[128,256]{1,0:T(8,128)(2,1)S(1)}, u32[]{:S(2)}, u32[]{:S(2)}) collective-permute-start(bf16[128,256]{1,0:T(8,128)(2,1)S(1)} %shard_map.99.refs_0_), channel_id=1, source_target_pairs={{0,2},{1,3},{2,0},{3,1},{4,6},{5,7},{6,4},{7,5},{8,10},{9,11},{10,... | collective-permute-start | bytes 196616 | tf_op jit(solution)/shard_map/ppermute | solution.py:147
  29.2 0.8 %collective-permute-start.15 = (bf16[128,256]{1,0:T(8,128)(2,1)S(1)}, bf16[128,256]{1,0:T(8,128)(2,1)S(1)}, u32[]{:S(2)}, u32[]{:S(2)}) collective-permute-start(bf16[128,256]{1,0:T(8,128)(2,1)S(1)} %shard_map.99.refs_0_), channel_id=1, source_target_pairs={{0,3},{1,2},{2,1},{3,0},{4,7},{5,6},{6,5},{7,4},{8,11},{9,10},{10,... | collective-permute-start | bytes 196616 | tf_op jit(solution)/shard_map/ppermute | solution.py:147
  30.0 0.0 collective-permute-done.13.refs_1_
  30.0 2.6 %collective-permute-done.14.refs_2_ = bf16[128,256]{1,0:T(8,128)(2,1)S(1)} collective-permute-done((bf16[128,256]{1,0:T(8,128)(2,1)S(1)}, bf16[128,256]{1,0:T(8,128)(2,1)S(1)}, u32[]{:S(2)}, u32[]{:S(2)}) %collective-permute-start.14) | collective-permute-done | bytes 65568 | tf_op jit(solution)/shard_map/ppermute | solution.py:147
  32.5 2.7 %collective-permute-done.15.refs_3_ = bf16[128,256]{1,0:T(8,128)(2,1)S(1)} collective-permute-done((bf16[128,256]{1,0:T(8,128)(2,1)S(1)}, bf16[128,256]{1,0:T(8,128)(2,1)S(1)}, u32[]{:S(2)}, u32[]{:S(2)}) %collective-permute-start.15) | collective-permute-done | bytes 65568 | tf_op jit(solution)/shard_map/ppermute | solution.py:147
  35.3 0.1 collective-permute-start.16
  35.4 0.1 copy.10.scale
  35.5 0.0 copy-done.1
  35.5 0.8 %shard_map.98 = f32[64,256]{1,0:T(8,128)} custom-call(f32[64,256]{1,0:T(8,128)S(1)} %get-tuple-element.11.pulled, f32[64,1]{1,0:T(8,128)S(1)} %copy.10.scale, bf16[256,256]{1,0:T(8,128)(2,1)S(1)} %copy-done.1, bf16[192,256]{1,0:T(8,128)(2,1)S(1)} %collective-permute-done.10.refs_0_, bf16[192,256]{1,0:T(8,128)(2,1)S(1)} %collective-permute-done.11.refs_1_, ...), custom_call_target="tpu_custom_call" | custom-call | flops 16777216 | bytes 557312 | tf_op jit(solution)/shard_map/pallas_call | solution.py:23
  36.3 0.4 %collective-permute-done.16.other = f32[128,256]{1,0:T(8,128)S(1)} collective-permute-done((f32[128,256]{1,0:T(8,128)S(1)}, f32[128,256]{1,0:T(8,128)S(1)}, u32[]{:S(2)}, u32[]{:S(2)}) %collective-permute-start.16) | collective-permute-done | bytes 131104 | tf_op jit(solution)/shard_map/ppermute | solution.py:147
  36.7 0.7 %shard_map.101 = f32[256,256]{1,0:T(8,128)} custom-call(f32[128,256]{1,0:T(8,128)S(1)} %shard_map.100.own, f32[128,256]{1,0:T(8,128)S(1)} %collective-permute-done.16.other), custom_call_target="tpu_custom_call" | custom-call | bytes 524288 | tf_op jit(solution)/shard_map/pallas_call | solution.py:23
  (4 shorter events, 0.1 us)
Async XLA Ops:
  0.6 12.2 %collective-permute-start = (bf16[1,1,6,128,128]{4,3,2,1,0:T(8,128)(2,1)}, bf16[1,1,6,128,128]{4,3,2,1,0:T(8,128)(2,1)S(1)}, u32[]{:S(2)}, u32[]{:S(2)}) collective-permute-start(bf16[1,1,6,128,128]{4,3,2,1,0:T(8,128)(2,1)} %own.1), channel_id=1, source_target_pairs={{0,4},{4,0},{8,12},{12,8},{16,20},{20,16},{24,28},{28,24},{1,5},{5... | collective-permute-start | bytes 589832 | tf_op jit(solution)/shard_map/ppermute | solution.py:147
  1.8 12.0 %copy-start = (bf16[1,1,6,128,128]{4,3,2,1,0:T(8,128)(2,1)S(1)}, bf16[1,1,6,128,128]{4,3,2,1,0:T(8,128)(2,1)}, u32[]{:S(2)}) copy-start(bf16[1,1,6,128,128]{4,3,2,1,0:T(8,128)(2,1)} %own.1) | copy-start | bytes 589828
  2.8 0.7 %copy-start.2 = (s32[1,1,6]{2,1,0:T(1,128)S(1)}, s32[1,1,6]{2,1,0:T(1,128)}, u32[]{:S(2)}) copy-start(s32[1,1,6]{2,1,0:T(1,128)} %own_slot.1) | copy-start | bytes 76
  2.8 1.3 %collective-permute-start.3 = (bf16[128,256]{1,0:T(8,128)(2,1)S(1)}, bf16[128,256]{1,0:T(8,128)(2,1)S(1)}, u32[]{:S(2)}, u32[]{:S(2)}) collective-permute-start(bf16[128,256]{1,0:T(8,128)(2,1)S(1)} %pad_maximum_fusion), channel_id=1, source_target_pairs={{0,4},{4,0},{8,12},{12,8},{16,20},{20,16},{24,28},{28,24},{1,5},{5... | collective-permute-start | bytes 196616 | tf_op jit(solution)/shard_map/ppermute | solution.py:147
  3.5 7.6 %collective-permute-start.1 = (s32[1,1,6]{2,1,0:T(1,128)S(1)}, s32[1,1,6]{2,1,0:T(1,128)S(1)}, u32[]{:S(2)}, u32[]{:S(2)}) collective-permute-start(s32[1,1,6]{2,1,0:T(1,128)S(1)} %copy-done.2), channel_id=1, source_target_pairs={{0,4},{4,0},{8,12},{12,8},{16,20},{20,16},{24,28},{28,24},{1,5},{5... | collective-permute-start | bytes 80 | tf_op jit(solution)/shard_map/ppermute | solution.py:147
  3.5 4.9 %collective-permute-start.2 = (s32[1,1]{1,0:T(1,128)}, s32[1,1]{1,0:T(1,128)}, u32[]{:S(2)}, u32[]{:S(2)}) collective-permute-start(s32[1,1]{1,0:T(1,128)} %param.15), channel_id=1, source_target_pairs={{0,4},{4,0},{8,12},{12,8},{16,20},{20,16},{24,28},{28,24},{1,5},{5... | collective-permute-start | bytes 20 | tf_op jit(solution)/shard_map/ppermute | solution.py:147
  4.2 7.1 %collective-permute-start.7 = (bf16[128,128]{1,0:T(8,128)(2,1)S(1)}, bf16[128,128]{1,0:T(8,128)(2,1)S(1)}, u32[]{:S(2)}, u32[]{:S(2)}) collective-permute-start(bf16[128,128]{1,0:T(8,128)(2,1)S(1)} %get-tuple-element.10.refs_5_), channel_id=1, source_target_pairs={{0,8},{4,12},{8,0},{12,4},{16,24},{20,28},{24,16},{28,20},{1,9},{5... | collective-permute-start | bytes 98312 | tf_op jit(solution)/shard_map/ppermute | solution.py:147
  6.9 10.7 %collective-permute-start.4 = (bf16[128,256]{1,0:T(8,128)(2,1)S(1)}, bf16[128,256]{1,0:T(8,128)(2,1)S(1)}, u32[]{:S(2)}, u32[]{:S(2)}) collective-permute-start(bf16[128,256]{1,0:T(8,128)(2,1)S(1)} %get-tuple-element.9.refs_1_), channel_id=1, source_target_pairs={{0,1},{1,0},{2,3},{3,2},{4,5},{5,4},{6,7},{7,6},{8,9},{9,8},{10,11... | collective-permute-start | bytes 196616 | tf_op jit(solution)/shard_map/ppermute | solution.py:147
  8.5 9.2 %collective-permute-start.5 = (bf16[128,256]{1,0:T(8,128)(2,1)S(1)}, bf16[128,256]{1,0:T(8,128)(2,1)S(1)}, u32[]{:S(2)}, u32[]{:S(2)}) collective-permute-start(bf16[128,256]{1,0:T(8,128)(2,1)S(1)} %get-tuple-element.9.refs_1_), channel_id=1, source_target_pairs={{0,2},{1,3},{2,0},{3,1},{4,6},{5,7},{6,4},{7,5},{8,10},{9,11},{10,... | collective-permute-start | bytes 196616 | tf_op jit(solution)/shard_map/ppermute | solution.py:147
  11.1 6.6 %collective-permute-start.6 = (bf16[128,256]{1,0:T(8,128)(2,1)S(1)}, bf16[128,256]{1,0:T(8,128)(2,1)S(1)}, u32[]{:S(2)}, u32[]{:S(2)}) collective-permute-start(bf16[128,256]{1,0:T(8,128)(2,1)S(1)} %get-tuple-element.9.refs_1_), channel_id=1, source_target_pairs={{0,3},{1,2},{2,1},{3,0},{4,7},{5,6},{6,5},{7,4},{8,11},{9,10},{10,... | collective-permute-start | bytes 196616 | tf_op jit(solution)/shard_map/ppermute | solution.py:147
  11.3 4.1 %collective-permute-start.8 = (bf16[128,128]{1,0:T(8,128)(2,1)S(1)}, bf16[128,128]{1,0:T(8,128)(2,1)S(1)}, u32[]{:S(2)}, u32[]{:S(2)}) collective-permute-start(bf16[128,128]{1,0:T(8,128)(2,1)S(1)} %get-tuple-element.10.refs_5_), channel_id=1, source_target_pairs={{0,16},{4,20},{8,24},{12,28},{16,0},{20,4},{24,8},{28,12},{1,17},{... | collective-permute-start | bytes 98312 | tf_op jit(solution)/shard_map/ppermute | solution.py:147
  12.8 4.8 %collective-permute-start.9 = (bf16[128,128]{1,0:T(8,128)(2,1)S(1)}, bf16[128,128]{1,0:T(8,128)(2,1)S(1)}, u32[]{:S(2)}, u32[]{:S(2)}) collective-permute-start(bf16[128,128]{1,0:T(8,128)(2,1)S(1)} %get-tuple-element.10.refs_5_), channel_id=1, source_target_pairs={{0,24},{4,28},{8,16},{12,20},{16,8},{20,12},{24,0},{28,4},{1,25},{... | collective-permute-start | bytes 98312 | tf_op jit(solution)/shard_map/ppermute | solution.py:147
  18.2 4.7 %collective-permute-start.10 = (bf16[192,256]{1,0:T(8,128)(2,1)S(1)}, bf16[192,256]{1,0:T(8,128)(2,1)S(1)}, u32[]{:S(2)}, u32[]{:S(2)}) collective-permute-start(bf16[192,256]{1,0:T(8,128)(2,1)S(1)} %get-tuple-element.12), channel_id=1, source_target_pairs={{0,8},{4,12},{8,0},{12,4},{16,24},{20,28},{24,16},{28,20},{1,9},{5... | collective-permute-start | bytes 294920 | tf_op jit(solution)/shard_map/ppermute | solution.py:147
  18.8 4.6 %collective-permute-start.11 = (bf16[192,256]{1,0:T(8,128)(2,1)S(1)}, bf16[192,256]{1,0:T(8,128)(2,1)S(1)}, u32[]{:S(2)}, u32[]{:S(2)}) collective-permute-start(bf16[192,256]{1,0:T(8,128)(2,1)S(1)} %get-tuple-element.13), channel_id=1, source_target_pairs={{0,16},{4,20},{8,24},{12,28},{16,0},{20,4},{24,8},{28,12},{1,17},{... | collective-permute-start | bytes 294920 | tf_op jit(solution)/shard_map/ppermute | solution.py:147
  19.9 5.5 %collective-permute-start.12 = (bf16[192,256]{1,0:T(8,128)(2,1)S(1)}, bf16[192,256]{1,0:T(8,128)(2,1)S(1)}, u32[]{:S(2)}, u32[]{:S(2)}) collective-permute-start(bf16[192,256]{1,0:T(8,128)(2,1)S(1)} %get-tuple-element.14), channel_id=1, source_target_pairs={{0,24},{4,28},{8,16},{12,20},{16,8},{20,12},{24,0},{28,4},{1,25},{... | collective-permute-start | bytes 294920 | tf_op jit(solution)/shard_map/ppermute | solution.py:147
  25.5 10.0 %copy-start.1 = (bf16[256,256]{1,0:T(8,128)(2,1)S(1)}, bf16[256,256]{1,0:T(8,128)(2,1)}, u32[]{:S(2)}) copy-start(bf16[256,256]{1,0:T(8,128)(2,1)} %weight.1) | copy-start | bytes 393220
  25.5 4.5 %collective-permute-start.13 = (bf16[128,256]{1,0:T(8,128)(2,1)S(1)}, bf16[128,256]{1,0:T(8,128)(2,1)S(1)}, u32[]{:S(2)}, u32[]{:S(2)}) collective-permute-start(bf16[128,256]{1,0:T(8,128)(2,1)S(1)} %shard_map.99.refs_0_), channel_id=1, source_target_pairs={{0,1},{1,0},{2,3},{3,2},{4,5},{5,4},{6,7},{7,6},{8,9},{9,8},{10,11... | collective-permute-start | bytes 196616 | tf_op jit(solution)/shard_map/ppermute | solution.py:147
  26.3 6.2 %collective-permute-start.14 = (bf16[128,256]{1,0:T(8,128)(2,1)S(1)}, bf16[128,256]{1,0:T(8,128)(2,1)S(1)}, u32[]{:S(2)}, u32[]{:S(2)}) collective-permute-start(bf16[128,256]{1,0:T(8,128)(2,1)S(1)} %shard_map.99.refs_0_), channel_id=1, source_target_pairs={{0,2},{1,3},{2,0},{3,1},{4,6},{5,7},{6,4},{7,5},{8,10},{9,11},{10,... | collective-permute-start | bytes 196616 | tf_op jit(solution)/shard_map/ppermute | solution.py:147
  29.2 6.1 %collective-permute-start.15 = (bf16[128,256]{1,0:T(8,128)(2,1)S(1)}, bf16[128,256]{1,0:T(8,128)(2,1)S(1)}, u32[]{:S(2)}, u32[]{:S(2)}) collective-permute-start(bf16[128,256]{1,0:T(8,128)(2,1)S(1)} %shard_map.99.refs_0_), channel_id=1, source_target_pairs={{0,3},{1,2},{2,1},{3,0},{4,7},{5,6},{6,5},{7,4},{8,11},{9,10},{10,... | collective-permute-start | bytes 196616 | tf_op jit(solution)/shard_map/ppermute | solution.py:147
  35.3 1.4 %collective-permute-start.16 = (f32[128,256]{1,0:T(8,128)S(1)}, f32[128,256]{1,0:T(8,128)S(1)}, u32[]{:S(2)}, u32[]{:S(2)}) collective-permute-start(f32[128,256]{1,0:T(8,128)S(1)} %shard_map.100.own), channel_id=1, source_target_pairs={{0,4},{4,0},{8,12},{12,8},{16,20},{20,16},{24,28},{28,24},{1,5},{5... | collective-permute-start | bytes 393224 | tf_op jit(solution)/shard_map/ppermute | solution.py:147

commit v2 on v1

--- a/solution.py
+++ b/solution.py
@@ -30,15 +30,29 @@
     )(*ins)
 
 
-def pair_up(sg, sf, other, gpair, xpair):
-    nodes, width = sg.shape
-    half = width // CORES
-    core = positions()[1]
-    columns = pl.ds(pl.multiple_of(core * half, half), half)
-    gpair[:nodes] = sg[...]
-    gpair[nodes:] = other[:nodes]
-    xpair[:nodes] = sf[:, columns]
-    xpair[nodes:] = other[nodes:, columns]
+def column(row):
+    n = row.shape[1]
+    across = lax.broadcasted_iota(jnp.int32, (n, n), 1)
+    down = lax.broadcasted_iota(jnp.int32, (n, n), 0)
+    return jnp.sum(jnp.where(across == down, row, 0.0), axis=1, keepdims=True)
+
+
+def scale_nodes(features, grad_out, relu_mask, degree, keep, send, scale_out):
+    core = positions()[1]
+    scale = column(lax.rsqrt(degree[...].astype(jnp.float32)))
+    masked = grad_out[...] * relu_mask[...].astype(jnp.bfloat16)
+    scaled_grad = (masked.astype(jnp.float32) * scale).astype(jnp.bfloat16)
+    scaled_feat = (features[...].astype(jnp.float32) * scale).astype(jnp.bfloat16)
+    keep[...] = jnp.where(core == 1, scaled_grad, scaled_feat)
+    send[...] = jnp.where(core == 1, scaled_feat, scaled_grad)
+    scale_out[...] = scale
+
+
+def pair_up(keep, other, pair):
+    nodes = keep.shape[0]
+    core = positions()[1]
+    pair[pl.ds(pl.multiple_of(core * nodes, nodes), nodes)] = keep[...]
+    pair[pl.ds(pl.multiple_of((1 - core) * nodes, nodes), nodes)] = other[...]
 
 
 def lay_out(nodes, own, theirs, own_slot, their_slot, own_count, their_count, dense):
@@ -47,8 +61,8 @@
     chip, core, col = positions()
     col_blocks = dense.shape[0] // block
     dense[...] = jnp.zeros_like(dense)
-    for p, (blocks, slots, count) in enumerate(
-        ((own, own_slot, own_count), (theirs, their_slot, their_count))
+    for where, blocks, slots, count in (
+        (core, own, own_slot, own_count), (1 - core, theirs, their_slot, their_count)
     ):
         @pl.loop(0, count[0, 0])
         def place(b):
@@ -58,41 +72,47 @@
             value = blocks[0, 0, b]
             swapped = jnp.concatenate([value[nodes:], value[:nodes]], axis=0)
             value = jnp.where(col % per_block == 1, swapped, value).T
-            swapped = jnp.concatenate([value[nodes:], value[:nodes]], axis=0)
-            value = jnp.where(core == 1, swapped, value)
             rows = pl.ds(pl.multiple_of(target * block, block), block)
-            columns = pl.ds(pl.multiple_of((source * CORES + p) * block, block), block)
+            columns = pl.ds(pl.multiple_of((source * CORES + where) * block, block), block)
             dense[rows, columns] = value
 
 
 def multiply(nodes, chips, cols, refs):
-    dense = refs[0]
-    grads = refs[1 : 1 + cols]
-    feats = refs[1 + cols : 1 + cols + chips]
-    pulled = refs[1 + cols + chips]
-    weighted = refs[2 + cols + chips]
-    sends = refs[3 + cols + chips :]
+    count = max(chips, cols)
+    dense, held, swapped = refs[0], refs[1 : 1 + count], refs[1 + count : 1 + 2 * count]
+    pulled, weighted = refs[1 + 2 * count : 3 + 2 * count]
+    sends = refs[3 + 2 * count :]
+    core = positions()[1]
     per_block = 2
+    grads = [jnp.where(core == 1, h[...], s[...]) for h, s in zip(held[:cols], swapped[:cols])]
     order = [
-        grads[per_block * kh + kl][p * nodes : (p + 1) * nodes]
+        grads[per_block * kh + kl][c * nodes : (c + 1) * nodes]
         for kh in range(cols // per_block)
-        for p in range(CORES)
+        for c in range(CORES)
         for kl in range(per_block)
     ]
     gathered = jnp.concatenate(order, axis=0)
     total = jnp.dot(dense[...], gathered, preferred_element_type=jnp.float32)
-    features = jnp.concatenate([f[...] for f in feats], axis=0)
+    half = weighted.shape[0]
+    mine = pl.ds(pl.multiple_of(core * half, half), half)
+    pieces = [-k % chips for k in range(chips)]
+    features = [jnp.where(core == 1, swapped[k][:, mine], held[k][:, mine]) for k in pieces]
+    features = jnp.concatenate(features, axis=0)
     high = total.astype(jnp.bfloat16)
     low = (total - high.astype(jnp.float32)).astype(jnp.bfloat16)
     rows = (((0,), (0,)), ((), ()))
     part = lax.dot_general(features, high, rows, preferred_element_type=jnp.float32)
     part = part + lax.dot_general(features, low, rows, preferred_element_type=jnp.float32)
     part = part.astype(jnp.bfloat16)
-    pulled[...] = total[:nodes]
     weighted[...] = part
+
+    def chunk(x, k):
+        at = k * CORES * nodes
+        return jnp.where(core == 1, x[at + nodes : at + 2 * nodes], x[at : at + nodes])
+
+    pulled[...] = chunk(total, 0)
     for k, send in enumerate(sends, 1):
-        at = k * CORES * nodes
-        send[:nodes] = high[at : at + nodes]
+        send[:nodes] = chunk(high, k)
         send[nodes:] = part
 
 
@@ -122,7 +142,7 @@
 
 
 def sum_cols(factor, *refs):
-    terms, out = refs[:-1], refs[-1]
+    terms, out = refs[:-2], refs[-1]
     out[...] = tree([t[...].astype(jnp.float32) for t in terms]) * factor
 
 
@@ -138,7 +158,6 @@
     rows = lax.axis_size("row")
     cols = lax.axis_size("col")
     chips = rows // CORES
-    block = adjacency.shape[-1]
     half = width // CORES
     bf16, f32 = jnp.bfloat16, jnp.float32
     shape = jax.ShapeDtypeStruct
@@ -146,22 +165,30 @@
     def swap(x, axis, size, k):
         return lax.ppermute(x, axis, [(d, d ^ k) for d in range(size)])
 
-    their_blocks = swap(adjacency, "row", rows, 1)
-    their_slot = swap(block_slot, "row", rows, 1)
-    their_count = swap(block_count, "row", rows, 1)
-    scale = lax.rsqrt(degree.astype(f32))[:, None]
-    masked = grad_out * relu_mask.astype(bf16)
-    scaled_grad = (masked.astype(f32) * scale).astype(bf16)
-    scaled_feat = (features.astype(f32) * scale).astype(bf16)
-    other = swap(jnp.concatenate([scaled_grad, scaled_feat], axis=0), "row", rows, 1)
-    gpair, xpair = call(
-        pair_up,
-        [shape((CORES * nodes, width), bf16), shape((CORES * nodes, half), bf16)],
-        [scaled_grad, scaled_feat, other],
-    )
-    grads = [gpair] + [swap(gpair, "col", cols, k) for k in range(1, cols)]
-    feats = [xpair] + [swap(xpair, "row", rows, CORES * k) for k in range(1, chips)]
-
+    def partner(x):
+        return swap(x, "row", rows, 1)
+
+    def both(x, kx, kz):
+        pairs = []
+        for r in range(rows):
+            for j in range(cols):
+                to = (r, j ^ kz) if r % CORES == 1 else (r ^ (CORES * kx), j)
+                pairs.append((r * cols + j, to[0] * cols + to[1]))
+        return lax.ppermute(x, ("row", "col"), pairs)
+
+    their_blocks = partner(adjacency)
+    their_slot = partner(block_slot)
+    their_count = partner(block_count)
+    keep, send, scale = call(
+        scale_nodes,
+        [shape((nodes, width), bf16), shape((nodes, width), bf16), shape((nodes, 1), f32)],
+        [features, grad_out, relu_mask, degree[None, :]],
+    )
+    (pair,) = call(pair_up, [shape((CORES * nodes, width), bf16)], [keep, partner(send)])
+    assert chips == cols
+    held = [pair] + [None] * (cols - 1)
+    for kz in range(cols - 1, 0, -1):
+        held[kz] = both(pair, chips - kz, kz)
     targets, sources = rows * nodes, CORES * cols * nodes
     size = targets * sources * 2
     (dense,) = call(
@@ -171,11 +198,12 @@
         [VMEM, VMEM, SMEM, SMEM, SMEM, SMEM],
         limit=8 * 2**20 + 3 * size,
     )
+    swapped = [partner(h) for h in held]
     out = call(
         lambda *refs: multiply(nodes, chips, cols, refs),
         [shape((nodes, width), f32), shape((half, width), bf16)]
         + [shape((nodes + half, width), bf16)] * (chips - 1),
-        [dense] + grads + feats,
+        [dense] + held + swapped,
         limit=8 * 2**20 + 3 * size,
         flops=2 * targets * sources * width + 4 * targets * half * width,
     )
@@ -192,9 +220,13 @@
         flops=4 * nodes * width * width,
     )
     factor = (nodes * rows * cols) ** (-0.5)
-    (own_half,) = call(functools.partial(sum_cols, factor), [shape((half, width), f32)], planes)
-    other_half = swap(own_half, "row", rows, 1)
-    (weight_grad,) = call(join, [shape((width, width), f32)], [own_half, other_half])
+    (own_half,) = call(
+        functools.partial(sum_cols, factor),
+        [shape((half, width), f32)],
+        planes + [grad_features],
+        [VMEM] * cols + [pl.ANY],
+    )
+    (weight_grad,) = call(join, [shape((width, width), f32)], [own_half, partner(own_half)])
     return grad_features, weight_grad
 
 

time: 37.6 us -> 38.1 us (1.013)
  local copies, waits for them, and re-layouts: 0.62 us -> 3.86 us
  starting transfers between devices: 18.2 us -> 16.1 us
  other arithmetic: 1.66 us -> 0 us
  waiting for transfers between devices: 11.8 us -> 12.2 us
    ppermute x17 -> x15, starting transfers between devices: 18.2 us -> 11.9 us  [swap(): return lax.ppermute(x, axis, [(d, d ^ k) for d in range(size)])]
    ppermute x0 -> x3, starting transfers between devices: none -> 4.25 us  [both(): return lax.ppermute(x, ('row', 'col'), pairs)]
    unnamed x6 -> x16, local copies, waits for them, and re-layouts: 0.52 us -> 3.86 us
    convert_element_type x1 -> x0, other arithmetic: 1 us -> none  [local(): scaled_feat = (features.astype(f32) * scale).astype(bf16)]
    broadcast_in_dim x1 -> x0, other arithmetic: 0.66 us -> none  [local(): scale = lax.rsqrt(degree.astype(f32))[:, None]]
    pallas_call x7 -> x8, Pallas kernels: 3.82 us -> 4.09 us  [call(): pl.pallas_call(body, out_shape=outs, in_specs=[pl.BlockSpec(memory_space=...]
    ppermute x17 -> x15, waiting for transfers between devices: 11.8 us -> 12 us  [swap(): return lax.ppermute(x, axis, [(d, d ^ k) for d in range(size)])]
  transfers between devices with their start and end apart: 17 -> 18, of which waited for: 8 -> 9; matrix products, arithmetic and copies ran while one was open for 5% -> 0% of each run, Pallas kernels for 6% -> 7%
where the time goes in v2:
time: 38.1 us; the launch traced here: 37.7 us
  starting transfers between devices  16.1 us (42%)
  waiting for transfers between devices  12.2 us (32%)
  Pallas kernels  4.09 us (11%)
  local copies, waits for them, and re-layouts  3.86 us (10%)
  between operations  1.4 us (4%)
    ppermute x15, waiting for transfers between devices, swap(): return lax.ppermute(x, axis, [(d, d ^ k) for d in range(size)])  12 us
    ppermute x15, starting transfers between devices, swap(): return lax.ppermute(x, axis, [(d, d ^ k) for d in range(size)])  11.9 us
    ppermute x3, starting transfers between devices, both(): return lax.ppermute(x, ('row', 'col'), pairs)  4.25 us
    pallas_call x8, Pallas kernels, call(): pl.pallas_call(body, out_shape=outs, in_specs=[pl.BlockSpec(memory_space=...  4.09 us
    unnamed x16, local copies, waits for them, and re-layouts  3.86 us
  transfers between devices with their start and end apart: 18, of which 9 were waited for; matrix products, arithmetic and copies ran while one was open for 0% of the time, Pallas kernels for 7%

profile of v2, /device:TPU:0, one launch (start us, length us, event | category | flops | bytes accessed | tf_op | source)
XLA Modules:
  0.0 37.7 jit_solution(6533018885415868270)
XLA Ops:
  0.6 0.5 %collective-permute-start = (bf16[1,1,6,128,128]{4,3,2,1,0:T(8,128)(2,1)}, bf16[1,1,6,128,128]{4,3,2,1,0:T(8,128)(2,1)S(1)}, u32[]{:S(2)}, u32[]{:S(2)}) collective-permute-start(bf16[1,1,6,128,128]{4,3,2,1,0:T(8,128)(2,1)} %own.1), channel_id=1, source_target_pairs={{0,4},{4,0},{8,12},{12,8},{16,20},{20,16},{24,28},{28,24},{1,5},{5... | collective-permute-start | bytes 589832 | tf_op jit(solution)/shard_map/ppermute | solution.py:166
  1.2 0.8 %copy-done.3 = s32[64,256]{1,0:T(8,128)S(1)} copy-done((s32[64,256]{1,0:T(8,128)S(1)}, s32[64,256]{1,0:T(8,128)}, u32[]{:S(2)}) %copy-start.3) | copy-done | bytes 65560
  2.0 0.8 %copy-done.4 = bf16[64,256]{1,0:T(8,128)(2,1)S(1)} copy-done((bf16[64,256]{1,0:T(8,128)(2,1)S(1)}, bf16[64,256]{1,0:T(8,128)(2,1)}, u32[]{:S(2)}) %copy-start.4) | copy-done | bytes 32792
  2.8 0.8 %copy-done.5 = bf16[64,256]{1,0:T(8,128)(2,1)S(1)} copy-done((bf16[64,256]{1,0:T(8,128)(2,1)S(1)}, bf16[64,256]{1,0:T(8,128)(2,1)}, u32[]{:S(2)}) %copy-start.5) | copy-done | bytes 32792
  3.5 0.7 %copy-done.7 = s32[64]{0:T(128)S(1)} copy-done((s32[64]{0:T(128)S(1)}, s32[64]{0:T(128)}, u32[]{:S(2)}) %copy-start.7) | copy-done | bytes 280
  4.2 0.1 shard_map.96
  4.3 0.1 collective-permute-start.3
  4.4 1.1 %collective-permute-done.3.other = bf16[64,256]{1,0:T(8,128)(2,1)S(1)} collective-permute-done((bf16[64,256]{1,0:T(8,128)(2,1)S(1)}, bf16[64,256]{1,0:T(8,128)(2,1)S(1)}, u32[]{:S(2)}, u32[]{:S(2)}) %collective-permute-start.3) | collective-permute-done | bytes 32800 | tf_op jit(solution)/shard_map/ppermute | solution.py:166
  5.6 2.7 %collective-permute-start.6 = (bf16[128,256]{1,0:T(8,128)(2,1)S(1)}, bf16[128,256]{1,0:T(8,128)(2,1)S(1)}, u32[]{:S(2)}, u32[]{:S(2)}) collective-permute-start(bf16[128,256]{1,0:T(8,128)(2,1)S(1)} %shard_map.97.refs_1_), channel_id=1, source_target_pairs={{0,8},{1,9},{2,10},{3,11},{4,7},{5,6},{6,5},{7,4},{8,0},{9,1},{10,... | collective-permute-start | bytes 196616 | tf_op jit(solution)/shard_map/ppermute | solution.py:177
  8.3 1.5 %collective-permute-start.5 = (bf16[128,256]{1,0:T(8,128)(2,1)S(1)}, bf16[128,256]{1,0:T(8,128)(2,1)S(1)}, u32[]{:S(2)}, u32[]{:S(2)}) collective-permute-start(bf16[128,256]{1,0:T(8,128)(2,1)S(1)} %shard_map.97.refs_1_), channel_id=1, source_target_pairs={{0,16},{1,17},{2,18},{3,19},{4,6},{5,7},{6,4},{7,5},{8,24},{9,25},... | collective-permute-start | bytes 196616 | tf_op jit(solution)/shard_map/ppermute | solution.py:177
  9.8 0.0 collective-permute-start.4
  9.8 1.0 %collective-permute-start.2 = (s32[1,1]{1,0:T(1,128)}, s32[1,1]{1,0:T(1,128)}, u32[]{:S(2)}, u32[]{:S(2)}) collective-permute-start(s32[1,1]{1,0:T(1,128)} %param.15), channel_id=1, source_target_pairs={{0,4},{4,0},{8,12},{12,8},{16,20},{20,16},{24,28},{28,24},{1,5},{5... | collective-permute-start | bytes 20 | tf_op jit(solution)/shard_map/ppermute | solution.py:166
  10.8 1.0 %collective-permute-done.2.their_count = s32[1,1]{1,0:T(1,128)} collective-permute-done((s32[1,1]{1,0:T(1,128)}, s32[1,1]{1,0:T(1,128)}, u32[]{:S(2)}, u32[]{:S(2)}) %collective-permute-start.2) | collective-permute-done | bytes 36 | tf_op jit(solution)/shard_map/ppermute | solution.py:166
  11.8 0.0 copy-done.6
  11.8 0.3 collective-permute-start.1
  12.1 0.8 %collective-permute-done.1.their_slot = s32[1,1,6]{2,1,0:T(1,128)S(1)} collective-permute-done((s32[1,1,6]{2,1,0:T(1,128)S(1)}, s32[1,1,6]{2,1,0:T(1,128)S(1)}, u32[]{:S(2)}, u32[]{:S(2)}) %collective-permute-start.1) | collective-permute-done | bytes 56 | tf_op jit(solution)/shard_map/ppermute | solution.py:166
  12.9 0.3 collective-permute-start.7
  13.2 0.0 collective-permute-done.6.refs_4_
  13.2 0.2 collective-permute-start.10
  13.4 0.0 collective-permute-done.5.refs_3_
  13.4 1.4 %collective-permute-start.9 = (bf16[128,256]{1,0:T(8,128)(2,1)S(1)}, bf16[128,256]{1,0:T(8,128)(2,1)S(1)}, u32[]{:S(2)}, u32[]{:S(2)}) collective-permute-start(bf16[128,256]{1,0:T(8,128)(2,1)S(1)} %collective-permute-done.5.refs_3_), channel_id=1, source_target_pairs={{0,4},{4,0},{8,12},{12,8},{16,20},{20,16},{24,28},{28,24},{1,5},{5... | collective-permute-start | bytes 196616 | tf_op jit(solution)/shard_map/ppermute | solution.py:166
  14.8 0.2 collective-permute-done.4.refs_2_
  15.0 0.0 collective-permute-start.8
  15.6 0.0 collective-permute-done.theirs
  15.6 0.0 copy-done.1
  15.6 1.7 %shard_map.95.refs_0_ = bf16[512,512]{1,0:T(8,128)(2,1)S(1)} custom-call(bf16[1,1,6,128,128]{4,3,2,1,0:T(8,128)(2,1)S(1)} %copy-done.1, bf16[1,1,6,128,128]{4,3,2,1,0:T(8,128)(2,1)S(1)} %collective-permute-done.theirs, s32[1,1,6]{2,1,0:T(1,128)S(1)} %copy-done.6, s32[1,1,6]{2,1,0:T(1,128)S(1)} %collective-permute-done.1.their_slot, ...), custom_call_target="tpu_custom_call" | custom-call | bytes 917560 | tf_op jit(solution)/shard_map/pallas_call | solution.py:23
  17.4 0.0 collective-permute-done.7.refs_5_
  17.4 0.0 collective-permute-done.10.refs_8_
  17.4 0.0 collective-permute-done.9.refs_7_
  17.4 0.0 collective-permute-done.8.refs_6_
  17.4 0.6 %shard_map.98 = (f32[64,256]{1,0:T(8,128)S(1)}, bf16[128,256]{1,0:T(8,128)(2,1)S(1)}, bf16[192,256]{1,0:T(8,128)(2,1)S(1)}, bf16[192,256]{1,0:T(8,128)(2,1)S(1)}, bf16[192,256]{1,0:T(8,128)(2,1)S(1)}) custom-call(bf16[512,512]{1,0:T(8,128)(2,1)S(1)} %shard_map.95.refs_0_, bf16[128,256]{1,0:T(8,128)(2,1)S(1)} %shard_map.97.refs_1_, ...), custom_call_target="tpu_custom_call" | custom-call | flops 201326592 | bytes 1474560 | tf_op jit(solution)/shard_map/pallas_call | solution.py:23
  18.0 1.1 %collective-permute-start.11 = (bf16[192,256]{1,0:T(8,128)(2,1)S(1)}, bf16[192,256]{1,0:T(8,128)(2,1)S(1)}, u32[]{:S(2)}, u32[]{:S(2)}) collective-permute-start(bf16[192,256]{1,0:T(8,128)(2,1)S(1)} %get-tuple-element.14), channel_id=1, source_target_pairs={{0,8},{4,12},{8,0},{12,4},{16,24},{20,28},{24,16},{28,20},{1,9},{5... | collective-permute-start | bytes 294920 | tf_op jit(solution)/shard_map/ppermute | solution.py:166
  19.2 1.1 %collective-permute-start.12 = (bf16[192,256]{1,0:T(8,128)(2,1)S(1)}, bf16[192,256]{1,0:T(8,128)(2,1)S(1)}, u32[]{:S(2)}, u32[]{:S(2)}) collective-permute-start(bf16[192,256]{1,0:T(8,128)(2,1)S(1)} %get-tuple-element.15), channel_id=1, source_target_pairs={{0,16},{4,20},{8,24},{12,28},{16,0},{20,4},{24,8},{28,12},{1,17},{... | collective-permute-start | bytes 294920 | tf_op jit(solution)/shard_map/ppermute | solution.py:166
  20.3 1.3 %collective-permute-start.13 = (bf16[192,256]{1,0:T(8,128)(2,1)S(1)}, bf16[192,256]{1,0:T(8,128)(2,1)S(1)}, u32[]{:S(2)}, u32[]{:S(2)}) collective-permute-start(bf16[192,256]{1,0:T(8,128)(2,1)S(1)} %get-tuple-element.16), channel_id=1, source_target_pairs={{0,24},{4,28},{8,16},{12,20},{16,8},{20,12},{24,0},{28,4},{1,25},{... | collective-permute-start | bytes 294920 | tf_op jit(solution)/shard_map/ppermute | solution.py:166
  21.6 1.8 %collective-permute-done.11.refs_0_ = bf16[192,256]{1,0:T(8,128)(2,1)S(1)} collective-permute-done((bf16[192,256]{1,0:T(8,128)(2,1)S(1)}, bf16[192,256]{1,0:T(8,128)(2,1)S(1)}, u32[]{:S(2)}, u32[]{:S(2)}) %collective-permute-start.11) | collective-permute-done | bytes 98336 | tf_op jit(solution)/shard_map/ppermute | solution.py:166
  23.4 2.9 %collective-permute-done.12.refs_1_ = bf16[192,256]{1,0:T(8,128)(2,1)S(1)} collective-permute-done((bf16[192,256]{1,0:T(8,128)(2,1)S(1)}, bf16[192,256]{1,0:T(8,128)(2,1)S(1)}, u32[]{:S(2)}, u32[]{:S(2)}) %collective-permute-start.12) | collective-permute-done | bytes 98336 | tf_op jit(solution)/shard_map/ppermute | solution.py:166
  26.2 0.0 collective-permute-done.13.refs_2_
  26.3 2.8 %collective-permute-start.16 = (bf16[128,256]{1,0:T(8,128)(2,1)S(1)}, bf16[128,256]{1,0:T(8,128)(2,1)S(1)}, u32[]{:S(2)}, u32[]{:S(2)}) collective-permute-start(bf16[128,256]{1,0:T(8,128)(2,1)S(1)} %shard_map.100.refs_0_), channel_id=1, source_target_pairs={{0,3},{1,2},{2,1},{3,0},{4,7},{5,6},{6,5},{7,4},{8,11},{9,10},{10,... | collective-permute-start | bytes 196616 | tf_op jit(solution)/shard_map/ppermute | solution.py:166
  29.1 0.0 collective-permute-start.15
  29.1 1.6 %collective-permute-start.14 = (bf16[128,256]{1,0:T(8,128)(2,1)S(1)}, bf16[128,256]{1,0:T(8,128)(2,1)S(1)}, u32[]{:S(2)}, u32[]{:S(2)}) collective-permute-start(bf16[128,256]{1,0:T(8,128)(2,1)S(1)} %shard_map.100.refs_0_), channel_id=1, source_target_pairs={{0,1},{1,0},{2,3},{3,2},{4,5},{5,4},{6,7},{7,6},{8,9},{9,8},{10,11... | collective-permute-start | bytes 196616 | tf_op jit(solution)/shard_map/ppermute | solution.py:166
  30.7 0.8 %shard_map.99.refs_4_ = f32[64,256]{1,0:T(8,128)} custom-call(f32[64,256]{1,0:T(8,128)S(1)} %get-tuple-element.12.pulled, f32[64,1]{1,0:T(8,128)S(1)} %get-tuple-element.13.scale, bf16[256,256]{1,0:T(8,128)(2,1)S(1)} %copy-done.2, bf16[192,256]{1,0:T(8,128)(2,1)S(1)} %collective-permute-done.11.refs_0_, ...), custom_call_target="tpu_custom_call" | custom-call | flops 16777216 | bytes 557312 | tf_op jit(solution)/shard_map/pallas_call | solution.py:23
  31.6 1.3 %collective-permute-done.16.refs_3_ = bf16[128,256]{1,0:T(8,128)(2,1)S(1)} collective-permute-done((bf16[128,256]{1,0:T(8,128)(2,1)S(1)}, bf16[128,256]{1,0:T(8,128)(2,1)S(1)}, u32[]{:S(2)}, u32[]{:S(2)}) %collective-permute-start.16) | collective-permute-done | bytes 65568 | tf_op jit(solution)/shard_map/ppermute | solution.py:166
  32.8 1.8 %collective-permute-done.15.refs_2_ = bf16[128,256]{1,0:T(8,128)(2,1)S(1)} collective-permute-done((bf16[128,256]{1,0:T(8,128)(2,1)S(1)}, bf16[128,256]{1,0:T(8,128)(2,1)S(1)}, u32[]{:S(2)}, u32[]{:S(2)}) %collective-permute-start.15) | collective-permute-done | bytes 65568 | tf_op jit(solution)/shard_map/ppermute | solution.py:166
  34.7 0.0 collective-permute-done.14.refs_1_
  34.7 0.8 %copy-done = f32[64,256]{1,0:T(8,128)S(1)} copy-done((f32[64,256]{1,0:T(8,128)S(1)}, f32[64,256]{1,0:T(8,128)}, u32[]{:S(2)}) %copy-start) | copy-done | bytes 65560
  35.5 0.1 collective-permute-start.17
  35.6 1.3 %collective-permute-done.17.other = f32[128,256]{1,0:T(8,128)S(1)} collective-permute-done((f32[128,256]{1,0:T(8,128)S(1)}, f32[128,256]{1,0:T(8,128)S(1)}, u32[]{:S(2)}, u32[]{:S(2)}) %collective-permute-start.17) | collective-permute-done | bytes 131104 | tf_op jit(solution)/shard_map/ppermute | solution.py:166
  37.0 0.7 %shard_map.102 = f32[256,256]{1,0:T(8,128)} custom-call(f32[128,256]{1,0:T(8,128)S(1)} %shard_map.101.own, f32[128,256]{1,0:T(8,128)S(1)} %collective-permute-done.17.other), custom_call_target="tpu_custom_call" | custom-call | bytes 524288 | tf_op jit(solution)/shard_map/pallas_call | solution.py:23
  (12 shorter events, 0.1 us)
Async XLA Ops:
  0.6 15.0 %copy-start.1 = (bf16[1,1,6,128,128]{4,3,2,1,0:T(8,128)(2,1)S(1)}, bf16[1,1,6,128,128]{4,3,2,1,0:T(8,128)(2,1)}, u32[]{:S(2)}) copy-start(bf16[1,1,6,128,128]{4,3,2,1,0:T(8,128)(2,1)} %own.1) | copy-start | bytes 589828
  0.6 15.0 %collective-permute-start = (bf16[1,1,6,128,128]{4,3,2,1,0:T(8,128)(2,1)}, bf16[1,1,6,128,128]{4,3,2,1,0:T(8,128)(2,1)S(1)}, u32[]{:S(2)}, u32[]{:S(2)}) collective-permute-start(bf16[1,1,6,128,128]{4,3,2,1,0:T(8,128)(2,1)} %own.1), channel_id=1, source_target_pairs={{0,4},{4,0},{8,12},{12,8},{16,20},{20,16},{24,28},{28,24},{1,5},{5... | collective-permute-start | bytes 589832 | tf_op jit(solution)/shard_map/ppermute | solution.py:166
  1.2 0.8 %copy-start.3 = (s32[64,256]{1,0:T(8,128)S(1)}, s32[64,256]{1,0:T(8,128)}, u32[]{:S(2)}) copy-start(s32[64,256]{1,0:T(8,128)} %relu_mask.1) | copy-start | bytes 196612
  2.0 0.8 %copy-start.4 = (bf16[64,256]{1,0:T(8,128)(2,1)S(1)}, bf16[64,256]{1,0:T(8,128)(2,1)}, u32[]{:S(2)}) copy-start(bf16[64,256]{1,0:T(8,128)(2,1)} %features.1) | copy-start | bytes 98308
  2.8 0.8 %copy-start.5 = (bf16[64,256]{1,0:T(8,128)(2,1)S(1)}, bf16[64,256]{1,0:T(8,128)(2,1)}, u32[]{:S(2)}) copy-start(bf16[64,256]{1,0:T(8,128)(2,1)} %grad_out.1) | copy-start | bytes 98308
  3.5 0.7 %copy-start.7 = (s32[64]{0:T(128)S(1)}, s32[64]{0:T(128)}, u32[]{:S(2)}) copy-start(s32[64]{0:T(128)} %param.11) | copy-start | bytes 772
  4.3 1.3 %collective-permute-start.3 = (bf16[64,256]{1,0:T(8,128)(2,1)S(1)}, bf16[64,256]{1,0:T(8,128)(2,1)S(1)}, u32[]{:S(2)}, u32[]{:S(2)}) collective-permute-start(bf16[64,256]{1,0:T(8,128)(2,1)S(1)} %get-tuple-element.11), channel_id=1, source_target_pairs={{0,4},{4,0},{8,12},{12,8},{16,20},{20,16},{24,28},{28,24},{1,5},{5... | collective-permute-start | bytes 98312 | tf_op jit(solution)/shard_map/ppermute | solution.py:166
  5.5 6.2 %copy-start.6 = (s32[1,1,6]{2,1,0:T(1,128)S(1)}, s32[1,1,6]{2,1,0:T(1,128)}, u32[]{:S(2)}) copy-start(s32[1,1,6]{2,1,0:T(1,128)} %own_slot.1) | copy-start | bytes 76
  5.6 7.6 %collective-permute-start.6 = (bf16[128,256]{1,0:T(8,128)(2,1)S(1)}, bf16[128,256]{1,0:T(8,128)(2,1)S(1)}, u32[]{:S(2)}, u32[]{:S(2)}) collective-permute-start(bf16[128,256]{1,0:T(8,128)(2,1)S(1)} %shard_map.97.refs_1_), channel_id=1, source_target_pairs={{0,8},{1,9},{2,10},{3,11},{4,7},{5,6},{6,5},{7,4},{8,0},{9,1},{10,... | collective-permute-start | bytes 196616 | tf_op jit(solution)/shard_map/ppermute | solution.py:177
  8.3 5.1 %collective-permute-start.5 = (bf16[128,256]{1,0:T(8,128)(2,1)S(1)}, bf16[128,256]{1,0:T(8,128)(2,1)S(1)}, u32[]{:S(2)}, u32[]{:S(2)}) collective-permute-start(bf16[128,256]{1,0:T(8,128)(2,1)S(1)} %shard_map.97.refs_1_), channel_id=1, source_target_pairs={{0,16},{1,17},{2,18},{3,19},{4,6},{5,7},{6,4},{7,5},{8,24},{9,25},... | collective-permute-start | bytes 196616 | tf_op jit(solution)/shard_map/ppermute | solution.py:177
  9.8 5.2 %collective-permute-start.4 = (bf16[128,256]{1,0:T(8,128)(2,1)S(1)}, bf16[128,256]{1,0:T(8,128)(2,1)S(1)}, u32[]{:S(2)}, u32[]{:S(2)}) collective-permute-start(bf16[128,256]{1,0:T(8,128)(2,1)S(1)} %shard_map.97.refs_1_), channel_id=1, source_target_pairs={{0,24},{1,25},{2,26},{3,27},{4,5},{5,4},{6,7},{7,6},{8,16},{9,17},... | collective-permute-start | bytes 196616 | tf_op jit(solution)/shard_map/ppermute | solution.py:177
  9.8 2.0 %collective-permute-start.2 = (s32[1,1]{1,0:T(1,128)}, s32[1,1]{1,0:T(1,128)}, u32[]{:S(2)}, u32[]{:S(2)}) collective-permute-start(s32[1,1]{1,0:T(1,128)} %param.15), channel_id=1, source_target_pairs={{0,4},{4,0},{8,12},{12,8},{16,20},{20,16},{24,28},{28,24},{1,5},{5... | collective-permute-start | bytes 20 | tf_op jit(solution)/shard_map/ppermute | solution.py:166
  11.8 1.1 %collective-permute-start.1 = (s32[1,1,6]{2,1,0:T(1,128)S(1)}, s32[1,1,6]{2,1,0:T(1,128)S(1)}, u32[]{:S(2)}, u32[]{:S(2)}) collective-permute-start(s32[1,1,6]{2,1,0:T(1,128)S(1)} %copy-done.6), channel_id=1, source_target_pairs={{0,4},{4,0},{8,12},{12,8},{16,20},{20,16},{24,28},{28,24},{1,5},{5... | collective-permute-start | bytes 80 | tf_op jit(solution)/shard_map/ppermute | solution.py:166
  12.9 4.5 %collective-permute-start.7 = (bf16[128,256]{1,0:T(8,128)(2,1)S(1)}, bf16[128,256]{1,0:T(8,128)(2,1)S(1)}, u32[]{:S(2)}, u32[]{:S(2)}) collective-permute-start(bf16[128,256]{1,0:T(8,128)(2,1)S(1)} %shard_map.97.refs_1_), channel_id=1, source_target_pairs={{0,4},{4,0},{8,12},{12,8},{16,20},{20,16},{24,28},{28,24},{1,5},{5... | collective-permute-start | bytes 196616 | tf_op jit(solution)/shard_map/ppermute | solution.py:166
  13.2 4.2 %collective-permute-start.10 = (bf16[128,256]{1,0:T(8,128)(2,1)S(1)}, bf16[128,256]{1,0:T(8,128)(2,1)S(1)}, u32[]{:S(2)}, u32[]{:S(2)}) collective-permute-start(bf16[128,256]{1,0:T(8,128)(2,1)S(1)} %collective-permute-done.6.refs_4_), channel_id=1, source_target_pairs={{0,4},{4,0},{8,12},{12,8},{16,20},{20,16},{24,28},{28,24},{1,5},{5... | collective-permute-start | bytes 196616 | tf_op jit(solution)/shard_map/ppermute | solution.py:166
  13.4 4.0 %collective-permute-start.9 = (bf16[128,256]{1,0:T(8,128)(2,1)S(1)}, bf16[128,256]{1,0:T(8,128)(2,1)S(1)}, u32[]{:S(2)}, u32[]{:S(2)}) collective-permute-start(bf16[128,256]{1,0:T(8,128)(2,1)S(1)} %collective-permute-done.5.refs_3_), channel_id=1, source_target_pairs={{0,4},{4,0},{8,12},{12,8},{16,20},{20,16},{24,28},{28,24},{1,5},{5... | collective-permute-start | bytes 196616 | tf_op jit(solution)/shard_map/ppermute | solution.py:166
  15.0 2.4 %collective-permute-start.8 = (bf16[128,256]{1,0:T(8,128)(2,1)S(1)}, bf16[128,256]{1,0:T(8,128)(2,1)S(1)}, u32[]{:S(2)}, u32[]{:S(2)}) collective-permute-start(bf16[128,256]{1,0:T(8,128)(2,1)S(1)} %collective-permute-done.4.refs_2_), channel_id=1, source_target_pairs={{0,4},{4,0},{8,12},{12,8},{16,20},{20,16},{24,28},{28,24},{1,5},{5... | collective-permute-start | bytes 196616 | tf_op jit(solution)/shard_map/ppermute | solution.py:166
  18.0 5.3 %collective-permute-start.11 = (bf16[192,256]{1,0:T(8,128)(2,1)S(1)}, bf16[192,256]{1,0:T(8,128)(2,1)S(1)}, u32[]{:S(2)}, u32[]{:S(2)}) collective-permute-start(bf16[192,256]{1,0:T(8,128)(2,1)S(1)} %get-tuple-element.14), channel_id=1, source_target_pairs={{0,8},{4,12},{8,0},{12,4},{16,24},{20,28},{24,16},{28,20},{1,9},{5... | collective-permute-start | bytes 294920 | tf_op jit(solution)/shard_map/ppermute | solution.py:166
  19.2 7.0 %collective-permute-start.12 = (bf16[192,256]{1,0:T(8,128)(2,1)S(1)}, bf16[192,256]{1,0:T(8,128)(2,1)S(1)}, u32[]{:S(2)}, u32[]{:S(2)}) collective-permute-start(bf16[192,256]{1,0:T(8,128)(2,1)S(1)} %get-tuple-element.15), channel_id=1, source_target_pairs={{0,16},{4,20},{8,24},{12,28},{16,0},{20,4},{24,8},{28,12},{1,17},{... | collective-permute-start | bytes 294920 | tf_op jit(solution)/shard_map/ppermute | solution.py:166
  20.3 5.9 %collective-permute-start.13 = (bf16[192,256]{1,0:T(8,128)(2,1)S(1)}, bf16[192,256]{1,0:T(8,128)(2,1)S(1)}, u32[]{:S(2)}, u32[]{:S(2)}) collective-permute-start(bf16[192,256]{1,0:T(8,128)(2,1)S(1)} %get-tuple-element.16), channel_id=1, source_target_pairs={{0,24},{4,28},{8,16},{12,20},{16,8},{20,12},{24,0},{28,4},{1,25},{... | collective-permute-start | bytes 294920 | tf_op jit(solution)/shard_map/ppermute | solution.py:166
  26.2 4.5 %copy-start.2 = (bf16[256,256]{1,0:T(8,128)(2,1)S(1)}, bf16[256,256]{1,0:T(8,128)(2,1)}, u32[]{:S(2)}) copy-start(bf16[256,256]{1,0:T(8,128)(2,1)} %weight.1) | copy-start | bytes 393220
  26.3 6.6 %collective-permute-start.16 = (bf16[128,256]{1,0:T(8,128)(2,1)S(1)}, bf16[128,256]{1,0:T(8,128)(2,1)S(1)}, u32[]{:S(2)}, u32[]{:S(2)}) collective-permute-start(bf16[128,256]{1,0:T(8,128)(2,1)S(1)} %shard_map.100.refs_0_), channel_id=1, source_target_pairs={{0,3},{1,2},{2,1},{3,0},{4,7},{5,6},{6,5},{7,4},{8,11},{9,10},{10,... | collective-permute-start | bytes 196616 | tf_op jit(solution)/shard_map/ppermute | solution.py:166
  29.1 5.6 %collective-permute-start.15 = (bf16[128,256]{1,0:T(8,128)(2,1)S(1)}, bf16[128,256]{1,0:T(8,128)(2,1)S(1)}, u32[]{:S(2)}, u32[]{:S(2)}) collective-permute-start(bf16[128,256]{1,0:T(8,128)(2,1)S(1)} %shard_map.100.refs_0_), channel_id=1, source_target_pairs={{0,2},{1,3},{2,0},{3,1},{4,6},{5,7},{6,4},{7,5},{8,10},{9,11},{10,... | collective-permute-start | bytes 196616 | tf_op jit(solution)/shard_map/ppermute | solution.py:166
  29.1 5.6 %collective-permute-start.14 = (bf16[128,256]{1,0:T(8,128)(2,1)S(1)}, bf16[128,256]{1,0:T(8,128)(2,1)S(1)}, u32[]{:S(2)}, u32[]{:S(2)}) collective-permute-start(bf16[128,256]{1,0:T(8,128)(2,1)S(1)} %shard_map.100.refs_0_), channel_id=1, source_target_pairs={{0,1},{1,0},{2,3},{3,2},{4,5},{5,4},{6,7},{7,6},{8,9},{9,8},{10,11... | collective-permute-start | bytes 196616 | tf_op jit(solution)/shard_map/ppermute | solution.py:166
  34.7 0.8 %copy-start = (f32[64,256]{1,0:T(8,128)S(1)}, f32[64,256]{1,0:T(8,128)}, u32[]{:S(2)}) copy-start(f32[64,256]{1,0:T(8,128)} %shard_map.99.refs_4_) | copy-start | bytes 196612
  35.5 1.4 %collective-permute-start.17 = (f32[128,256]{1,0:T(8,128)S(1)}, f32[128,256]{1,0:T(8,128)S(1)}, u32[]{:S(2)}, u32[]{:S(2)}) collective-permute-start(f32[128,256]{1,0:T(8,128)S(1)} %shard_map.101.own), channel_id=1, source_target_pairs={{0,4},{4,0},{8,12},{12,8},{16,20},{20,16},{24,28},{28,24},{1,5},{5... | collective-permute-start | bytes 393224 | tf_op jit(solution)/shard_map/ppermute | solution.py:166

commit v3 on v2

v3 whole, which is shorter than its diff:
```python
import functools

import jax
import jax.numpy as jnp
from jax import lax
from jax.experimental import pallas as pl
from jax.experimental.pallas import tpu as pltpu
from jax.sharding import PartitionSpec as P

VMEM = pltpu.VMEM
SMEM = pltpu.SMEM
CORES = 2


def positions():
    row = lax.axis_index("row")
    return row // CORES, row % CORES, lax.axis_index("col")


def turned(k):
    return k & ~3 | (k & 1) << 1 | (k >> 1) & 1


def call(
    body, outs, ins, spaces=None, limit=8 * 2**20, flops=0, scratch=(), out_space=VMEM, alias=None
):
    spaces = spaces or [VMEM] * len(ins)
    moved = sum(x.size * x.dtype.itemsize for x in list(ins) + list(outs))
    return pl.pallas_call(
        body,
        out_shape=outs,
        in_specs=[pl.BlockSpec(memory_space=s) for s in spaces],
        out_specs=[pl.BlockSpec(memory_space=out_space) for _ in outs],
        input_output_aliases=alias or {},
        scratch_shapes=list(scratch),
        compiler_params=pltpu.CompilerParams(vmem_limit_bytes=limit),
        cost_estimate=pl.CostEstimate(flops=flops, bytes_accessed=moved, transcendentals=0),
    )(*ins)


def column(row):
    n = row.shape[1]
    across = lax.broadcasted_iota(jnp.int32, (n, n), 1)
    down = lax.broadcasted_iota(jnp.int32, (n, n), 0)
    return jnp.sum(jnp.where(across == down, row, 0.0), axis=1, keepdims=True)


def scale_nodes(
    features, grad_out, relu_mask, degree, scaled, scale_out, vfeat, vgrad, vmask, vdegree, sems
):
    copies = [
        pltpu.make_async_copy(src, dst, sems.at[n])
        for n, (src, dst) in enumerate(
            ((degree, vdegree), (grad_out, vgrad), (relu_mask, vmask), (features, vfeat))
        )
    ]
    for c in copies:
        c.start()
    for c in copies:
        c.wait()
    nodes = vgrad.shape[0]
    scale = column(lax.rsqrt(vdegree[...].astype(jnp.float32)))
    masked = vgrad[...] * vmask[...].astype(jnp.bfloat16)
    scaled[:nodes] = (masked.astype(jnp.float32) * scale).astype(jnp.bfloat16)
    scaled[nodes:] = (vfeat[...].astype(jnp.float32) * scale).astype(jnp.bfloat16)
    scale_out[...] = scale


def pair_up(scaled, other, pair, pair_left):
    nodes = scaled.shape[0] // 2
    core = positions()[1]
    mine = pl.ds(pl.multiple_of(core * nodes, nodes), nodes)
    theirs = pl.ds(pl.multiple_of((1 - core) * nodes, nodes), nodes)
    sends, stays = jnp.where(core == 0, 0, nodes), jnp.where(core == 0, nodes, 0)
    for out, at in ((pair, sends), (pair_left, stays)):
        rows = pl.ds(pl.multiple_of(at, nodes), nodes)
        out[mine] = scaled[rows]
        out[theirs] = other[rows]


def lay_out(nodes, blocks, slots, count, after, dense):
    block = blocks.shape[-1]
    per_block = block // nodes
    chip, _, col = positions()
    col_blocks = dense.shape[0] // block
    dense[...] = jnp.zeros_like(dense)

    @pl.loop(0, count[0, 0])
    def place(b):
        slot = slots[0, 0, b]
        source = (slot // col_blocks) ^ (col // per_block)
        target = (slot % col_blocks) ^ chip
        value = blocks[0, 0, b]
        swapped = jnp.concatenate([value[nodes:], value[:nodes]], axis=0)
        value = jnp.where(col % per_block == 1, swapped, value).T
        rows = pl.ds(pl.multiple_of(target * block, block), block)
        columns = pl.ds(pl.multiple_of(source * block, block), block)
        dense[rows, columns] = value


def multiply(nodes, chips, cols, refs):
    own, other = refs[:2]
    first, second = refs[2 : 2 + cols], refs[2 + cols : 2 + 2 * cols]
    leave, stay, chunks, chunk_sends = refs[2 + 2 * cols :]
    core = positions()[1]
    width = leave.shape[1]
    half = leave.shape[0]
    grads = [jnp.where(core == 1, f[...], s[...]) for f, s in zip(first, second)]
    feats = [jnp.where(core == 1, s[...], f[...]) for f, s in zip(first, second)]
    by_core = [
        jnp.concatenate([g[c * nodes : (c + 1) * nodes] for g in grads], axis=0)
        for c in range(CORES)
    ]
    mine = jnp.where(core == 1, by_core[1], by_core[0])
    theirs = jnp.where(core == 1, by_core[0], by_core[1])
    total = jnp.dot(own[...], mine, preferred_element_type=jnp.float32) + jnp.dot(
        other[...], theirs, preferred_element_type=jnp.float32
    )
    features = jnp.concatenate([feats[turned(k)] for k in range(chips)], axis=0)
    high = total.astype(jnp.bfloat16)
    low = (total - high.astype(jnp.float32)).astype(jnp.bfloat16)
    rows = (((0,), (0,)), ((), ()))
    part = lax.dot_general(features, high, rows, preferred_element_type=jnp.float32)
    part = part + lax.dot_general(features, low, rows, preferred_element_type=jnp.float32)
    part = part.astype(jnp.bfloat16)
    leave[...] = jnp.where(core == 0, part[:half], part[half:])
    stay[...] = jnp.where(core == 0, part[half:], part[:half])

    def chunk(x, k, other):
        at = k * CORES * nodes
        return jnp.where(core == 1 - other, x[at + nodes : at + 2 * nodes], x[at : at + nodes])

    for n, k in enumerate(halving(chips)):
        steps = bin(k).count("1")
        if n < chips // 2:
            chunks[n * nodes : (n + 1) * nodes] = chunk(total, k, steps % 2)
        else:
            at = (n - chips // 2) * nodes
            chunk_sends[at : at + nodes] = chunk(high, k, steps % 2)


def halving(n):
    if n == 1:
        return [0]
    return [2 * k for k in halving(n // 2)] + [2 * k + 1 for k in halving(n // 2)]


def fold(kept, received, keep, send):
    total = kept[...] + received[...].astype(jnp.float32)
    half = keep.shape[0]
    keep[...] = total[:half]
    send[...] = total[half:].astype(jnp.bfloat16)


def tree(terms):
    while len(terms) > 1:
        terms = [a + b for a, b in zip(terms[::2], terms[1::2])]
    return terms[0]


def sum_parts(*refs):
    terms, out = refs[:-2], refs[-1]
    out[...] = tree([t[...].astype(jnp.float32) for t in terms]).astype(jnp.bfloat16)


def mark(after, token):
    token[...] = jnp.zeros_like(token)


def finish_features(kept, received, scale, weight, out, token):
    token[...] = jnp.zeros_like(token)
    total = (kept[...] + received[...].astype(jnp.float32)) * scale[...]
    high = total.astype(jnp.bfloat16)
    low = (total - high.astype(jnp.float32)).astype(jnp.bfloat16)
    last = (((1,), (1,)), ((), ()))
    w = weight[...]
    out[...] = lax.dot_general(high, w, last, preferred_element_type=jnp.float32)
    out[...] += lax.dot_general(low, w, last, preferred_element_type=jnp.float32)


def finish_weight(factor, *refs):
    terms, low, high = refs[:-3], refs[-2], refs[-1]
    total = tree([t[...].astype(jnp.float32) for t in terms]) * factor
    part = low.shape[0]
    low[...] = total[:part]
    high[...] = total[part:]


def place_half(whose, low, high, *refs):
    out, sems = refs[-2:]
    part = low.shape[0]
    core = positions()[1]
    at = (1 - core if whose else core) * 2 * part
    copies = [
        pltpu.make_async_copy(
            src, out.at[pl.ds(pl.multiple_of(at + n * part, part), part)], sems.at[n]
        )
        for n, src in enumerate((low, high))
    ]
    for c in copies:
        c.start()
    for c in copies:
        c.wait()


def local(features, grad_out, relu_mask, degree, weight, adjacency, block_slot, block_count):
    nodes, width = features.shape
    rows = lax.axis_size("row")
    cols = lax.axis_size("col")
    chips = rows // CORES
    half = width // CORES
    bf16, f32 = jnp.bfloat16, jnp.float32
    shape = jax.ShapeDtypeStruct
    assert chips == cols

    def swap(x, k):
        return lax.ppermute(x, "row", [(d, d ^ k) for d in range(rows)])

    def partner(x):
        return swap(x, 1)

    def cross(x, k):
        pairs = []
        for r in range(rows):
            for j in range(cols):
                to = (r ^ 1, j ^ k) if r % CORES == 0 else (r ^ 1 ^ (CORES * turned(k)), j)
                pairs.append((r * cols + j, to[0] * cols + to[1]))
        return lax.ppermute(x, ("row", "col"), pairs)

    def spread(x):
        return [cross(x, k) for k in range(1, cols)]

    scaled, scale = call(
        scale_nodes,
        [shape((2 * nodes, width), bf16), shape((nodes, 1), f32)],
        [
            pltpu.with_memory_space_constraint(x, pltpu.HBM)
            for x in (features, grad_out, relu_mask, degree[None, :])
        ],
        [pl.ANY] * 4,
        scratch=[
            VMEM((nodes, width), bf16), VMEM((nodes, width), bf16),
            VMEM((nodes, width), jnp.int32), VMEM((1, nodes), jnp.int32),
            pltpu.SemaphoreType.DMA((4,)),
        ],
    )
    pair, pair_left = call(
        pair_up, [shape((CORES * nodes, width), bf16)] * 2, [scaled, partner(scaled)]
    )
    moved = spread(pair)
    targets, sources = rows * nodes, cols * nodes
    size = targets * sources * 2
    (dense,) = call(
        functools.partial(lay_out, nodes),
        [shape((targets, sources), bf16)],
        [adjacency, block_slot, block_count, pair],
        [VMEM, SMEM, SMEM, VMEM],
        limit=8 * 2**20 + 3 * size,
    )
    first, second = [pair_left], [pair]
    for n in range(cols - 2, -1, -1):
        moved[n], dense = lax.optimization_barrier((moved[n], dense))
    first += moved
    second += [partner(x) for x in moved]
    leave, stay, kept, leaving = call(
        lambda *refs: multiply(nodes, chips, cols, refs),
        [
            shape((half, width), bf16), shape((half, width), bf16),
            shape((chips // 2 * nodes, width), f32), shape((chips // 2 * nodes, width), bf16),
        ],
        [dense, partner(dense)] + first + second,
        limit=8 * 2**20 + 4 * size,
        flops=4 * targets * sources * width + 4 * targets * width * width,
    )
    bit = 1
    while 2 * bit < chips:
        received = swap(leaving, CORES * bit + 1)
        bit *= 2
        count = chips // (2 * bit)
        kept, leaving = call(
            fold,
            [shape((count * nodes, width), f32), shape((count * nodes, width), bf16)],
            [kept, received],
        )
    received = swap(leaving, CORES * bit + 1)
    (landed,) = call(mark, [shape((8, 128), f32)], [received])
    grad_features, token = call(
        finish_features,
        [shape((nodes, width), f32), shape((8, 128), f32)],
        [kept, received, scale, weight],
        flops=4 * nodes * width * width,
    )
    (once,) = call(sum_parts, [shape((half, width), bf16)], [stay] + spread(leave) + [landed])
    factor = (nodes * rows * cols) ** (-0.5)
    own = call(
        functools.partial(finish_weight, factor),
        [shape((half // 2, width), f32)] * 2,
        [partner(once)] + spread(once) + [token],
    )
    other = [partner(x) for x in own]
    full = [shape((width, width), f32)]
    sems = [pltpu.SemaphoreType.DMA((2,))]
    held = call(functools.partial(place_half, 0), full, own, scratch=sems, out_space=pl.ANY)
    (weight_grad,) = call(
        functools.partial(place_half, 1), full, other + list(held), [VMEM, VMEM, pl.ANY],
        scratch=sems, out_space=pl.ANY, alias={2: 0},
    )
    return grad_features, weight_grad


def solution(mesh):
    placed = (
        P(("row", "col"), None),
        P(("row", "col"), None),
        P(("row", "col"), None),
        P(("row", "col")),
        P(),
        P("row", "col", None, None, None),
        P("row", "col", None),
        P("row", "col"),
    )
    return jax.shard_map(
        local, mesh=mesh, in_specs=placed, out_specs=(P(("row", "col"), None), P()), check_vma=False
    )
```

time: 38.1 us -> 33.3 us (0.87)
  local copies, waits for them, and re-layouts: 3.86 us -> 0.02 us
  waiting for transfers between devices: 12.2 us -> 9.09 us
  starting transfers between devices: 16.1 us -> 17.9 us
  Pallas kernels: 4.09 us -> 4.72 us
    unnamed x16 -> x6, local copies, waits for them, and re-layouts: 3.86 us -> 0.02 us
    ppermute x18 -> x19, waiting for transfers between devices: 12.2 us -> 9.09 us  [the longest x10 4.73 us: swap(): return lax.ppermute(x, 'row', [(d, d ^ k) for d in range(rows)])]
    ppermute x18 -> x19, starting transfers between devices: 16.1 us -> 17.9 us  [the longest x9 12 us: cross(): return lax.ppermute(x, ('row', 'col'), pairs)]
    pallas_call x8 -> x11, Pallas kernels: 4.09 us -> 4.72 us  [call(): pl.pallas_call(body, out_shape=outs, in_specs=[pl.BlockSpec(memory_space=...]
  transfers between devices with their start and end apart: 18 -> 19, of which waited for: 9 -> 12; matrix products, arithmetic and copies ran while one was open for 0% -> 0% of each run, Pallas kernels for 7% -> 7%
where the time goes in v3:
time: 33.3 us; the launch traced here: 33.2 us
  starting transfers between devices  17.9 us (54%)
  waiting for transfers between devices  9.09 us (27%)
  Pallas kernels  4.72 us (14%)
  between operations  1.41 us (4%)
    ppermute x9, starting transfers between devices, cross(): return lax.ppermute(x, ('row', 'col'), pairs)  12 us
    ppermute x10, starting transfers between devices, swap(): return lax.ppermute(x, 'row', [(d, d ^ k) for d in range(rows)])  5.95 us
    ppermute x10, waiting for transfers between devices, swap(): return lax.ppermute(x, 'row', [(d, d ^ k) for d in range(rows)])  4.73 us
    pallas_call x11, Pallas kernels, call(): pl.pallas_call(body, out_shape=outs, in_specs=[pl.BlockSpec(memory_space=...  4.72 us
    ppermute x9, waiting for transfers between devices, cross(): return lax.ppermute(x, ('row', 'col'), pairs)  4.36 us
  transfers between devices with their start and end apart: 19, of which 12 were waited for; matrix products, arithmetic and copies ran while one was open for 0% of the time, Pallas kernels for 7%

profile of v3, /device:TPU:0, one launch (start us, length us, event | category | flops | bytes accessed | tf_op | source)
XLA Modules:
  0.0 33.2 jit_solution(13213506203443184)
XLA Ops:
  0.6 0.0 copy-start
  0.6 1.0 %shard_map.95 = (bf16[128,256]{1,0:T(8,128)(2,1)S(1)}, f32[64,1]{1,0:T(8,128)S(1)}) custom-call(bf16[64,256]{1,0:T(8,128)(2,1)} %features.1, bf16[64,256]{1,0:T(8,128)(2,1)} %grad_out.1, s32[64,256]{1,0:T(8,128)} %relu_mask.1, s32[1,64]{1,0:T(1,128)} %bitcast.1), custom_call_target="tpu_custom_call" | custom-call | bytes 197120 | tf_op jit(solution)/shard_map/pallas_call | solution.py:29
  1.7 0.5 %collective-permute-start = (bf16[128,256]{1,0:T(8,128)(2,1)S(1)}, bf16[128,256]{1,0:T(8,128)(2,1)S(1)}, u32[]{:S(2)}, u32[]{:S(2)}) collective-permute-start(bf16[128,256]{1,0:T(8,128)(2,1)S(1)} %get-tuple-element.22.scaled), channel_id=1, source_target_pairs={{0,4},{4,0},{8,12},{12,8},{16,20},{20,16},{24,28},{28,24},{1,5},{5... | collective-permute-start | bytes 196616 | tf_op jit(solution)/shard_map/ppermute | solution.py:217
  2.2 0.9 %collective-permute-done.other = bf16[128,256]{1,0:T(8,128)(2,1)S(1)} collective-permute-done((bf16[128,256]{1,0:T(8,128)(2,1)S(1)}, bf16[128,256]{1,0:T(8,128)(2,1)S(1)}, u32[]{:S(2)}, u32[]{:S(2)}) %collective-permute-start) | collective-permute-done | bytes 65568 | tf_op jit(solution)/shard_map/ppermute | solution.py:217
  3.1 0.0 copy-start.2
  3.1 4.8 %collective-permute-start.3 = (bf16[128,256]{1,0:T(8,128)(2,1)S(1)}, bf16[128,256]{1,0:T(8,128)(2,1)S(1)}, u32[]{:S(2)}, u32[]{:S(2)}) collective-permute-start(bf16[128,256]{1,0:T(8,128)(2,1)S(1)} %get-tuple-element.23.after.refs_6_), channel_id=1, source_target_pairs={{0,7},{1,6},{2,5},{3,4},{4,24},{5,25},{6,26},{7,27},{8,15},{9,14},... | collective-permute-start | bytes 196616 | tf_op jit(solution)/shard_map/ppermute | solution.py:228
  7.9 1.4 %collective-permute-start.2 = (bf16[128,256]{1,0:T(8,128)(2,1)S(1)}, bf16[128,256]{1,0:T(8,128)(2,1)S(1)}, u32[]{:S(2)}, u32[]{:S(2)}) collective-permute-start(bf16[128,256]{1,0:T(8,128)(2,1)S(1)} %get-tuple-element.23.after.refs_6_), channel_id=1, source_target_pairs={{0,6},{1,7},{2,4},{3,5},{4,8},{5,9},{6,10},{7,11},{8,14},{9,15},{1... | collective-permute-start | bytes 196616 | tf_op jit(solution)/shard_map/ppermute | solution.py:228
  9.3 0.0 collective-permute-start.1
  10.0 0.6 %shard_map.97.refs_0_ = bf16[512,256]{1,0:T(8,128)(2,1)S(1)} custom-call(bf16[1,1,6,128,128]{4,3,2,1,0:T(8,128)(2,1)S(1)} %copy-done, s32[1,1,6]{2,1,0:T(1,128)S(1)} %copy-done.2, s32[1,1]{1,0:T(1,128)S(6)} %copy.12.count, bf16[128,256]{1,0:T(8,128)(2,1)S(1)} %get-tuple-element.23.after.refs_6_), custom_call_target="tpu_custom_call" | custom-call | bytes 524316 | tf_op jit(solution)/shard_map/pallas_call | solution.py:29
  10.6 0.0 collective-permute-done.3.refs_5_
  10.6 1.0 %collective-permute-done.2.refs_4_ = bf16[128,256]{1,0:T(8,128)(2,1)S(1)} collective-permute-done((bf16[128,256]{1,0:T(8,128)(2,1)S(1)}, bf16[128,256]{1,0:T(8,128)(2,1)S(1)}, u32[]{:S(2)}, u32[]{:S(2)}) %collective-permute-start.2) | collective-permute-done | bytes 65568 | tf_op jit(solution)/shard_map/ppermute | solution.py:228
  11.6 1.4 %collective-permute-done.1.refs_3_ = bf16[128,256]{1,0:T(8,128)(2,1)S(1)} collective-permute-done((bf16[128,256]{1,0:T(8,128)(2,1)S(1)}, bf16[128,256]{1,0:T(8,128)(2,1)S(1)}, u32[]{:S(2)}, u32[]{:S(2)}) %collective-permute-start.1) | collective-permute-done | bytes 65568 | tf_op jit(solution)/shard_map/ppermute | solution.py:228
  13.0 0.2 collective-permute-start.4
  13.2 0.3 collective-permute-start.5
  13.5 0.2 collective-permute-start.6
  13.7 0.3 collective-permute-start.7
  14.0 0.6 %collective-permute-done.5.refs_7_ = bf16[128,256]{1,0:T(8,128)(2,1)S(1)} collective-permute-done((bf16[128,256]{1,0:T(8,128)(2,1)S(1)}, bf16[128,256]{1,0:T(8,128)(2,1)S(1)}, u32[]{:S(2)}, u32[]{:S(2)}) %collective-permute-start.5) | collective-permute-done | bytes 65568 | tf_op jit(solution)/shard_map/ppermute | solution.py:217
  14.6 0.1 collective-permute-done.6.refs_8_
  14.8 0.2 collective-permute-done.7.refs_9_
  15.0 0.0 collective-permute-done.4.refs_1_
  15.0 0.8 %shard_map.98 = (bf16[128,256]{1,0:T(8,128)(2,1)S(1)}, bf16[128,256]{1,0:T(8,128)(2,1)S(1)}, f32[128,256]{1,0:T(8,128)S(1)}, bf16[128,256]{1,0:T(8,128)(2,1)S(1)}) custom-call(bf16[512,256]{1,0:T(8,128)(2,1)S(1)} %shard_map.97.refs_0_, bf16[512,256]{1,0:T(8,128)(2,1)S(1)} %collective-permute-done.4.refs_1_, bf16[128,256]{1,0:T(8,128)(2,1)S(1)} %get-tuple-element.27.refs_2_, ...), custom_call_target="tpu_custom_call" | custom-call | flops 268435456 | bytes 1376256 | tf_op jit(solution)/shard_map/pallas_call | solution.py:29
  15.7 0.5 %collective-permute-start.8 = (bf16[128,256]{1,0:T(8,128)(2,1)S(1)}, bf16[128,256]{1,0:T(8,128)(2,1)S(1)}, u32[]{:S(2)}, u32[]{:S(2)}) collective-permute-start(bf16[128,256]{1,0:T(8,128)(2,1)S(1)} %get-tuple-element.32), channel_id=1, source_target_pairs={{0,12},{4,8},{8,4},{12,0},{16,28},{20,24},{24,20},{28,16},{1,13},{... | collective-permute-start | bytes 196616 | tf_op jit(solution)/shard_map/ppermute | solution.py:217
  16.2 2.8 %collective-permute-start.12 = (bf16[128,256]{1,0:T(8,128)(2,1)S(1)}, bf16[128,256]{1,0:T(8,128)(2,1)S(1)}, u32[]{:S(2)}, u32[]{:S(2)}) collective-permute-start(bf16[128,256]{1,0:T(8,128)(2,1)S(1)} %get-tuple-element.38), channel_id=1, source_target_pairs={{0,7},{1,6},{2,5},{3,4},{4,24},{5,25},{6,26},{7,27},{8,15},{9,14},... | collective-permute-start | bytes 196616 | tf_op jit(solution)/shard_map/ppermute | solution.py:228
  19.0 0.0 collective-permute-start.11
  19.0 0.0 collective-permute-start.10
  19.0 0.8 %collective-permute-done.8.received = bf16[128,256]{1,0:T(8,128)(2,1)S(1)} collective-permute-done((bf16[128,256]{1,0:T(8,128)(2,1)S(1)}, bf16[128,256]{1,0:T(8,128)(2,1)S(1)}, u32[]{:S(2)}, u32[]{:S(2)}) %collective-permute-start.8) | collective-permute-done | bytes 65568 | tf_op jit(solution)/shard_map/ppermute | solution.py:217
  19.8 2.0 %collective-permute-start.9 = (bf16[64,256]{1,0:T(8,128)(2,1)S(1)}, bf16[64,256]{1,0:T(8,128)(2,1)S(1)}, u32[]{:S(2)}, u32[]{:S(2)}) collective-permute-start(bf16[64,256]{1,0:T(8,128)(2,1)S(1)} %get-tuple-element.34), channel_id=1, source_target_pairs={{0,20},{4,16},{8,28},{12,24},{16,4},{20,0},{24,12},{28,8},{1,21},{... | collective-permute-start | bytes 98312 | tf_op jit(solution)/shard_map/ppermute | solution.py:217
  21.9 1.6 %collective-permute-done.9.received.after = bf16[64,256]{1,0:T(8,128)(2,1)S(1)} collective-permute-done((bf16[64,256]{1,0:T(8,128)(2,1)S(1)}, bf16[64,256]{1,0:T(8,128)(2,1)S(1)}, u32[]{:S(2)}, u32[]{:S(2)}) %collective-permute-start.9) | collective-permute-done | bytes 32800 | tf_op jit(solution)/shard_map/ppermute | solution.py:217
  23.5 0.0 collective-permute-done.12.refs_3_
  23.5 0.0 collective-permute-done.11.refs_2_
  23.5 0.0 collective-permute-done.10.refs_1_
  23.5 0.0 copy-start.1
  23.5 3.0 %collective-permute-start.16 = (bf16[128,256]{1,0:T(8,128)(2,1)S(1)}, bf16[128,256]{1,0:T(8,128)(2,1)S(1)}, u32[]{:S(2)}, u32[]{:S(2)}) collective-permute-start(bf16[128,256]{1,0:T(8,128)(2,1)S(1)} %shard_map.102), channel_id=1, source_target_pairs={{0,7},{1,6},{2,5},{3,4},{4,24},{5,25},{6,26},{7,27},{8,15},{9,14},... | collective-permute-start | bytes 196616 | tf_op jit(solution)/shard_map/ppermute | solution.py:228
  26.5 0.0 collective-permute-start.15
  26.5 0.1 collective-permute-start.14
  26.6 0.8 %collective-permute-start.13 = (bf16[128,256]{1,0:T(8,128)(2,1)S(1)}, bf16[128,256]{1,0:T(8,128)(2,1)S(1)}, u32[]{:S(2)}, u32[]{:S(2)}) collective-permute-start(bf16[128,256]{1,0:T(8,128)(2,1)S(1)} %shard_map.102), channel_id=1, source_target_pairs={{0,4},{4,0},{8,12},{12,8},{16,20},{20,16},{24,28},{28,24},{1,5},{5... | collective-permute-start | bytes 196616 | tf_op jit(solution)/shard_map/ppermute | solution.py:217
  27.3 0.0 copy-done.1
  27.3 0.8 %shard_map.100 = (f32[64,256]{1,0:T(8,128)}, f32[8,128]{1,0:T(8,128)S(1)}) custom-call(f32[64,256]{1,0:T(8,128)S(1)} %get-tuple-element.33.kept, bf16[64,256]{1,0:T(8,128)(2,1)S(1)} %collective-permute-done.9.received.after, f32[64,1]{1,0:T(8,128)S(1)} %get-tuple-element.35.scale, bf16[256,256]{1,0:T(8,128)(2,1)S(1)} %copy-done.1), custom_call_target="tpu_custom_call" | custom-call | flops 16777216 | bytes 299264 | tf_op jit(solution)/shard_map/pallas_call | solution.py:29
  28.2 0.2 collective-permute-done.16.refs_3_
  28.4 1.8 %collective-permute-done.15.refs_2_ = bf16[128,256]{1,0:T(8,128)(2,1)S(1)} collective-permute-done((bf16[128,256]{1,0:T(8,128)(2,1)S(1)}, bf16[128,256]{1,0:T(8,128)(2,1)S(1)}, u32[]{:S(2)}, u32[]{:S(2)}) %collective-permute-start.15) | collective-permute-done | bytes 65568 | tf_op jit(solution)/shard_map/ppermute | solution.py:228
  30.2 0.0 collective-permute-done.14.refs_1_
  30.2 0.0 collective-permute-done.13.refs_0_
  30.2 1.0 %collective-permute-start.17 = (f32[64,256]{1,0:T(8,128)S(1)}, f32[64,256]{1,0:T(8,128)S(1)}, u32[]{:S(2)}, u32[]{:S(2)}) collective-permute-start(f32[64,256]{1,0:T(8,128)S(1)} %get-tuple-element.40.low), channel_id=1, source_target_pairs={{0,4},{4,0},{8,12},{12,8},{16,20},{20,16},{24,28},{28,24},{1,5},{5... | collective-permute-start | bytes 196616 | tf_op jit(solution)/shard_map/ppermute | solution.py:217
  31.2 0.1 collective-permute-start.18
  31.3 0.7 %shard_map.104.refs_0_ = f32[256,256]{1,0:T(8,128)} custom-call(f32[64,256]{1,0:T(8,128)S(1)} %get-tuple-element.40.low, f32[64,256]{1,0:T(8,128)S(1)} %get-tuple-element.41.high), custom_call_target="tpu_custom_call" | custom-call | bytes 393216 | tf_op jit(solution)/shard_map/pallas_call | solution.py:29
  32.0 0.1 collective-permute-done.17.low
  32.1 0.4 %collective-permute-done.18.high = f32[64,256]{1,0:T(8,128)S(1)} collective-permute-done((f32[64,256]{1,0:T(8,128)S(1)}, f32[64,256]{1,0:T(8,128)S(1)}, u32[]{:S(2)}, u32[]{:S(2)}) %collective-permute-start.18) | collective-permute-done | bytes 65568 | tf_op jit(solution)/shard_map/ppermute | solution.py:217
  32.5 0.7 %shard_map.105 = f32[256,256]{1,0:T(8,128)} custom-call(f32[64,256]{1,0:T(8,128)S(1)} %collective-permute-done.17.low, f32[64,256]{1,0:T(8,128)S(1)} %collective-permute-done.18.high, f32[256,256]{1,0:T(8,128)} %shard_map.104.refs_0_), custom_call_target="tpu_custom_call", output_to_operand_aliasing={{}: (2, {})} | custom-call | bytes 655360 | tf_op jit(solution)/shard_map/pallas_call | solution.py:29
  (7 shorter events, 0.1 us)
Async XLA Ops:
  0.6 9.3 %copy-start = (bf16[1,1,6,128,128]{4,3,2,1,0:T(8,128)(2,1)S(1)}, bf16[1,1,6,128,128]{4,3,2,1,0:T(8,128)(2,1)}, u32[]{:S(2)}) copy-start(bf16[1,1,6,128,128]{4,3,2,1,0:T(8,128)(2,1)} %blocks.1) | copy-start | bytes 589828
  1.7 1.4 %collective-permute-start = (bf16[128,256]{1,0:T(8,128)(2,1)S(1)}, bf16[128,256]{1,0:T(8,128)(2,1)S(1)}, u32[]{:S(2)}, u32[]{:S(2)}) collective-permute-start(bf16[128,256]{1,0:T(8,128)(2,1)S(1)} %get-tuple-element.22.scaled), channel_id=1, source_target_pairs={{0,4},{4,0},{8,12},{12,8},{16,20},{20,16},{24,28},{28,24},{1,5},{5... | collective-permute-start | bytes 196616 | tf_op jit(solution)/shard_map/ppermute | solution.py:217
  3.1 6.8 %copy-start.2 = (s32[1,1,6]{2,1,0:T(1,128)S(1)}, s32[1,1,6]{2,1,0:T(1,128)}, u32[]{:S(2)}) copy-start(s32[1,1,6]{2,1,0:T(1,128)} %slots.1) | copy-start | bytes 76
  3.1 7.5 %collective-permute-start.3 = (bf16[128,256]{1,0:T(8,128)(2,1)S(1)}, bf16[128,256]{1,0:T(8,128)(2,1)S(1)}, u32[]{:S(2)}, u32[]{:S(2)}) collective-permute-start(bf16[128,256]{1,0:T(8,128)(2,1)S(1)} %get-tuple-element.23.after.refs_6_), channel_id=1, source_target_pairs={{0,7},{1,6},{2,5},{3,4},{4,24},{5,25},{6,26},{7,27},{8,15},{9,14},... | collective-permute-start | bytes 196616 | tf_op jit(solution)/shard_map/ppermute | solution.py:228
  7.9 3.7 %collective-permute-start.2 = (bf16[128,256]{1,0:T(8,128)(2,1)S(1)}, bf16[128,256]{1,0:T(8,128)(2,1)S(1)}, u32[]{:S(2)}, u32[]{:S(2)}) collective-permute-start(bf16[128,256]{1,0:T(8,128)(2,1)S(1)} %get-tuple-element.23.after.refs_6_), channel_id=1, source_target_pairs={{0,6},{1,7},{2,4},{3,5},{4,8},{5,9},{6,10},{7,11},{8,14},{9,15},{1... | collective-permute-start | bytes 196616 | tf_op jit(solution)/shard_map/ppermute | solution.py:228
  9.3 3.7 %collective-permute-start.1 = (bf16[128,256]{1,0:T(8,128)(2,1)S(1)}, bf16[128,256]{1,0:T(8,128)(2,1)S(1)}, u32[]{:S(2)}, u32[]{:S(2)}) collective-permute-start(bf16[128,256]{1,0:T(8,128)(2,1)S(1)} %get-tuple-element.23.after.refs_6_), channel_id=1, source_target_pairs={{0,5},{1,4},{2,7},{3,6},{4,16},{5,17},{6,18},{7,19},{8,13},{9,12},... | collective-permute-start | bytes 196616 | tf_op jit(solution)/shard_map/ppermute | solution.py:228
  13.0 2.0 %collective-permute-start.4 = (bf16[512,256]{1,0:T(8,128)(2,1)S(1)}, bf16[512,256]{1,0:T(8,128)(2,1)S(1)}, u32[]{:S(2)}, u32[]{:S(2)}) collective-permute-start(bf16[512,256]{1,0:T(8,128)(2,1)S(1)} %shard_map.97.refs_0_), channel_id=1, source_target_pairs={{0,4},{4,0},{8,12},{12,8},{16,20},{20,16},{24,28},{28,24},{1,5},{5... | collective-permute-start | bytes 786440 | tf_op jit(solution)/shard_map/ppermute | solution.py:217
  13.2 1.4 %collective-permute-start.5 = (bf16[128,256]{1,0:T(8,128)(2,1)S(1)}, bf16[128,256]{1,0:T(8,128)(2,1)S(1)}, u32[]{:S(2)}, u32[]{:S(2)}) collective-permute-start(bf16[128,256]{1,0:T(8,128)(2,1)S(1)} %collective-permute-done.1.refs_3_), channel_id=1, source_target_pairs={{0,4},{4,0},{8,12},{12,8},{16,20},{20,16},{24,28},{28,24},{1,5},{5... | collective-permute-start | bytes 196616 | tf_op jit(solution)/shard_map/ppermute | solution.py:217
  13.5 1.3 %collective-permute-start.6 = (bf16[128,256]{1,0:T(8,128)(2,1)S(1)}, bf16[128,256]{1,0:T(8,128)(2,1)S(1)}, u32[]{:S(2)}, u32[]{:S(2)}) collective-permute-start(bf16[128,256]{1,0:T(8,128)(2,1)S(1)} %collective-permute-done.2.refs_4_), channel_id=1, source_target_pairs={{0,4},{4,0},{8,12},{12,8},{16,20},{20,16},{24,28},{28,24},{1,5},{5... | collective-permute-start | bytes 196616 | tf_op jit(solution)/shard_map/ppermute | solution.py:217
  13.7 1.3 %collective-permute-start.7 = (bf16[128,256]{1,0:T(8,128)(2,1)S(1)}, bf16[128,256]{1,0:T(8,128)(2,1)S(1)}, u32[]{:S(2)}, u32[]{:S(2)}) collective-permute-start(bf16[128,256]{1,0:T(8,128)(2,1)S(1)} %collective-permute-done.3.refs_5_), channel_id=1, source_target_pairs={{0,4},{4,0},{8,12},{12,8},{16,20},{20,16},{24,28},{28,24},{1,5},{5... | collective-permute-start | bytes 196616 | tf_op jit(solution)/shard_map/ppermute | solution.py:217
  15.7 4.1 %collective-permute-start.8 = (bf16[128,256]{1,0:T(8,128)(2,1)S(1)}, bf16[128,256]{1,0:T(8,128)(2,1)S(1)}, u32[]{:S(2)}, u32[]{:S(2)}) collective-permute-start(bf16[128,256]{1,0:T(8,128)(2,1)S(1)} %get-tuple-element.32), channel_id=1, source_target_pairs={{0,12},{4,8},{8,4},{12,0},{16,28},{20,24},{24,20},{28,16},{1,13},{... | collective-permute-start | bytes 196616 | tf_op jit(solution)/shard_map/ppermute | solution.py:217
  16.2 7.2 %collective-permute-start.12 = (bf16[128,256]{1,0:T(8,128)(2,1)S(1)}, bf16[128,256]{1,0:T(8,128)(2,1)S(1)}, u32[]{:S(2)}, u32[]{:S(2)}) collective-permute-start(bf16[128,256]{1,0:T(8,128)(2,1)S(1)} %get-tuple-element.38), channel_id=1, source_target_pairs={{0,7},{1,6},{2,5},{3,4},{4,24},{5,25},{6,26},{7,27},{8,15},{9,14},... | collective-permute-start | bytes 196616 | tf_op jit(solution)/shard_map/ppermute | solution.py:228
  19.0 4.5 %collective-permute-start.11 = (bf16[128,256]{1,0:T(8,128)(2,1)S(1)}, bf16[128,256]{1,0:T(8,128)(2,1)S(1)}, u32[]{:S(2)}, u32[]{:S(2)}) collective-permute-start(bf16[128,256]{1,0:T(8,128)(2,1)S(1)} %get-tuple-element.38), channel_id=1, source_target_pairs={{0,6},{1,7},{2,4},{3,5},{4,8},{5,9},{6,10},{7,11},{8,14},{9,15},{1... | collective-permute-start | bytes 196616 | tf_op jit(solution)/shard_map/ppermute | solution.py:228
  19.0 4.5 %collective-permute-start.10 = (bf16[128,256]{1,0:T(8,128)(2,1)S(1)}, bf16[128,256]{1,0:T(8,128)(2,1)S(1)}, u32[]{:S(2)}, u32[]{:S(2)}) collective-permute-start(bf16[128,256]{1,0:T(8,128)(2,1)S(1)} %get-tuple-element.38), channel_id=1, source_target_pairs={{0,5},{1,4},{2,7},{3,6},{4,16},{5,17},{6,18},{7,19},{8,13},{9,12},... | collective-permute-start | bytes 196616 | tf_op jit(solution)/shard_map/ppermute | solution.py:228
  19.8 3.6 %collective-permute-start.9 = (bf16[64,256]{1,0:T(8,128)(2,1)S(1)}, bf16[64,256]{1,0:T(8,128)(2,1)S(1)}, u32[]{:S(2)}, u32[]{:S(2)}) collective-permute-start(bf16[64,256]{1,0:T(8,128)(2,1)S(1)} %get-tuple-element.34), channel_id=1, source_target_pairs={{0,20},{4,16},{8,28},{12,24},{16,4},{20,0},{24,12},{28,8},{1,21},{... | collective-permute-start | bytes 98312 | tf_op jit(solution)/shard_map/ppermute | solution.py:217
  23.5 3.9 %copy-start.1 = (bf16[256,256]{1,0:T(8,128)(2,1)S(1)}, bf16[256,256]{1,0:T(8,128)(2,1)}, u32[]{:S(2)}) copy-start(bf16[256,256]{1,0:T(8,128)(2,1)} %weight.1) | copy-start | bytes 393220
  23.5 4.9 %collective-permute-start.16 = (bf16[128,256]{1,0:T(8,128)(2,1)S(1)}, bf16[128,256]{1,0:T(8,128)(2,1)S(1)}, u32[]{:S(2)}, u32[]{:S(2)}) collective-permute-start(bf16[128,256]{1,0:T(8,128)(2,1)S(1)} %shard_map.102), channel_id=1, source_target_pairs={{0,7},{1,6},{2,5},{3,4},{4,24},{5,25},{6,26},{7,27},{8,15},{9,14},... | collective-permute-start | bytes 196616 | tf_op jit(solution)/shard_map/ppermute | solution.py:228
  26.5 3.7 %collective-permute-start.15 = (bf16[128,256]{1,0:T(8,128)(2,1)S(1)}, bf16[128,256]{1,0:T(8,128)(2,1)S(1)}, u32[]{:S(2)}, u32[]{:S(2)}) collective-permute-start(bf16[128,256]{1,0:T(8,128)(2,1)S(1)} %shard_map.102), channel_id=1, source_target_pairs={{0,6},{1,7},{2,4},{3,5},{4,8},{5,9},{6,10},{7,11},{8,14},{9,15},{1... | collective-permute-start | bytes 196616 | tf_op jit(solution)/shard_map/ppermute | solution.py:228
  26.5 3.7 %collective-permute-start.14 = (bf16[128,256]{1,0:T(8,128)(2,1)S(1)}, bf16[128,256]{1,0:T(8,128)(2,1)S(1)}, u32[]{:S(2)}, u32[]{:S(2)}) collective-permute-start(bf16[128,256]{1,0:T(8,128)(2,1)S(1)} %shard_map.102), channel_id=1, source_target_pairs={{0,5},{1,4},{2,7},{3,6},{4,16},{5,17},{6,18},{7,19},{8,13},{9,12},... | collective-permute-start | bytes 196616 | tf_op jit(solution)/shard_map/ppermute | solution.py:228
  26.6 3.6 %collective-permute-start.13 = (bf16[128,256]{1,0:T(8,128)(2,1)S(1)}, bf16[128,256]{1,0:T(8,128)(2,1)S(1)}, u32[]{:S(2)}, u32[]{:S(2)}) collective-permute-start(bf16[128,256]{1,0:T(8,128)(2,1)S(1)} %shard_map.102), channel_id=1, source_target_pairs={{0,4},{4,0},{8,12},{12,8},{16,20},{20,16},{24,28},{28,24},{1,5},{5... | collective-permute-start | bytes 196616 | tf_op jit(solution)/shard_map/ppermute | solution.py:217
  30.2 1.9 %collective-permute-start.17 = (f32[64,256]{1,0:T(8,128)S(1)}, f32[64,256]{1,0:T(8,128)S(1)}, u32[]{:S(2)}, u32[]{:S(2)}) collective-permute-start(f32[64,256]{1,0:T(8,128)S(1)} %get-tuple-element.40.low), channel_id=1, source_target_pairs={{0,4},{4,0},{8,12},{12,8},{16,20},{20,16},{24,28},{28,24},{1,5},{5... | collective-permute-start | bytes 196616 | tf_op jit(solution)/shard_map/ppermute | solution.py:217
  31.2 1.3 %collective-permute-start.18 = (f32[64,256]{1,0:T(8,128)S(1)}, f32[64,256]{1,0:T(8,128)S(1)}, u32[]{:S(2)}, u32[]{:S(2)}) collective-permute-start(f32[64,256]{1,0:T(8,128)S(1)} %get-tuple-element.41.high), channel_id=1, source_target_pairs={{0,4},{4,0},{8,12},{12,8},{16,20},{20,16},{24,28},{28,24},{1,5},{5... | collective-permute-start | bytes 196616 | tf_op jit(solution)/shard_map/ppermute | solution.py:217

commit v4 on v3

--- a/solution.py
+++ b/solution.py
@@ -99,9 +99,11 @@
 
 
 def multiply(nodes, chips, cols, refs):
-    own, other = refs[:2]
-    first, second = refs[2 : 2 + cols], refs[2 + cols : 2 + 2 * cols]
-    leave, stay, chunks, chunk_sends = refs[2 + 2 * cols :]
+    own, other, pair, pair_left, brought = refs[:5]
+    rows = CORES * nodes
+    first = [pair_left] + list(refs[5 : 4 + cols])
+    second = [pair] + [brought.at[n * rows : (n + 1) * rows] for n in range(cols - 1)]
+    leave, stay, chunks, chunk_sends = refs[4 + cols :]
     core = positions()[1]
     width = leave.shape[1]
     half = leave.shape[0]
@@ -119,9 +121,9 @@
     features = jnp.concatenate([feats[turned(k)] for k in range(chips)], axis=0)
     high = total.astype(jnp.bfloat16)
     low = (total - high.astype(jnp.float32)).astype(jnp.bfloat16)
-    rows = (((0,), (0,)), ((), ()))
-    part = lax.dot_general(features, high, rows, preferred_element_type=jnp.float32)
-    part = part + lax.dot_general(features, low, rows, preferred_element_type=jnp.float32)
+    first_rows = (((0,), (0,)), ((), ()))
+    part = lax.dot_general(features, high, first_rows, preferred_element_type=jnp.float32)
+    part = part + lax.dot_general(features, low, first_rows, preferred_element_type=jnp.float32)
     part = part.astype(jnp.bfloat16)
     leave[...] = jnp.where(core == 0, part[:half], part[half:])
     stay[...] = jnp.where(core == 0, part[half:], part[:half])
@@ -137,6 +139,13 @@
         else:
             at = (n - chips // 2) * nodes
             chunk_sends[at : at + nodes] = chunk(high, k, steps % 2)
+
+
+def pack(*refs):
+    out = refs[-1]
+    rows = refs[0].shape[0]
+    for n, r in enumerate(refs[:-2]):
+        out[n * rows : (n + 1) * rows] = r[...]
 
 
 def halving(n):
@@ -257,18 +266,15 @@
         [VMEM, SMEM, SMEM, VMEM],
         limit=8 * 2**20 + 3 * size,
     )
-    first, second = [pair_left], [pair]
-    for n in range(cols - 2, -1, -1):
-        moved[n], dense = lax.optimization_barrier((moved[n], dense))
-    first += moved
-    second += [partner(x) for x in moved]
+    (packed,) = call(pack, [shape(((cols - 1) * CORES * nodes, width), bf16)], moved + [dense])
+    brought = partner(packed)
     leave, stay, kept, leaving = call(
         lambda *refs: multiply(nodes, chips, cols, refs),
         [
             shape((half, width), bf16), shape((half, width), bf16),
             shape((chips // 2 * nodes, width), f32), shape((chips // 2 * nodes, width), bf16),
         ],
-        [dense, partner(dense)] + first + second,
+        [dense, partner(dense), pair, pair_left, brought] + moved,
         limit=8 * 2**20 + 4 * size,
         flops=4 * targets * sources * width + 4 * targets * width * width,
     )

time: 33.3 us -> 32.7 us (0.982)
  waiting for transfers between devices: 9.09 us -> 8.42 us
  Pallas kernels: 4.72 us -> 5.12 us
    ppermute x9, waiting for transfers between devices: 4.36 us -> 3.82 us  [cross(): return lax.ppermute(x, ('row', 'col'), pairs)]
    pallas_call x11 -> x12, Pallas kernels: 4.72 us -> 5.12 us  [call(): pl.pallas_call(body, out_shape=outs, in_specs=[pl.BlockSpec(memory_space=...]
    ppermute x10 -> x8, waiting for transfers between devices: 4.73 us -> 4.6 us  [swap(): return lax.ppermute(x, 'row', [(d, d ^ k) for d in range(rows)])]
    ppermute x10 -> x8, starting transfers between devices: 5.95 us -> 5.84 us  [swap(): return lax.ppermute(x, 'row', [(d, d ^ k) for d in range(rows)])]
  transfers between devices with their start and end apart: 19 -> 17, of which waited for: 12 -> 10; matrix products, arithmetic and copies ran while one was open for 0% -> 0% of each run, Pallas kernels for 7% -> 8%
where the time goes in v4:
time: 32.7 us; the launch traced here: 32.6 us
  starting transfers between devices  17.6 us (54%)
  waiting for transfers between devices  8.42 us (26%)
  Pallas kernels  5.12 us (16%)
  between operations  1.39 us (4%)
    ppermute x9, starting transfers between devices, cross(): return lax.ppermute(x, ('row', 'col'), pairs)  11.8 us
    ppermute x8, starting transfers between devices, swap(): return lax.ppermute(x, 'row', [(d, d ^ k) for d in range(rows)])  5.84 us
    pallas_call x12, Pallas kernels, call(): pl.pallas_call(body, out_shape=outs, in_specs=[pl.BlockSpec(memory_space=...  5.12 us
    ppermute x8, waiting for transfers between devices, swap(): return lax.ppermute(x, 'row', [(d, d ^ k) for d in range(rows)])  4.6 us
    ppermute x9, waiting for transfers between devices, cross(): return lax.ppermute(x, ('row', 'col'), pairs)  3.82 us
  transfers between devices with their start and end apart: 17, of which 10 were waited for; matrix products, arithmetic and copies ran while one was open for 0% of the time, Pallas kernels for 8%

profile of v4, /device:TPU:0, one launch (start us, length us, event | category | flops | bytes accessed | tf_op | source)
XLA Modules:
  0.0 32.6 jit_solution(10357247408737733645)
XLA Ops:
  0.6 0.0 copy-start
  0.6 1.0 %shard_map.95 = (bf16[128,256]{1,0:T(8,128)(2,1)S(1)}, f32[64,1]{1,0:T(8,128)S(1)}) custom-call(bf16[64,256]{1,0:T(8,128)(2,1)} %features.1, bf16[64,256]{1,0:T(8,128)(2,1)} %grad_out.1, s32[64,256]{1,0:T(8,128)} %relu_mask.1, s32[1,64]{1,0:T(1,128)} %bitcast.1), custom_call_target="tpu_custom_call" | custom-call | bytes 197120 | tf_op jit(solution)/shard_map/pallas_call | solution.py:29
  1.7 0.5 %collective-permute-start = (bf16[128,256]{1,0:T(8,128)(2,1)S(1)}, bf16[128,256]{1,0:T(8,128)(2,1)S(1)}, u32[]{:S(2)}, u32[]{:S(2)}) collective-permute-start(bf16[128,256]{1,0:T(8,128)(2,1)S(1)} %get-tuple-element.16.scaled), channel_id=1, source_target_pairs={{0,4},{4,0},{8,12},{12,8},{16,20},{20,16},{24,28},{28,24},{1,5},{5... | collective-permute-start | bytes 196616 | tf_op jit(solution)/shard_map/ppermute | solution.py:226
  2.9 0.3 collective-permute-done.other
  3.1 0.0 copy-start.2
  3.1 4.8 %collective-permute-start.4 = (bf16[128,256]{1,0:T(8,128)(2,1)S(1)}, bf16[128,256]{1,0:T(8,128)(2,1)S(1)}, u32[]{:S(2)}, u32[]{:S(2)}) collective-permute-start(bf16[128,256]{1,0:T(8,128)(2,1)S(1)} %get-tuple-element.17.after.refs_2_), channel_id=1, source_target_pairs={{0,7},{1,6},{2,5},{3,4},{4,24},{5,25},{6,26},{7,27},{8,15},{9,14},... | collective-permute-start | bytes 196616 | tf_op jit(solution)/shard_map/ppermute | solution.py:237
  7.9 1.4 %collective-permute-start.3 = (bf16[128,256]{1,0:T(8,128)(2,1)S(1)}, bf16[128,256]{1,0:T(8,128)(2,1)S(1)}, u32[]{:S(2)}, u32[]{:S(2)}) collective-permute-start(bf16[128,256]{1,0:T(8,128)(2,1)S(1)} %get-tuple-element.17.after.refs_2_), channel_id=1, source_target_pairs={{0,6},{1,7},{2,4},{3,5},{4,8},{5,9},{6,10},{7,11},{8,14},{9,15},{1... | collective-permute-start | bytes 196616 | tf_op jit(solution)/shard_map/ppermute | solution.py:237
  9.3 0.0 collective-permute-start.2
  9.3 0.0 copy-done
  9.3 0.0 copy-done.2
  9.3 1.0 %shard_map.97.refs_3_.refs_0_ = bf16[512,256]{1,0:T(8,128)(2,1)S(1)} custom-call(bf16[1,1,6,128,128]{4,3,2,1,0:T(8,128)(2,1)S(1)} %copy-done, s32[1,1,6]{2,1,0:T(1,128)S(1)} %copy-done.2, s32[1,1]{1,0:T(1,128)S(6)} %copy.12.count, bf16[128,256]{1,0:T(8,128)(2,1)S(1)} %get-tuple-element.17.after.refs_2_), custom_call_target="tpu_custom_call" | custom-call | bytes 524316 | tf_op jit(solution)/shard_map/pallas_call | solution.py:29
  10.3 0.5 %collective-permute-start.1 = (bf16[512,256]{1,0:T(8,128)(2,1)S(1)}, bf16[512,256]{1,0:T(8,128)(2,1)S(1)}, u32[]{:S(2)}, u32[]{:S(2)}) collective-permute-start(bf16[512,256]{1,0:T(8,128)(2,1)S(1)} %shard_map.97.refs_3_.refs_0_), channel_id=1, source_target_pairs={{0,4},{4,0},{8,12},{12,8},{16,20},{20,16},{24,28},{28,24},{1,5},{5... | collective-permute-start | bytes 786440 | tf_op jit(solution)/shard_map/ppermute | solution.py:226
  10.9 0.0 collective-permute-done.4.refs_2_.refs_7_
  10.9 0.7 %collective-permute-done.3.refs_1_.refs_6_ = bf16[128,256]{1,0:T(8,128)(2,1)S(1)} collective-permute-done((bf16[128,256]{1,0:T(8,128)(2,1)S(1)}, bf16[128,256]{1,0:T(8,128)(2,1)S(1)}, u32[]{:S(2)}, u32[]{:S(2)}) %collective-permute-start.3) | collective-permute-done | bytes 65568 | tf_op jit(solution)/shard_map/ppermute | solution.py:237
  11.6 1.4 %collective-permute-done.2.refs_0_.refs_5_ = bf16[128,256]{1,0:T(8,128)(2,1)S(1)} collective-permute-done((bf16[128,256]{1,0:T(8,128)(2,1)S(1)}, bf16[128,256]{1,0:T(8,128)(2,1)S(1)}, u32[]{:S(2)}, u32[]{:S(2)}) %collective-permute-start.2) | collective-permute-done | bytes 65568 | tf_op jit(solution)/shard_map/ppermute | solution.py:237
  13.0 0.3 collective-permute-start.5
  13.3 1.2 %collective-permute-done.5.refs_4_ = bf16[384,256]{1,0:T(8,128)(2,1)S(1)} collective-permute-done((bf16[384,256]{1,0:T(8,128)(2,1)S(1)}, bf16[384,256]{1,0:T(8,128)(2,1)S(1)}, u32[]{:S(2)}, u32[]{:S(2)}) %collective-permute-start.5) | collective-permute-done | bytes 196640 | tf_op jit(solution)/shard_map/ppermute | solution.py:226
  14.5 0.0 collective-permute-done.1.refs_1_
  14.5 0.8 %shard_map.99 = (bf16[128,256]{1,0:T(8,128)(2,1)S(1)}, bf16[128,256]{1,0:T(8,128)(2,1)S(1)}, f32[128,256]{1,0:T(8,128)S(1)}, bf16[128,256]{1,0:T(8,128)(2,1)S(1)}) custom-call(bf16[512,256]{1,0:T(8,128)(2,1)S(1)} %shard_map.97.refs_3_.refs_0_, bf16[512,256]{1,0:T(8,128)(2,1)S(1)} %collective-permute-done.1.refs_1_, ...), custom_call_target="tpu_custom_call" | custom-call | flops 268435456 | bytes 1376256 | tf_op jit(solution)/shard_map/pallas_call | solution.py:29
  15.3 0.4 %collective-permute-start.6 = (bf16[128,256]{1,0:T(8,128)(2,1)S(1)}, bf16[128,256]{1,0:T(8,128)(2,1)S(1)}, u32[]{:S(2)}, u32[]{:S(2)}) collective-permute-start(bf16[128,256]{1,0:T(8,128)(2,1)S(1)} %get-tuple-element.20), channel_id=1, source_target_pairs={{0,12},{4,8},{8,4},{12,0},{16,28},{20,24},{24,20},{28,16},{1,13},{... | collective-permute-start | bytes 196616 | tf_op jit(solution)/shard_map/ppermute | solution.py:226
  15.7 2.7 %collective-permute-start.10 = (bf16[128,256]{1,0:T(8,128)(2,1)S(1)}, bf16[128,256]{1,0:T(8,128)(2,1)S(1)}, u32[]{:S(2)}, u32[]{:S(2)}) collective-permute-start(bf16[128,256]{1,0:T(8,128)(2,1)S(1)} %get-tuple-element.26), channel_id=1, source_target_pairs={{0,7},{1,6},{2,5},{3,4},{4,24},{5,25},{6,26},{7,27},{8,15},{9,14},... | collective-permute-start | bytes 196616 | tf_op jit(solution)/shard_map/ppermute | solution.py:237
  18.4 0.0 collective-permute-start.9
  18.4 0.0 collective-permute-start.8
  18.4 1.0 %collective-permute-done.6.received = bf16[128,256]{1,0:T(8,128)(2,1)S(1)} collective-permute-done((bf16[128,256]{1,0:T(8,128)(2,1)S(1)}, bf16[128,256]{1,0:T(8,128)(2,1)S(1)}, u32[]{:S(2)}, u32[]{:S(2)}) %collective-permute-start.6) | collective-permute-done | bytes 65568 | tf_op jit(solution)/shard_map/ppermute | solution.py:226
  19.4 1.9 %collective-permute-start.7 = (bf16[64,256]{1,0:T(8,128)(2,1)S(1)}, bf16[64,256]{1,0:T(8,128)(2,1)S(1)}, u32[]{:S(2)}, u32[]{:S(2)}) collective-permute-start(bf16[64,256]{1,0:T(8,128)(2,1)S(1)} %get-tuple-element.22), channel_id=1, source_target_pairs={{0,20},{4,16},{8,28},{12,24},{16,4},{20,0},{24,12},{28,8},{1,21},{... | collective-permute-start | bytes 98312 | tf_op jit(solution)/shard_map/ppermute | solution.py:226
  21.4 1.6 %collective-permute-done.7.received.after = bf16[64,256]{1,0:T(8,128)(2,1)S(1)} collective-permute-done((bf16[64,256]{1,0:T(8,128)(2,1)S(1)}, bf16[64,256]{1,0:T(8,128)(2,1)S(1)}, u32[]{:S(2)}, u32[]{:S(2)}) %collective-permute-start.7) | collective-permute-done | bytes 32800 | tf_op jit(solution)/shard_map/ppermute | solution.py:226
  23.0 0.0 collective-permute-done.10.refs_3_
  23.0 0.0 collective-permute-done.9.refs_2_
  23.0 0.0 collective-permute-done.8.refs_1_
  23.0 0.0 copy-start.1
  23.1 2.5 %collective-permute-start.14 = (bf16[128,256]{1,0:T(8,128)(2,1)S(1)}, bf16[128,256]{1,0:T(8,128)(2,1)S(1)}, u32[]{:S(2)}, u32[]{:S(2)}) collective-permute-start(bf16[128,256]{1,0:T(8,128)(2,1)S(1)} %shard_map.103), channel_id=1, source_target_pairs={{0,7},{1,6},{2,5},{3,4},{4,24},{5,25},{6,26},{7,27},{8,15},{9,14},... | collective-permute-start | bytes 196616 | tf_op jit(solution)/shard_map/ppermute | solution.py:237
  25.5 0.3 collective-permute-start.13
  25.8 0.1 collective-permute-start.12
  26.0 1.0 %collective-permute-start.11 = (bf16[128,256]{1,0:T(8,128)(2,1)S(1)}, bf16[128,256]{1,0:T(8,128)(2,1)S(1)}, u32[]{:S(2)}, u32[]{:S(2)}) collective-permute-start(bf16[128,256]{1,0:T(8,128)(2,1)S(1)} %shard_map.103), channel_id=1, source_target_pairs={{0,4},{4,0},{8,12},{12,8},{16,20},{20,16},{24,28},{28,24},{1,5},{5... | collective-permute-start | bytes 196616 | tf_op jit(solution)/shard_map/ppermute | solution.py:226
  27.0 0.0 copy-done.1
  27.0 0.8 %shard_map.101 = (f32[64,256]{1,0:T(8,128)}, f32[8,128]{1,0:T(8,128)S(1)}) custom-call(f32[64,256]{1,0:T(8,128)S(1)} %get-tuple-element.21.kept, bf16[64,256]{1,0:T(8,128)(2,1)S(1)} %collective-permute-done.7.received.after, f32[64,1]{1,0:T(8,128)S(1)} %get-tuple-element.23.scale, bf16[256,256]{1,0:T(8,128)(2,1)S(1)} %copy-done.1), custom_call_target="tpu_custom_call" | custom-call | flops 16777216 | bytes 299264 | tf_op jit(solution)/shard_map/pallas_call | solution.py:29
  27.8 0.0 collective-permute-done.14.refs_3_
  27.8 1.4 %collective-permute-done.13.refs_2_ = bf16[128,256]{1,0:T(8,128)(2,1)S(1)} collective-permute-done((bf16[128,256]{1,0:T(8,128)(2,1)S(1)}, bf16[128,256]{1,0:T(8,128)(2,1)S(1)}, u32[]{:S(2)}, u32[]{:S(2)}) %collective-permute-start.13) | collective-permute-done | bytes 65568 | tf_op jit(solution)/shard_map/ppermute | solution.py:237
  29.2 0.3 collective-permute-done.12.refs_1_
  29.5 0.0 collective-permute-done.11.refs_0_
  29.6 1.1 %collective-permute-start.15 = (f32[64,256]{1,0:T(8,128)S(1)}, f32[64,256]{1,0:T(8,128)S(1)}, u32[]{:S(2)}, u32[]{:S(2)}) collective-permute-start(f32[64,256]{1,0:T(8,128)S(1)} %get-tuple-element.28.low), channel_id=1, source_target_pairs={{0,4},{4,0},{8,12},{12,8},{16,20},{20,16},{24,28},{28,24},{1,5},{5... | collective-permute-start | bytes 196616 | tf_op jit(solution)/shard_map/ppermute | solution.py:226
  30.6 0.1 collective-permute-start.16
  30.7 0.7 %shard_map.105.refs_0_ = f32[256,256]{1,0:T(8,128)} custom-call(f32[64,256]{1,0:T(8,128)S(1)} %get-tuple-element.28.low, f32[64,256]{1,0:T(8,128)S(1)} %get-tuple-element.29.high), custom_call_target="tpu_custom_call" | custom-call | bytes 393216 | tf_op jit(solution)/shard_map/pallas_call | solution.py:29
  31.4 0.1 collective-permute-done.15.low
  31.5 0.4 %collective-permute-done.16.high = f32[64,256]{1,0:T(8,128)S(1)} collective-permute-done((f32[64,256]{1,0:T(8,128)S(1)}, f32[64,256]{1,0:T(8,128)S(1)}, u32[]{:S(2)}, u32[]{:S(2)}) %collective-permute-start.16) | collective-permute-done | bytes 65568 | tf_op jit(solution)/shard_map/ppermute | solution.py:226
  31.9 0.7 %shard_map.106 = f32[256,256]{1,0:T(8,128)} custom-call(f32[64,256]{1,0:T(8,128)S(1)} %collective-permute-done.15.low, f32[64,256]{1,0:T(8,128)S(1)} %collective-permute-done.16.high, f32[256,256]{1,0:T(8,128)} %shard_map.105.refs_0_), custom_call_target="tpu_custom_call", output_to_operand_aliasing={{}: (2, {})} | custom-call | bytes 655360 | tf_op jit(solution)/shard_map/pallas_call | solution.py:29
  (6 shorter events, 0.1 us)
Async XLA Ops:
  0.6 8.7 %copy-start = (bf16[1,1,6,128,128]{4,3,2,1,0:T(8,128)(2,1)S(1)}, bf16[1,1,6,128,128]{4,3,2,1,0:T(8,128)(2,1)}, u32[]{:S(2)}) copy-start(bf16[1,1,6,128,128]{4,3,2,1,0:T(8,128)(2,1)} %blocks.1) | copy-start | bytes 589828
  1.7 1.4 %collective-permute-start = (bf16[128,256]{1,0:T(8,128)(2,1)S(1)}, bf16[128,256]{1,0:T(8,128)(2,1)S(1)}, u32[]{:S(2)}, u32[]{:S(2)}) collective-permute-start(bf16[128,256]{1,0:T(8,128)(2,1)S(1)} %get-tuple-element.16.scaled), channel_id=1, source_target_pairs={{0,4},{4,0},{8,12},{12,8},{16,20},{20,16},{24,28},{28,24},{1,5},{5... | collective-permute-start | bytes 196616 | tf_op jit(solution)/shard_map/ppermute | solution.py:226
  3.1 6.2 %copy-start.2 = (s32[1,1,6]{2,1,0:T(1,128)S(1)}, s32[1,1,6]{2,1,0:T(1,128)}, u32[]{:S(2)}) copy-start(s32[1,1,6]{2,1,0:T(1,128)} %slots.1) | copy-start | bytes 76
  3.1 7.7 %collective-permute-start.4 = (bf16[128,256]{1,0:T(8,128)(2,1)S(1)}, bf16[128,256]{1,0:T(8,128)(2,1)S(1)}, u32[]{:S(2)}, u32[]{:S(2)}) collective-permute-start(bf16[128,256]{1,0:T(8,128)(2,1)S(1)} %get-tuple-element.17.after.refs_2_), channel_id=1, source_target_pairs={{0,7},{1,6},{2,5},{3,4},{4,24},{5,25},{6,26},{7,27},{8,15},{9,14},... | collective-permute-start | bytes 196616 | tf_op jit(solution)/shard_map/ppermute | solution.py:237
  7.9 3.7 %collective-permute-start.3 = (bf16[128,256]{1,0:T(8,128)(2,1)S(1)}, bf16[128,256]{1,0:T(8,128)(2,1)S(1)}, u32[]{:S(2)}, u32[]{:S(2)}) collective-permute-start(bf16[128,256]{1,0:T(8,128)(2,1)S(1)} %get-tuple-element.17.after.refs_2_), channel_id=1, source_target_pairs={{0,6},{1,7},{2,4},{3,5},{4,8},{5,9},{6,10},{7,11},{8,14},{9,15},{1... | collective-permute-start | bytes 196616 | tf_op jit(solution)/shard_map/ppermute | solution.py:237
  9.3 3.7 %collective-permute-start.2 = (bf16[128,256]{1,0:T(8,128)(2,1)S(1)}, bf16[128,256]{1,0:T(8,128)(2,1)S(1)}, u32[]{:S(2)}, u32[]{:S(2)}) collective-permute-start(bf16[128,256]{1,0:T(8,128)(2,1)S(1)} %get-tuple-element.17.after.refs_2_), channel_id=1, source_target_pairs={{0,5},{1,4},{2,7},{3,6},{4,16},{5,17},{6,18},{7,19},{8,13},{9,12},... | collective-permute-start | bytes 196616 | tf_op jit(solution)/shard_map/ppermute | solution.py:237
  10.3 4.2 %collective-permute-start.1 = (bf16[512,256]{1,0:T(8,128)(2,1)S(1)}, bf16[512,256]{1,0:T(8,128)(2,1)S(1)}, u32[]{:S(2)}, u32[]{:S(2)}) collective-permute-start(bf16[512,256]{1,0:T(8,128)(2,1)S(1)} %shard_map.97.refs_3_.refs_0_), channel_id=1, source_target_pairs={{0,4},{4,0},{8,12},{12,8},{16,20},{20,16},{24,28},{28,24},{1,5},{5... | collective-permute-start | bytes 786440 | tf_op jit(solution)/shard_map/ppermute | solution.py:226
  13.0 1.5 %collective-permute-start.5 = (bf16[384,256]{1,0:T(8,128)(2,1)S(1)}, bf16[384,256]{1,0:T(8,128)(2,1)S(1)}, u32[]{:S(2)}, u32[]{:S(2)}) collective-permute-start(bf16[384,256]{1,0:T(8,128)(2,1)S(1)} %shard_map.98), channel_id=1, source_target_pairs={{0,4},{4,0},{8,12},{12,8},{16,20},{20,16},{24,28},{28,24},{1,5},{5... | collective-permute-start | bytes 589832 | tf_op jit(solution)/shard_map/ppermute | solution.py:226
  15.3 4.2 %collective-permute-start.6 = (bf16[128,256]{1,0:T(8,128)(2,1)S(1)}, bf16[128,256]{1,0:T(8,128)(2,1)S(1)}, u32[]{:S(2)}, u32[]{:S(2)}) collective-permute-start(bf16[128,256]{1,0:T(8,128)(2,1)S(1)} %get-tuple-element.20), channel_id=1, source_target_pairs={{0,12},{4,8},{8,4},{12,0},{16,28},{20,24},{24,20},{28,16},{1,13},{... | collective-permute-start | bytes 196616 | tf_op jit(solution)/shard_map/ppermute | solution.py:226
  15.7 7.3 %collective-permute-start.10 = (bf16[128,256]{1,0:T(8,128)(2,1)S(1)}, bf16[128,256]{1,0:T(8,128)(2,1)S(1)}, u32[]{:S(2)}, u32[]{:S(2)}) collective-permute-start(bf16[128,256]{1,0:T(8,128)(2,1)S(1)} %get-tuple-element.26), channel_id=1, source_target_pairs={{0,7},{1,6},{2,5},{3,4},{4,24},{5,25},{6,26},{7,27},{8,15},{9,14},... | collective-permute-start | bytes 196616 | tf_op jit(solution)/shard_map/ppermute | solution.py:237
  18.4 4.6 %collective-permute-start.9 = (bf16[128,256]{1,0:T(8,128)(2,1)S(1)}, bf16[128,256]{1,0:T(8,128)(2,1)S(1)}, u32[]{:S(2)}, u32[]{:S(2)}) collective-permute-start(bf16[128,256]{1,0:T(8,128)(2,1)S(1)} %get-tuple-element.26), channel_id=1, source_target_pairs={{0,6},{1,7},{2,4},{3,5},{4,8},{5,9},{6,10},{7,11},{8,14},{9,15},{1... | collective-permute-start | bytes 196616 | tf_op jit(solution)/shard_map/ppermute | solution.py:237
  18.4 4.6 %collective-permute-start.8 = (bf16[128,256]{1,0:T(8,128)(2,1)S(1)}, bf16[128,256]{1,0:T(8,128)(2,1)S(1)}, u32[]{:S(2)}, u32[]{:S(2)}) collective-permute-start(bf16[128,256]{1,0:T(8,128)(2,1)S(1)} %get-tuple-element.26), channel_id=1, source_target_pairs={{0,5},{1,4},{2,7},{3,6},{4,16},{5,17},{6,18},{7,19},{8,13},{9,12},... | collective-permute-start | bytes 196616 | tf_op jit(solution)/shard_map/ppermute | solution.py:237
  19.4 3.5 %collective-permute-start.7 = (bf16[64,256]{1,0:T(8,128)(2,1)S(1)}, bf16[64,256]{1,0:T(8,128)(2,1)S(1)}, u32[]{:S(2)}, u32[]{:S(2)}) collective-permute-start(bf16[64,256]{1,0:T(8,128)(2,1)S(1)} %get-tuple-element.22), channel_id=1, source_target_pairs={{0,20},{4,16},{8,28},{12,24},{16,4},{20,0},{24,12},{28,8},{1,21},{... | collective-permute-start | bytes 98312 | tf_op jit(solution)/shard_map/ppermute | solution.py:226
  23.0 4.0 %copy-start.1 = (bf16[256,256]{1,0:T(8,128)(2,1)S(1)}, bf16[256,256]{1,0:T(8,128)(2,1)}, u32[]{:S(2)}) copy-start(bf16[256,256]{1,0:T(8,128)(2,1)} %weight.1) | copy-start | bytes 393220
  23.1 4.8 %collective-permute-start.14 = (bf16[128,256]{1,0:T(8,128)(2,1)S(1)}, bf16[128,256]{1,0:T(8,128)(2,1)S(1)}, u32[]{:S(2)}, u32[]{:S(2)}) collective-permute-start(bf16[128,256]{1,0:T(8,128)(2,1)S(1)} %shard_map.103), channel_id=1, source_target_pairs={{0,7},{1,6},{2,5},{3,4},{4,24},{5,25},{6,26},{7,27},{8,15},{9,14},... | collective-permute-start | bytes 196616 | tf_op jit(solution)/shard_map/ppermute | solution.py:237
  25.5 3.7 %collective-permute-start.13 = (bf16[128,256]{1,0:T(8,128)(2,1)S(1)}, bf16[128,256]{1,0:T(8,128)(2,1)S(1)}, u32[]{:S(2)}, u32[]{:S(2)}) collective-permute-start(bf16[128,256]{1,0:T(8,128)(2,1)S(1)} %shard_map.103), channel_id=1, source_target_pairs={{0,6},{1,7},{2,4},{3,5},{4,8},{5,9},{6,10},{7,11},{8,14},{9,15},{1... | collective-permute-start | bytes 196616 | tf_op jit(solution)/shard_map/ppermute | solution.py:237
  25.8 3.7 %collective-permute-start.12 = (bf16[128,256]{1,0:T(8,128)(2,1)S(1)}, bf16[128,256]{1,0:T(8,128)(2,1)S(1)}, u32[]{:S(2)}, u32[]{:S(2)}) collective-permute-start(bf16[128,256]{1,0:T(8,128)(2,1)S(1)} %shard_map.103), channel_id=1, source_target_pairs={{0,5},{1,4},{2,7},{3,6},{4,16},{5,17},{6,18},{7,19},{8,13},{9,12},... | collective-permute-start | bytes 196616 | tf_op jit(solution)/shard_map/ppermute | solution.py:237
  26.0 3.5 %collective-permute-start.11 = (bf16[128,256]{1,0:T(8,128)(2,1)S(1)}, bf16[128,256]{1,0:T(8,128)(2,1)S(1)}, u32[]{:S(2)}, u32[]{:S(2)}) collective-permute-start(bf16[128,256]{1,0:T(8,128)(2,1)S(1)} %shard_map.103), channel_id=1, source_target_pairs={{0,4},{4,0},{8,12},{12,8},{16,20},{20,16},{24,28},{28,24},{1,5},{5... | collective-permute-start | bytes 196616 | tf_op jit(solution)/shard_map/ppermute | solution.py:226
  29.6 2.0 %collective-permute-start.15 = (f32[64,256]{1,0:T(8,128)S(1)}, f32[64,256]{1,0:T(8,128)S(1)}, u32[]{:S(2)}, u32[]{:S(2)}) collective-permute-start(f32[64,256]{1,0:T(8,128)S(1)} %get-tuple-element.28.low), channel_id=1, source_target_pairs={{0,4},{4,0},{8,12},{12,8},{16,20},{20,16},{24,28},{28,24},{1,5},{5... | collective-permute-start | bytes 196616 | tf_op jit(solution)/shard_map/ppermute | solution.py:226
  30.6 1.3 %collective-permute-start.16 = (f32[64,256]{1,0:T(8,128)S(1)}, f32[64,256]{1,0:T(8,128)S(1)}, u32[]{:S(2)}, u32[]{:S(2)}) collective-permute-start(f32[64,256]{1,0:T(8,128)S(1)} %get-tuple-element.29.high), channel_id=1, source_target_pairs={{0,4},{4,0},{8,12},{12,8},{16,20},{20,16},{24,28},{28,24},{1,5},{5... | collective-permute-start | bytes 196616 | tf_op jit(solution)/shard_map/ppermute | solution.py:226

commit v5 on v4

--- a/solution.py
+++ b/solution.py
@@ -10,6 +10,7 @@
 VMEM = pltpu.VMEM
 SMEM = pltpu.SMEM
 CORES = 2
+SPREAD_OUT = 4 * 10**9
 
 
 def positions():
@@ -168,12 +169,8 @@
 
 
 def sum_parts(*refs):
-    terms, out = refs[:-2], refs[-1]
+    terms, out = refs[:-1], refs[-1]
     out[...] = tree([t[...].astype(jnp.float32) for t in terms]).astype(jnp.bfloat16)
-
-
-def mark(after, token):
-    token[...] = jnp.zeros_like(token)
 
 
 def finish_features(kept, received, scale, weight, out, token):
@@ -188,24 +185,24 @@
 
 
 def finish_weight(factor, *refs):
-    terms, low, high = refs[:-3], refs[-2], refs[-1]
-    total = tree([t[...].astype(jnp.float32) for t in terms]) * factor
-    part = low.shape[0]
-    low[...] = total[:part]
-    high[...] = total[part:]
-
-
-def place_half(whose, low, high, *refs):
+    terms, out = refs[:-1], refs[-1]
+    out[...] = tree([t[...].astype(jnp.float32) for t in terms]) * factor
+
+
+def join(after, *refs):
     out, sems = refs[-2:]
-    part = low.shape[0]
+    parts = refs[:-2]
+    rows = parts[0].shape[0]
+    half = len(parts) // 2
     core = positions()[1]
-    at = (1 - core if whose else core) * 2 * part
-    copies = [
-        pltpu.make_async_copy(
-            src, out.at[pl.ds(pl.multiple_of(at + n * part, part), part)], sems.at[n]
+    copies = []
+    for n, part in enumerate(parts):
+        at = (core if n < half else 1 - core) * half * rows + n % half * rows
+        copies.append(
+            pltpu.make_async_copy(
+                part, out.at[pl.ds(pl.multiple_of(at, rows), rows)], sems.at[n]
+            )
         )
-        for n, src in enumerate((low, high))
-    ]
     for c in copies:
         c.start()
     for c in copies:
@@ -289,27 +286,23 @@
             [kept, received],
         )
     received = swap(leaving, CORES * bit + 1)
-    (landed,) = call(mark, [shape((8, 128), f32)], [received])
     grad_features, token = call(
         finish_features,
         [shape((nodes, width), f32), shape((8, 128), f32)],
         [kept, received, scale, weight],
-        flops=4 * nodes * width * width,
-    )
-    (once,) = call(sum_parts, [shape((half, width), bf16)], [stay] + spread(leave) + [landed])
+        flops=SPREAD_OUT,
+    )
+    (once,) = call(sum_parts, [shape((half, width), bf16)], [stay] + spread(leave))
     factor = (nodes * rows * cols) ** (-0.5)
     own = call(
         functools.partial(finish_weight, factor),
-        [shape((half // 2, width), f32)] * 2,
-        [partner(once)] + spread(once) + [token],
+        [shape((half, width), f32)],
+        [partner(once)] + spread(once),
     )
     other = [partner(x) for x in own]
-    full = [shape((width, width), f32)]
-    sems = [pltpu.SemaphoreType.DMA((2,))]
-    held = call(functools.partial(place_half, 0), full, own, scratch=sems, out_space=pl.ANY)
     (weight_grad,) = call(
-        functools.partial(place_half, 1), full, other + list(held), [VMEM, VMEM, pl.ANY],
-        scratch=sems, out_space=pl.ANY, alias={2: 0},
+        join, [shape((width, width), f32)], [token] + list(own) + other,
+        scratch=[pltpu.SemaphoreType.DMA((2 * len(other),))], out_space=pl.ANY,
     )
     return grad_features, weight_grad
 

time: 32.7 us -> 31.6 us (0.966)
  Pallas kernels: 5.12 us -> 4.1 us
  waiting for transfers between devices: 8.42 us -> 7.69 us
  starting transfers between devices: 17.6 us -> 18.2 us
    ppermute x8 -> x7, waiting for transfers between devices: 4.6 us -> 1.63 us  [swap(): return lax.ppermute(x, 'row', [(d, d ^ k) for d in range(rows)])]
    ppermute x9, waiting for transfers between devices: 3.82 us -> 6.06 us  [cross(): return lax.ppermute(x, ('row', 'col'), pairs)]
    pallas_call x12 -> x10, Pallas kernels: 5.12 us -> 4.1 us  [call(): pl.pallas_call(body, out_shape=outs, in_specs=[pl.BlockSpec(memory_space=...]
    ppermute x8 -> x7, starting transfers between devices: 5.84 us -> 6.26 us  [swap(): return lax.ppermute(x, 'row', [(d, d ^ k) for d in range(rows)])]
  transfers between devices with their start and end apart: 17 -> 16, of which waited for: 10 -> 9; matrix products, arithmetic and copies ran while one was open for 0% -> 0% of each run, Pallas kernels for 8% -> 5%
where the time goes in v5:
time: 31.6 us; the launch traced here: 31.4 us
  starting transfers between devices  18.2 us (58%)
  waiting for transfers between devices  7.69 us (24%)
  Pallas kernels  4.1 us (13%)
  between operations  1.37 us (4%)
    ppermute x9, starting transfers between devices, cross(): return lax.ppermute(x, ('row', 'col'), pairs)  12 us
    ppermute x7, starting transfers between devices, swap(): return lax.ppermute(x, 'row', [(d, d ^ k) for d in range(rows)])  6.26 us
    ppermute x9, waiting for transfers between devices, cross(): return lax.ppermute(x, ('row', 'col'), pairs)  6.06 us
    pallas_call x10, Pallas kernels, call(): pl.pallas_call(body, out_shape=outs, in_specs=[pl.BlockSpec(memory_space=...  4.1 us
    ppermute x7, waiting for transfers between devices, swap(): return lax.ppermute(x, 'row', [(d, d ^ k) for d in range(rows)])  1.63 us
  transfers between devices with their start and end apart: 16, of which 9 were waited for; matrix products, arithmetic and copies ran while one was open for 0% of the time, Pallas kernels for 5%

profile of v5, /device:TPU:0, one launch (start us, length us, event | category | flops | bytes accessed | tf_op | source)
XLA Modules:
  0.0 31.4 jit_solution(289826898527364143)
XLA Ops:
  0.6 0.0 copy-start
  0.6 1.0 %shard_map.95 = (bf16[128,256]{1,0:T(8,128)(2,1)S(1)}, f32[64,1]{1,0:T(8,128)S(1)}) custom-call(bf16[64,256]{1,0:T(8,128)(2,1)} %features.1, bf16[64,256]{1,0:T(8,128)(2,1)} %grad_out.1, s32[64,256]{1,0:T(8,128)} %relu_mask.1, s32[1,64]{1,0:T(1,128)} %bitcast.1), custom_call_target="tpu_custom_call" | custom-call | bytes 197120 | tf_op jit(solution)/shard_map/pallas_call | solution.py:30
  1.7 0.5 %collective-permute-start = (bf16[128,256]{1,0:T(8,128)(2,1)S(1)}, bf16[128,256]{1,0:T(8,128)(2,1)S(1)}, u32[]{:S(2)}, u32[]{:S(2)}) collective-permute-start(bf16[128,256]{1,0:T(8,128)(2,1)S(1)} %get-tuple-element.14.scaled), channel_id=1, source_target_pairs={{0,4},{4,0},{8,12},{12,8},{16,20},{20,16},{24,28},{28,24},{1,5},{5... | collective-permute-start | bytes 196616 | tf_op jit(solution)/shard_map/ppermute | solution.py:223
  2.9 0.3 collective-permute-done.other
  3.1 0.0 copy-start.1
  3.1 4.8 %collective-permute-start.4 = (bf16[128,256]{1,0:T(8,128)(2,1)S(1)}, bf16[128,256]{1,0:T(8,128)(2,1)S(1)}, u32[]{:S(2)}, u32[]{:S(2)}) collective-permute-start(bf16[128,256]{1,0:T(8,128)(2,1)S(1)} %get-tuple-element.15.after.refs_2_), channel_id=1, source_target_pairs={{0,7},{1,6},{2,5},{3,4},{4,24},{5,25},{6,26},{7,27},{8,15},{9,14},... | collective-permute-start | bytes 196616 | tf_op jit(solution)/shard_map/ppermute | solution.py:234
  7.9 1.4 %collective-permute-start.3 = (bf16[128,256]{1,0:T(8,128)(2,1)S(1)}, bf16[128,256]{1,0:T(8,128)(2,1)S(1)}, u32[]{:S(2)}, u32[]{:S(2)}) collective-permute-start(bf16[128,256]{1,0:T(8,128)(2,1)S(1)} %get-tuple-element.15.after.refs_2_), channel_id=1, source_target_pairs={{0,6},{1,7},{2,4},{3,5},{4,8},{5,9},{6,10},{7,11},{8,14},{9,15},{1... | collective-permute-start | bytes 196616 | tf_op jit(solution)/shard_map/ppermute | solution.py:234
  9.3 0.0 collective-permute-start.2
  9.3 0.0 copy-done
  9.3 0.0 copy-done.1
  9.3 0.6 %shard_map.97.refs_3_.refs_0_ = bf16[512,256]{1,0:T(8,128)(2,1)S(1)} custom-call(bf16[1,1,6,128,128]{4,3,2,1,0:T(8,128)(2,1)S(1)} %copy-done, s32[1,1,6]{2,1,0:T(1,128)S(1)} %copy-done.1, s32[1,1]{1,0:T(1,128)S(6)} %copy.10.count, bf16[128,256]{1,0:T(8,128)(2,1)S(1)} %get-tuple-element.15.after.refs_2_), custom_call_target="tpu_custom_call" | custom-call | bytes 524316 | tf_op jit(solution)/shard_map/pallas_call | solution.py:30
  10.0 0.8 %collective-permute-start.1 = (bf16[512,256]{1,0:T(8,128)(2,1)S(1)}, bf16[512,256]{1,0:T(8,128)(2,1)S(1)}, u32[]{:S(2)}, u32[]{:S(2)}) collective-permute-start(bf16[512,256]{1,0:T(8,128)(2,1)S(1)} %shard_map.97.refs_3_.refs_0_), channel_id=1, source_target_pairs={{0,4},{4,0},{8,12},{12,8},{16,20},{20,16},{24,28},{28,24},{1,5},{5... | collective-permute-start | bytes 786440 | tf_op jit(solution)/shard_map/ppermute | solution.py:223
  10.7 0.0 collective-permute-done.4.refs_2_.refs_7_
  10.7 0.9 %collective-permute-done.3.refs_1_.refs_6_ = bf16[128,256]{1,0:T(8,128)(2,1)S(1)} collective-permute-done((bf16[128,256]{1,0:T(8,128)(2,1)S(1)}, bf16[128,256]{1,0:T(8,128)(2,1)S(1)}, u32[]{:S(2)}, u32[]{:S(2)}) %collective-permute-start.3) | collective-permute-done | bytes 65568 | tf_op jit(solution)/shard_map/ppermute | solution.py:234
  11.6 1.4 %collective-permute-done.2.refs_0_.refs_5_ = bf16[128,256]{1,0:T(8,128)(2,1)S(1)} collective-permute-done((bf16[128,256]{1,0:T(8,128)(2,1)S(1)}, bf16[128,256]{1,0:T(8,128)(2,1)S(1)}, u32[]{:S(2)}, u32[]{:S(2)}) %collective-permute-start.2) | collective-permute-done | bytes 65568 | tf_op jit(solution)/shard_map/ppermute | solution.py:234
  13.0 0.3 collective-permute-start.5
  13.3 1.2 %collective-permute-done.5.refs_4_ = bf16[384,256]{1,0:T(8,128)(2,1)S(1)} collective-permute-done((bf16[384,256]{1,0:T(8,128)(2,1)S(1)}, bf16[384,256]{1,0:T(8,128)(2,1)S(1)}, u32[]{:S(2)}, u32[]{:S(2)}) %collective-permute-start.5) | collective-permute-done | bytes 196640 | tf_op jit(solution)/shard_map/ppermute | solution.py:223
  14.5 0.0 collective-permute-done.1.refs_1_
  14.5 0.8 %shard_map.99 = (bf16[128,256]{1,0:T(8,128)(2,1)S(1)}, bf16[128,256]{1,0:T(8,128)(2,1)S(1)}, f32[128,256]{1,0:T(8,128)S(1)}, bf16[128,256]{1,0:T(8,128)(2,1)S(1)}) custom-call(bf16[512,256]{1,0:T(8,128)(2,1)S(1)} %shard_map.97.refs_3_.refs_0_, bf16[512,256]{1,0:T(8,128)(2,1)S(1)} %collective-permute-done.1.refs_1_, ...), custom_call_target="tpu_custom_call" | custom-call | flops 268435456 | bytes 1376256 | tf_op jit(solution)/shard_map/pallas_call | solution.py:30
  15.3 2.6 %collective-permute-start.10 = (bf16[128,256]{1,0:T(8,128)(2,1)S(1)}, bf16[128,256]{1,0:T(8,128)(2,1)S(1)}, u32[]{:S(2)}, u32[]{:S(2)}) collective-permute-start(bf16[128,256]{1,0:T(8,128)(2,1)S(1)} %get-tuple-element.25), channel_id=1, source_target_pairs={{0,7},{1,6},{2,5},{3,4},{4,24},{5,25},{6,26},{7,27},{8,15},{9,14},... | collective-permute-start | bytes 196616 | tf_op jit(solution)/shard_map/ppermute | solution.py:234
  17.8 0.0 collective-permute-start.9
  17.8 0.0 collective-permute-start.8
  17.8 1.7 %collective-permute-start.6 = (bf16[128,256]{1,0:T(8,128)(2,1)S(1)}, bf16[128,256]{1,0:T(8,128)(2,1)S(1)}, u32[]{:S(2)}, u32[]{:S(2)}) collective-permute-start(bf16[128,256]{1,0:T(8,128)(2,1)S(1)} %get-tuple-element.18), channel_id=1, source_target_pairs={{0,12},{4,8},{8,4},{12,0},{16,28},{20,24},{24,20},{28,16},{1,13},{... | collective-permute-start | bytes 196616 | tf_op jit(solution)/shard_map/ppermute | solution.py:223
  19.6 0.3 %collective-permute-done.10.refs_3_ = bf16[128,256]{1,0:T(8,128)(2,1)S(1)} collective-permute-done((bf16[128,256]{1,0:T(8,128)(2,1)S(1)}, bf16[128,256]{1,0:T(8,128)(2,1)S(1)}, u32[]{:S(2)}, u32[]{:S(2)}) %collective-permute-start.10) | collective-permute-done | bytes 65568 | tf_op jit(solution)/shard_map/ppermute | solution.py:234
  19.9 1.6 %collective-permute-done.9.refs_2_ = bf16[128,256]{1,0:T(8,128)(2,1)S(1)} collective-permute-done((bf16[128,256]{1,0:T(8,128)(2,1)S(1)}, bf16[128,256]{1,0:T(8,128)(2,1)S(1)}, u32[]{:S(2)}, u32[]{:S(2)}) %collective-permute-start.9) | collective-permute-done | bytes 65568 | tf_op jit(solution)/shard_map/ppermute | solution.py:234
  21.5 0.0 collective-permute-done.8.refs_1_
  21.6 3.3 %collective-permute-start.14 = (bf16[128,256]{1,0:T(8,128)(2,1)S(1)}, bf16[128,256]{1,0:T(8,128)(2,1)S(1)}, u32[]{:S(2)}, u32[]{:S(2)}) collective-permute-start(bf16[128,256]{1,0:T(8,128)(2,1)S(1)} %shard_map.102), channel_id=1, source_target_pairs={{0,7},{1,6},{2,5},{3,4},{4,24},{5,25},{6,26},{7,27},{8,15},{9,14},... | collective-permute-start | bytes 196616 | tf_op jit(solution)/shard_map/ppermute | solution.py:234
  24.8 0.0 collective-permute-start.13
  24.8 0.0 collective-permute-start.12
  24.8 1.1 %collective-permute-start.11 = (bf16[128,256]{1,0:T(8,128)(2,1)S(1)}, bf16[128,256]{1,0:T(8,128)(2,1)S(1)}, u32[]{:S(2)}, u32[]{:S(2)}) collective-permute-start(bf16[128,256]{1,0:T(8,128)(2,1)S(1)} %shard_map.102), channel_id=1, source_target_pairs={{0,4},{4,0},{8,12},{12,8},{16,20},{20,16},{24,28},{28,24},{1,5},{5... | collective-permute-start | bytes 196616 | tf_op jit(solution)/shard_map/ppermute | solution.py:223
  25.9 0.0 collective-permute-done.6.received
  25.9 0.0 copy-start.2
  25.9 0.8 %collective-permute-start.7 = (bf16[64,256]{1,0:T(8,128)(2,1)S(1)}, bf16[64,256]{1,0:T(8,128)(2,1)S(1)}, u32[]{:S(2)}, u32[]{:S(2)}) collective-permute-start(bf16[64,256]{1,0:T(8,128)(2,1)S(1)} %get-tuple-element.20), channel_id=1, source_target_pairs={{0,20},{4,16},{8,28},{12,24},{16,4},{20,0},{24,12},{28,8},{1,21},{... | collective-permute-start | bytes 98312 | tf_op jit(solution)/shard_map/ppermute | solution.py:223
  26.7 0.1 collective-permute-done.14.refs_3_
  26.7 1.8 %collective-permute-done.13.refs_2_ = bf16[128,256]{1,0:T(8,128)(2,1)S(1)} collective-permute-done((bf16[128,256]{1,0:T(8,128)(2,1)S(1)}, bf16[128,256]{1,0:T(8,128)(2,1)S(1)}, u32[]{:S(2)}, u32[]{:S(2)}) %collective-permute-start.13) | collective-permute-done | bytes 65568 | tf_op jit(solution)/shard_map/ppermute | solution.py:234
  28.5 0.0 collective-permute-done.12.refs_1_
  28.5 0.0 collective-permute-done.11.refs_0_
  28.6 1.1 %collective-permute-start.15 = (f32[128,256]{1,0:T(8,128)S(1)}, f32[128,256]{1,0:T(8,128)S(1)}, u32[]{:S(2)}, u32[]{:S(2)}) collective-permute-start(f32[128,256]{1,0:T(8,128)S(1)} %shard_map.103.refs_0_), channel_id=1, source_target_pairs={{0,4},{4,0},{8,12},{12,8},{16,20},{20,16},{24,28},{28,24},{1,5},{5... | collective-permute-start | bytes 393224 | tf_op jit(solution)/shard_map/ppermute | solution.py:223
  29.7 0.0 collective-permute-done.7.received
  29.7 0.0 copy-done.2
  29.7 0.8 %shard_map.101 = (f32[64,256]{1,0:T(8,128)}, f32[8,128]{1,0:T(8,128)S(1)}) custom-call(f32[64,256]{1,0:T(8,128)S(1)} %get-tuple-element.19.kept, bf16[64,256]{1,0:T(8,128)(2,1)S(1)} %collective-permute-done.7.received, f32[64,1]{1,0:T(8,128)S(1)} %get-tuple-element.21.scale, bf16[256,256]{1,0:T(8,128)(2,1)S(1)} %copy-done.2), custom_call_target="tpu_custom_call" | custom-call | flops 4000000000 | bytes 299264 | tf_op jit(solution)/shard_map/pallas_call | solution.py:30
  30.6 0.1 collective-permute-done.15.refs_1_
  30.7 0.7 %shard_map.104 = f32[256,256]{1,0:T(8,128)} custom-call(f32[8,128]{1,0:T(8,128)S(1)} %get-tuple-element.23.after, f32[128,256]{1,0:T(8,128)S(1)} %shard_map.103.refs_0_, f32[128,256]{1,0:T(8,128)S(1)} %collective-permute-done.15.refs_1_), custom_call_target="tpu_custom_call" | custom-call | bytes 528384 | tf_op jit(solution)/shard_map/pallas_call | solution.py:30
  (5 shorter events, 0.1 us)
Async XLA Ops:
  0.6 8.7 %copy-start = (bf16[1,1,6,128,128]{4,3,2,1,0:T(8,128)(2,1)S(1)}, bf16[1,1,6,128,128]{4,3,2,1,0:T(8,128)(2,1)}, u32[]{:S(2)}) copy-start(bf16[1,1,6,128,128]{4,3,2,1,0:T(8,128)(2,1)} %blocks.1) | copy-start | bytes 589828
  1.7 1.4 %collective-permute-start = (bf16[128,256]{1,0:T(8,128)(2,1)S(1)}, bf16[128,256]{1,0:T(8,128)(2,1)S(1)}, u32[]{:S(2)}, u32[]{:S(2)}) collective-permute-start(bf16[128,256]{1,0:T(8,128)(2,1)S(1)} %get-tuple-element.14.scaled), channel_id=1, source_target_pairs={{0,4},{4,0},{8,12},{12,8},{16,20},{20,16},{24,28},{28,24},{1,5},{5... | collective-permute-start | bytes 196616 | tf_op jit(solution)/shard_map/ppermute | solution.py:223
  3.1 6.2 %copy-start.1 = (s32[1,1,6]{2,1,0:T(1,128)S(1)}, s32[1,1,6]{2,1,0:T(1,128)}, u32[]{:S(2)}) copy-start(s32[1,1,6]{2,1,0:T(1,128)} %slots.1) | copy-start | bytes 76
  3.1 7.6 %collective-permute-start.4 = (bf16[128,256]{1,0:T(8,128)(2,1)S(1)}, bf16[128,256]{1,0:T(8,128)(2,1)S(1)}, u32[]{:S(2)}, u32[]{:S(2)}) collective-permute-start(bf16[128,256]{1,0:T(8,128)(2,1)S(1)} %get-tuple-element.15.after.refs_2_), channel_id=1, source_target_pairs={{0,7},{1,6},{2,5},{3,4},{4,24},{5,25},{6,26},{7,27},{8,15},{9,14},... | collective-permute-start | bytes 196616 | tf_op jit(solution)/shard_map/ppermute | solution.py:234
  7.9 3.7 %collective-permute-start.3 = (bf16[128,256]{1,0:T(8,128)(2,1)S(1)}, bf16[128,256]{1,0:T(8,128)(2,1)S(1)}, u32[]{:S(2)}, u32[]{:S(2)}) collective-permute-start(bf16[128,256]{1,0:T(8,128)(2,1)S(1)} %get-tuple-element.15.after.refs_2_), channel_id=1, source_target_pairs={{0,6},{1,7},{2,4},{3,5},{4,8},{5,9},{6,10},{7,11},{8,14},{9,15},{1... | collective-permute-start | bytes 196616 | tf_op jit(solution)/shard_map/ppermute | solution.py:234
  9.3 3.7 %collective-permute-start.2 = (bf16[128,256]{1,0:T(8,128)(2,1)S(1)}, bf16[128,256]{1,0:T(8,128)(2,1)S(1)}, u32[]{:S(2)}, u32[]{:S(2)}) collective-permute-start(bf16[128,256]{1,0:T(8,128)(2,1)S(1)} %get-tuple-element.15.after.refs_2_), channel_id=1, source_target_pairs={{0,5},{1,4},{2,7},{3,6},{4,16},{5,17},{6,18},{7,19},{8,13},{9,12},... | collective-permute-start | bytes 196616 | tf_op jit(solution)/shard_map/ppermute | solution.py:234
  10.0 4.6 %collective-permute-start.1 = (bf16[512,256]{1,0:T(8,128)(2,1)S(1)}, bf16[512,256]{1,0:T(8,128)(2,1)S(1)}, u32[]{:S(2)}, u32[]{:S(2)}) collective-permute-start(bf16[512,256]{1,0:T(8,128)(2,1)S(1)} %shard_map.97.refs_3_.refs_0_), channel_id=1, source_target_pairs={{0,4},{4,0},{8,12},{12,8},{16,20},{20,16},{24,28},{28,24},{1,5},{5... | collective-permute-start | bytes 786440 | tf_op jit(solution)/shard_map/ppermute | solution.py:223
  13.0 1.5 %collective-permute-start.5 = (bf16[384,256]{1,0:T(8,128)(2,1)S(1)}, bf16[384,256]{1,0:T(8,128)(2,1)S(1)}, u32[]{:S(2)}, u32[]{:S(2)}) collective-permute-start(bf16[384,256]{1,0:T(8,128)(2,1)S(1)} %shard_map.98), channel_id=1, source_target_pairs={{0,4},{4,0},{8,12},{12,8},{16,20},{20,16},{24,28},{28,24},{1,5},{5... | collective-permute-start | bytes 589832 | tf_op jit(solution)/shard_map/ppermute | solution.py:223
  15.3 4.6 %collective-permute-start.10 = (bf16[128,256]{1,0:T(8,128)(2,1)S(1)}, bf16[128,256]{1,0:T(8,128)(2,1)S(1)}, u32[]{:S(2)}, u32[]{:S(2)}) collective-permute-start(bf16[128,256]{1,0:T(8,128)(2,1)S(1)} %get-tuple-element.25), channel_id=1, source_target_pairs={{0,7},{1,6},{2,5},{3,4},{4,24},{5,25},{6,26},{7,27},{8,15},{9,14},... | collective-permute-start | bytes 196616 | tf_op jit(solution)/shard_map/ppermute | solution.py:234
  17.8 3.7 %collective-permute-start.9 = (bf16[128,256]{1,0:T(8,128)(2,1)S(1)}, bf16[128,256]{1,0:T(8,128)(2,1)S(1)}, u32[]{:S(2)}, u32[]{:S(2)}) collective-permute-start(bf16[128,256]{1,0:T(8,128)(2,1)S(1)} %get-tuple-element.25), channel_id=1, source_target_pairs={{0,6},{1,7},{2,4},{3,5},{4,8},{5,9},{6,10},{7,11},{8,14},{9,15},{1... | collective-permute-start | bytes 196616 | tf_op jit(solution)/shard_map/ppermute | solution.py:234
  17.8 3.7 %collective-permute-start.8 = (bf16[128,256]{1,0:T(8,128)(2,1)S(1)}, bf16[128,256]{1,0:T(8,128)(2,1)S(1)}, u32[]{:S(2)}, u32[]{:S(2)}) collective-permute-start(bf16[128,256]{1,0:T(8,128)(2,1)S(1)} %get-tuple-element.25), channel_id=1, source_target_pairs={{0,5},{1,4},{2,7},{3,6},{4,16},{5,17},{6,18},{7,19},{8,13},{9,12},... | collective-permute-start | bytes 196616 | tf_op jit(solution)/shard_map/ppermute | solution.py:234
  17.8 8.0 %collective-permute-start.6 = (bf16[128,256]{1,0:T(8,128)(2,1)S(1)}, bf16[128,256]{1,0:T(8,128)(2,1)S(1)}, u32[]{:S(2)}, u32[]{:S(2)}) collective-permute-start(bf16[128,256]{1,0:T(8,128)(2,1)S(1)} %get-tuple-element.18), channel_id=1, source_target_pairs={{0,12},{4,8},{8,4},{12,0},{16,28},{20,24},{24,20},{28,16},{1,13},{... | collective-permute-start | bytes 196616 | tf_op jit(solution)/shard_map/ppermute | solution.py:223
  21.6 5.2 %collective-permute-start.14 = (bf16[128,256]{1,0:T(8,128)(2,1)S(1)}, bf16[128,256]{1,0:T(8,128)(2,1)S(1)}, u32[]{:S(2)}, u32[]{:S(2)}) collective-permute-start(bf16[128,256]{1,0:T(8,128)(2,1)S(1)} %shard_map.102), channel_id=1, source_target_pairs={{0,7},{1,6},{2,5},{3,4},{4,24},{5,25},{6,26},{7,27},{8,15},{9,14},... | collective-permute-start | bytes 196616 | tf_op jit(solution)/shard_map/ppermute | solution.py:234
  24.8 3.7 %collective-permute-start.13 = (bf16[128,256]{1,0:T(8,128)(2,1)S(1)}, bf16[128,256]{1,0:T(8,128)(2,1)S(1)}, u32[]{:S(2)}, u32[]{:S(2)}) collective-permute-start(bf16[128,256]{1,0:T(8,128)(2,1)S(1)} %shard_map.102), channel_id=1, source_target_pairs={{0,6},{1,7},{2,4},{3,5},{4,8},{5,9},{6,10},{7,11},{8,14},{9,15},{1... | collective-permute-start | bytes 196616 | tf_op jit(solution)/shard_map/ppermute | solution.py:234
  24.8 3.7 %collective-permute-start.12 = (bf16[128,256]{1,0:T(8,128)(2,1)S(1)}, bf16[128,256]{1,0:T(8,128)(2,1)S(1)}, u32[]{:S(2)}, u32[]{:S(2)}) collective-permute-start(bf16[128,256]{1,0:T(8,128)(2,1)S(1)} %shard_map.102), channel_id=1, source_target_pairs={{0,5},{1,4},{2,7},{3,6},{4,16},{5,17},{6,18},{7,19},{8,13},{9,12},... | collective-permute-start | bytes 196616 | tf_op jit(solution)/shard_map/ppermute | solution.py:234
  24.8 3.7 %collective-permute-start.11 = (bf16[128,256]{1,0:T(8,128)(2,1)S(1)}, bf16[128,256]{1,0:T(8,128)(2,1)S(1)}, u32[]{:S(2)}, u32[]{:S(2)}) collective-permute-start(bf16[128,256]{1,0:T(8,128)(2,1)S(1)} %shard_map.102), channel_id=1, source_target_pairs={{0,4},{4,0},{8,12},{12,8},{16,20},{20,16},{24,28},{28,24},{1,5},{5... | collective-permute-start | bytes 196616 | tf_op jit(solution)/shard_map/ppermute | solution.py:223
  25.9 3.8 %copy-start.2 = (bf16[256,256]{1,0:T(8,128)(2,1)S(1)}, bf16[256,256]{1,0:T(8,128)(2,1)}, u32[]{:S(2)}) copy-start(bf16[256,256]{1,0:T(8,128)(2,1)} %weight.1) | copy-start | bytes 393220
  25.9 3.8 %collective-permute-start.7 = (bf16[64,256]{1,0:T(8,128)(2,1)S(1)}, bf16[64,256]{1,0:T(8,128)(2,1)S(1)}, u32[]{:S(2)}, u32[]{:S(2)}) collective-permute-start(bf16[64,256]{1,0:T(8,128)(2,1)S(1)} %get-tuple-element.20), channel_id=1, source_target_pairs={{0,20},{4,16},{8,28},{12,24},{16,4},{20,0},{24,12},{28,8},{1,21},{... | collective-permute-start | bytes 98312 | tf_op jit(solution)/shard_map/ppermute | solution.py:223
  28.6 2.1 %collective-permute-start.15 = (f32[128,256]{1,0:T(8,128)S(1)}, f32[128,256]{1,0:T(8,128)S(1)}, u32[]{:S(2)}, u32[]{:S(2)}) collective-permute-start(f32[128,256]{1,0:T(8,128)S(1)} %shard_map.103.refs_0_), channel_id=1, source_target_pairs={{0,4},{4,0},{8,12},{12,8},{16,20},{20,16},{24,28},{28,24},{1,5},{5... | collective-permute-start | bytes 393224 | tf_op jit(solution)/shard_map/ppermute | solution.py:223

commit v6 on v5

--- a/solution.py
+++ b/solution.py
@@ -10,7 +10,7 @@
 VMEM = pltpu.VMEM
 SMEM = pltpu.SMEM
 CORES = 2
-SPREAD_OUT = 4 * 10**9
+HEAVY = 4 * 10**9
 
 
 def positions():
@@ -22,9 +22,7 @@
     return k & ~3 | (k & 1) << 1 | (k >> 1) & 1
 
 
-def call(
-    body, outs, ins, spaces=None, limit=8 * 2**20, flops=0, scratch=(), out_space=VMEM, alias=None
-):
+def call(body, outs, ins, spaces=None, limit=8 * 2**20, flops=0, scratch=(), out_space=VMEM):
     spaces = spaces or [VMEM] * len(ins)
     moved = sum(x.size * x.dtype.itemsize for x in list(ins) + list(outs))
     return pl.pallas_call(
@@ -32,7 +30,6 @@
         out_shape=outs,
         in_specs=[pl.BlockSpec(memory_space=s) for s in spaces],
         out_specs=[pl.BlockSpec(memory_space=out_space) for _ in outs],
-        input_output_aliases=alias or {},
         scratch_shapes=list(scratch),
         compiler_params=pltpu.CompilerParams(vmem_limit_bytes=limit),
         cost_estimate=pl.CostEstimate(flops=flops, bytes_accessed=moved, transcendentals=0),
@@ -67,7 +64,7 @@
     scale_out[...] = scale
 
 
-def pair_up(scaled, other, pair, pair_left):
+def pair_up(scaled, other, count, pair, pair_left):
     nodes = scaled.shape[0] // 2
     core = positions()[1]
     mine = pl.ds(pl.multiple_of(core * nodes, nodes), nodes)
@@ -100,11 +97,11 @@
 
 
 def multiply(nodes, chips, cols, refs):
-    own, other, pair, pair_left, brought = refs[:5]
+    own, other, pair, pair_left, near, far = refs[:6]
     rows = CORES * nodes
-    first = [pair_left] + list(refs[5 : 4 + cols])
-    second = [pair] + [brought.at[n * rows : (n + 1) * rows] for n in range(cols - 1)]
-    leave, stay, chunks, chunk_sends = refs[4 + cols :]
+    first = [pair_left] + list(refs[6 : 5 + cols])
+    second = [pair, near] + [far.at[n * rows : (n + 1) * rows] for n in range(cols - 2)]
+    leave, chunks, chunk_sends = refs[5 + cols :]
     core = positions()[1]
     width = leave.shape[1]
     half = leave.shape[0]
@@ -119,6 +116,7 @@
     total = jnp.dot(own[...], mine, preferred_element_type=jnp.float32) + jnp.dot(
         other[...], theirs, preferred_element_type=jnp.float32
     )
+    feats = [jnp.where(core == 0, x[:, :half], x[:, half:]) for x in feats]
     features = jnp.concatenate([feats[turned(k)] for k in range(chips)], axis=0)
     high = total.astype(jnp.bfloat16)
     low = (total - high.astype(jnp.float32)).astype(jnp.bfloat16)
@@ -126,8 +124,7 @@
     part = lax.dot_general(features, high, first_rows, preferred_element_type=jnp.float32)
     part = part + lax.dot_general(features, low, first_rows, preferred_element_type=jnp.float32)
     part = part.astype(jnp.bfloat16)
-    leave[...] = jnp.where(core == 0, part[:half], part[half:])
-    stay[...] = jnp.where(core == 0, part[half:], part[:half])
+    leave[...] = part
 
     def chunk(x, k, other):
         at = k * CORES * nodes
@@ -189,20 +186,15 @@
     out[...] = tree([t[...].astype(jnp.float32) for t in terms]) * factor
 
 
-def join(after, *refs):
-    out, sems = refs[-2:]
-    parts = refs[:-2]
-    rows = parts[0].shape[0]
-    half = len(parts) // 2
+def join(after, own, other, out, sems):
+    rows = own.shape[0]
     core = positions()[1]
-    copies = []
-    for n, part in enumerate(parts):
-        at = (core if n < half else 1 - core) * half * rows + n % half * rows
-        copies.append(
-            pltpu.make_async_copy(
-                part, out.at[pl.ds(pl.multiple_of(at, rows), rows)], sems.at[n]
-            )
+    copies = [
+        pltpu.make_async_copy(
+            part, out.at[pl.ds(pl.multiple_of(at * rows, rows), rows)], sems.at[n]
         )
+        for n, (at, part) in enumerate(((core, own), (1 - core, other)))
+    ]
     for c in copies:
         c.start()
     for c in copies:
@@ -251,7 +243,8 @@
         ],
     )
     pair, pair_left = call(
-        pair_up, [shape((CORES * nodes, width), bf16)] * 2, [scaled, partner(scaled)]
+        pair_up, [shape((CORES * nodes, width), bf16)] * 2,
+        [scaled, partner(scaled), block_count], [VMEM, VMEM, SMEM],
     )
     moved = spread(pair)
     targets, sources = rows * nodes, cols * nodes
@@ -263,15 +256,17 @@
         [VMEM, SMEM, SMEM, VMEM],
         limit=8 * 2**20 + 3 * size,
     )
-    (packed,) = call(pack, [shape(((cols - 1) * CORES * nodes, width), bf16)], moved + [dense])
-    brought = partner(packed)
-    leave, stay, kept, leaving = call(
+    (packed,) = call(
+        pack, [shape(((cols - 2) * CORES * nodes, width), bf16)], moved[1:] + [dense], flops=HEAVY
+    )
+    brought = [partner(moved[0]), partner(packed)]
+    leave, kept, leaving = call(
         lambda *refs: multiply(nodes, chips, cols, refs),
         [
-            shape((half, width), bf16), shape((half, width), bf16),
+            shape((half, width), bf16),
             shape((chips // 2 * nodes, width), f32), shape((chips // 2 * nodes, width), bf16),
         ],
-        [dense, partner(dense), pair, pair_left, brought] + moved,
+        [dense, partner(dense), pair, pair_left] + brought + moved,
         limit=8 * 2**20 + 4 * size,
         flops=4 * targets * sources * width + 4 * targets * width * width,
     )
@@ -290,19 +285,18 @@
         finish_features,
         [shape((nodes, width), f32), shape((8, 128), f32)],
         [kept, received, scale, weight],
-        flops=SPREAD_OUT,
-    )
-    (once,) = call(sum_parts, [shape((half, width), bf16)], [stay] + spread(leave))
+        flops=HEAVY,
+    )
+    (once,) = call(sum_parts, [shape((half, width), bf16)], [partner(leave)] + spread(leave))
     factor = (nodes * rows * cols) ** (-0.5)
-    own = call(
+    (own_half,) = call(
         functools.partial(finish_weight, factor),
         [shape((half, width), f32)],
         [partner(once)] + spread(once),
     )
-    other = [partner(x) for x in own]
     (weight_grad,) = call(
-        join, [shape((width, width), f32)], [token] + list(own) + other,
-        scratch=[pltpu.SemaphoreType.DMA((2 * len(other),))], out_space=pl.ANY,
+        join, [shape((width, width), f32)], [token, own_half, partner(own_half)],
+        scratch=[pltpu.SemaphoreType.DMA((2,))], out_space=pl.ANY,
     )
     return grad_features, weight_grad
 

time: 31.6 us -> 31.3 us (level)
    ppermute x7 -> x9, starting transfers between devices: 6.26 us -> 5.9 us  [swap(): return lax.ppermute(x, 'row', [(d, d ^ k) for d in range(rows)])]
    ppermute x7 -> x9, waiting for transfers between devices: 1.63 us -> 1.44 us  [swap(): return lax.ppermute(x, 'row', [(d, d ^ k) for d in range(rows)])]
  transfers between devices with their start and end apart: 16 -> 18, of which waited for: 9 -> 10; matrix products, arithmetic and copies ran while one was open for 0% -> 0% of each run, Pallas kernels for 5% -> 5%
where the time goes in v6:
time: 31.3 us; the launch traced here: 31.1 us
  starting transfers between devices  18.1 us (58%)
  waiting for transfers between devices  7.59 us (24%)
  Pallas kernels  4.03 us (13%)
  between operations  1.37 us (4%)
    ppermute x9, starting transfers between devices, cross(): return lax.ppermute(x, ('row', 'col'), pairs)  12.2 us
    ppermute x9, waiting for transfers between devices, cross(): return lax.ppermute(x, ('row', 'col'), pairs)  6.15 us
    ppermute x9, starting transfers between devices, swap(): return lax.ppermute(x, 'row', [(d, d ^ k) for d in range(rows)])  5.9 us
    pallas_call x10, Pallas kernels, call(): pl.pallas_call(body, out_shape=outs, in_specs=[pl.BlockSpec(memory_space=...  4.03 us
    ppermute x9, waiting for transfers between devices, swap(): return lax.ppermute(x, 'row', [(d, d ^ k) for d in range(rows)])  1.44 us
  transfers between devices with their start and end apart: 18, of which 10 were waited for; matrix products, arithmetic and copies ran while one was open for 0% of the time, Pallas kernels for 5%

profile of v6, /device:TPU:0, one launch (start us, length us, event | category | flops | bytes accessed | tf_op | source)
XLA Modules:
  0.0 31.1 jit_solution(2414399621216845476)
XLA Ops:
  0.6 0.0 copy-start
  0.6 1.0 %shard_map.95 = (bf16[128,256]{1,0:T(8,128)(2,1)S(1)}, f32[64,1]{1,0:T(8,128)S(1)}) custom-call(bf16[64,256]{1,0:T(8,128)(2,1)} %features.1, bf16[64,256]{1,0:T(8,128)(2,1)} %grad_out.1, s32[64,256]{1,0:T(8,128)} %relu_mask.1, s32[1,64]{1,0:T(1,128)} %bitcast.1), custom_call_target="tpu_custom_call" | custom-call | bytes 197120 | tf_op jit(solution)/shard_map/pallas_call | solution.py:28
  1.7 0.5 %collective-permute-start = (bf16[128,256]{1,0:T(8,128)(2,1)S(1)}, bf16[128,256]{1,0:T(8,128)(2,1)S(1)}, u32[]{:S(2)}, u32[]{:S(2)}) collective-permute-start(bf16[128,256]{1,0:T(8,128)(2,1)S(1)} %get-tuple-element.13.scaled), channel_id=1, source_target_pairs={{0,4},{4,0},{8,12},{12,8},{16,20},{20,16},{24,28},{28,24},{1,5},{5... | collective-permute-start | bytes 196616 | tf_op jit(solution)/shard_map/ppermute | solution.py:215
  2.9 0.3 collective-permute-done.other
  3.1 0.0 copy-start.1
  3.1 4.8 %collective-permute-start.5 = (bf16[128,256]{1,0:T(8,128)(2,1)S(1)}, bf16[128,256]{1,0:T(8,128)(2,1)S(1)}, u32[]{:S(2)}, u32[]{:S(2)}) collective-permute-start(bf16[128,256]{1,0:T(8,128)(2,1)S(1)} %get-tuple-element.14.after.refs_2_), channel_id=1, source_target_pairs={{0,7},{1,6},{2,5},{3,4},{4,24},{5,25},{6,26},{7,27},{8,15},{9,14},... | collective-permute-start | bytes 196616 | tf_op jit(solution)/shard_map/ppermute | solution.py:226
  7.9 1.4 %collective-permute-start.4 = (bf16[128,256]{1,0:T(8,128)(2,1)S(1)}, bf16[128,256]{1,0:T(8,128)(2,1)S(1)}, u32[]{:S(2)}, u32[]{:S(2)}) collective-permute-start(bf16[128,256]{1,0:T(8,128)(2,1)S(1)} %get-tuple-element.14.after.refs_2_), channel_id=1, source_target_pairs={{0,6},{1,7},{2,4},{3,5},{4,8},{5,9},{6,10},{7,11},{8,14},{9,15},{1... | collective-permute-start | bytes 196616 | tf_op jit(solution)/shard_map/ppermute | solution.py:226
  9.3 0.0 collective-permute-start.2
  9.3 0.0 copy-done
  9.3 0.0 copy-done.1
  9.3 0.7 %shard_map.97.refs_2_.refs_0_ = bf16[512,256]{1,0:T(8,128)(2,1)S(1)} custom-call(bf16[1,1,6,128,128]{4,3,2,1,0:T(8,128)(2,1)S(1)} %copy-done, s32[1,1,6]{2,1,0:T(1,128)S(1)} %copy-done.1, s32[1,1]{1,0:T(1,128)S(6)} %copy.10.count, bf16[128,256]{1,0:T(8,128)(2,1)S(1)} %get-tuple-element.14.after.refs_2_), custom_call_target="tpu_custom_call" | custom-call | bytes 524316 | tf_op jit(solution)/shard_map/pallas_call | solution.py:28
  10.0 0.6 %collective-permute-start.1 = (bf16[512,256]{1,0:T(8,128)(2,1)S(1)}, bf16[512,256]{1,0:T(8,128)(2,1)S(1)}, u32[]{:S(2)}, u32[]{:S(2)}) collective-permute-start(bf16[512,256]{1,0:T(8,128)(2,1)S(1)} %shard_map.97.refs_2_.refs_0_), channel_id=1, source_target_pairs={{0,4},{4,0},{8,12},{12,8},{16,20},{20,16},{24,28},{28,24},{1,5},{5... | collective-permute-start | bytes 786440 | tf_op jit(solution)/shard_map/ppermute | solution.py:215
  10.6 0.0 collective-permute-done.5.refs_1_.refs_8_
  10.6 1.0 %collective-permute-done.4.refs_0_.refs_7_ = bf16[128,256]{1,0:T(8,128)(2,1)S(1)} collective-permute-done((bf16[128,256]{1,0:T(8,128)(2,1)S(1)}, bf16[128,256]{1,0:T(8,128)(2,1)S(1)}, u32[]{:S(2)}, u32[]{:S(2)}) %collective-permute-start.4) | collective-permute-done | bytes 65568 | tf_op jit(solution)/shard_map/ppermute | solution.py:226
  11.6 0.2 collective-permute-start.6
  11.8 1.2 %collective-permute-done.2.refs_6_ = bf16[128,256]{1,0:T(8,128)(2,1)S(1)} collective-permute-done((bf16[128,256]{1,0:T(8,128)(2,1)S(1)}, bf16[128,256]{1,0:T(8,128)(2,1)S(1)}, u32[]{:S(2)}, u32[]{:S(2)}) %collective-permute-start.2) | collective-permute-done | bytes 65568 | tf_op jit(solution)/shard_map/ppermute | solution.py:226
  13.0 0.2 collective-permute-start.3
  13.2 1.0 %collective-permute-done.3.refs_4_ = bf16[128,256]{1,0:T(8,128)(2,1)S(1)} collective-permute-done((bf16[128,256]{1,0:T(8,128)(2,1)S(1)}, bf16[128,256]{1,0:T(8,128)(2,1)S(1)}, u32[]{:S(2)}, u32[]{:S(2)}) %collective-permute-start.3) | collective-permute-done | bytes 65568 | tf_op jit(solution)/shard_map/ppermute | solution.py:215
  14.2 0.0 collective-permute-done.6.refs_5_
  14.2 0.0 collective-permute-done.1.refs_1_
  14.2 0.6 %shard_map.99 = (bf16[128,256]{1,0:T(8,128)(2,1)S(1)}, f32[128,256]{1,0:T(8,128)S(1)}, bf16[128,256]{1,0:T(8,128)(2,1)S(1)}) custom-call(bf16[512,256]{1,0:T(8,128)(2,1)S(1)} %shard_map.97.refs_2_.refs_0_, bf16[512,256]{1,0:T(8,128)(2,1)S(1)} %collective-permute-done.1.refs_1_, bf16[128,256]{1,0:T(8,128)(2,1)S(1)} %get-tuple-element.14.after.refs_2_, ...), custom_call_target="tpu_custom_call" | custom-call | flops 268435456 | bytes 1310720 | tf_op jit(solution)/shard_map/pallas_call | solution.py:28
  14.9 2.8 %collective-permute-start.12 = (bf16[128,256]{1,0:T(8,128)(2,1)S(1)}, bf16[128,256]{1,0:T(8,128)(2,1)S(1)}, u32[]{:S(2)}, u32[]{:S(2)}) collective-permute-start(bf16[128,256]{1,0:T(8,128)(2,1)S(1)} %get-tuple-element.23), channel_id=1, source_target_pairs={{0,7},{1,6},{2,5},{3,4},{4,24},{5,25},{6,26},{7,27},{8,15},{9,14},... | collective-permute-start | bytes 196616 | tf_op jit(solution)/shard_map/ppermute | solution.py:226
  17.7 0.2 collective-permute-start.11
  17.9 0.0 collective-permute-start.10
  17.9 0.7 %collective-permute-start.9 = (bf16[128,256]{1,0:T(8,128)(2,1)S(1)}, bf16[128,256]{1,0:T(8,128)(2,1)S(1)}, u32[]{:S(2)}, u32[]{:S(2)}) collective-permute-start(bf16[128,256]{1,0:T(8,128)(2,1)S(1)} %get-tuple-element.23), channel_id=1, source_target_pairs={{0,4},{4,0},{8,12},{12,8},{16,20},{20,16},{24,28},{28,24},{1,5},{5... | collective-permute-start | bytes 196616 | tf_op jit(solution)/shard_map/ppermute | solution.py:215
  18.6 0.8 %collective-permute-start.7 = (bf16[128,256]{1,0:T(8,128)(2,1)S(1)}, bf16[128,256]{1,0:T(8,128)(2,1)S(1)}, u32[]{:S(2)}, u32[]{:S(2)}) collective-permute-start(bf16[128,256]{1,0:T(8,128)(2,1)S(1)} %get-tuple-element.17), channel_id=1, source_target_pairs={{0,12},{4,8},{8,4},{12,0},{16,28},{20,24},{24,20},{28,16},{1,13},{... | collective-permute-start | bytes 196616 | tf_op jit(solution)/shard_map/ppermute | solution.py:215
  19.4 0.2 collective-permute-done.12.refs_3_
  19.6 1.8 %collective-permute-done.11.refs_2_ = bf16[128,256]{1,0:T(8,128)(2,1)S(1)} collective-permute-done((bf16[128,256]{1,0:T(8,128)(2,1)S(1)}, bf16[128,256]{1,0:T(8,128)(2,1)S(1)}, u32[]{:S(2)}, u32[]{:S(2)}) %collective-permute-start.11) | collective-permute-done | bytes 65568 | tf_op jit(solution)/shard_map/ppermute | solution.py:226
  21.4 0.2 collective-permute-done.10.refs_1_
  21.6 0.0 collective-permute-done.9.refs_0_
  21.6 3.1 %collective-permute-start.16 = (bf16[128,256]{1,0:T(8,128)(2,1)S(1)}, bf16[128,256]{1,0:T(8,128)(2,1)S(1)}, u32[]{:S(2)}, u32[]{:S(2)}) collective-permute-start(bf16[128,256]{1,0:T(8,128)(2,1)S(1)} %shard_map.102), channel_id=1, source_target_pairs={{0,7},{1,6},{2,5},{3,4},{4,24},{5,25},{6,26},{7,27},{8,15},{9,14},... | collective-permute-start | bytes 196616 | tf_op jit(solution)/shard_map/ppermute | solution.py:226
  24.7 0.0 collective-permute-start.15
  24.7 0.0 collective-permute-start.14
  24.7 0.9 %collective-permute-start.13 = (bf16[128,256]{1,0:T(8,128)(2,1)S(1)}, bf16[128,256]{1,0:T(8,128)(2,1)S(1)}, u32[]{:S(2)}, u32[]{:S(2)}) collective-permute-start(bf16[128,256]{1,0:T(8,128)(2,1)S(1)} %shard_map.102), channel_id=1, source_target_pairs={{0,4},{4,0},{8,12},{12,8},{16,20},{20,16},{24,28},{28,24},{1,5},{5... | collective-permute-start | bytes 196616 | tf_op jit(solution)/shard_map/ppermute | solution.py:215
  25.6 0.0 collective-permute-done.7.received
  25.6 0.0 copy-start.2
  25.7 0.9 %collective-permute-start.8 = (bf16[64,256]{1,0:T(8,128)(2,1)S(1)}, bf16[64,256]{1,0:T(8,128)(2,1)S(1)}, u32[]{:S(2)}, u32[]{:S(2)}) collective-permute-start(bf16[64,256]{1,0:T(8,128)(2,1)S(1)} %get-tuple-element.19), channel_id=1, source_target_pairs={{0,20},{4,16},{8,28},{12,24},{16,4},{20,0},{24,12},{28,8},{1,21},{... | collective-permute-start | bytes 98312 | tf_op jit(solution)/shard_map/ppermute | solution.py:215
  26.5 0.1 collective-permute-done.16.refs_3_
  26.6 1.8 %collective-permute-done.15.refs_2_ = bf16[128,256]{1,0:T(8,128)(2,1)S(1)} collective-permute-done((bf16[128,256]{1,0:T(8,128)(2,1)S(1)}, bf16[128,256]{1,0:T(8,128)(2,1)S(1)}, u32[]{:S(2)}, u32[]{:S(2)}) %collective-permute-start.15) | collective-permute-done | bytes 65568 | tf_op jit(solution)/shard_map/ppermute | solution.py:226
  28.4 0.0 collective-permute-done.14.refs_1_
  28.4 0.0 collective-permute-done.13.refs_0_
  28.4 1.0 %collective-permute-start.17 = (f32[128,256]{1,0:T(8,128)S(1)}, f32[128,256]{1,0:T(8,128)S(1)}, u32[]{:S(2)}, u32[]{:S(2)}) collective-permute-start(f32[128,256]{1,0:T(8,128)S(1)} %shard_map.103.own), channel_id=1, source_target_pairs={{0,4},{4,0},{8,12},{12,8},{16,20},{20,16},{24,28},{28,24},{1,5},{5... | collective-permute-start | bytes 393224 | tf_op jit(solution)/shard_map/ppermute | solution.py:215
  29.4 0.0 collective-permute-done.8.received
  29.4 0.0 copy-done.2
  29.5 0.8 %shard_map.101 = (f32[64,256]{1,0:T(8,128)}, f32[8,128]{1,0:T(8,128)S(1)}) custom-call(f32[64,256]{1,0:T(8,128)S(1)} %get-tuple-element.18.kept, bf16[64,256]{1,0:T(8,128)(2,1)S(1)} %collective-permute-done.8.received, f32[64,1]{1,0:T(8,128)S(1)} %get-tuple-element.20.scale, bf16[256,256]{1,0:T(8,128)(2,1)S(1)} %copy-done.2), custom_call_target="tpu_custom_call" | custom-call | flops 4000000000 | bytes 299264 | tf_op jit(solution)/shard_map/pallas_call | solution.py:28
  30.3 0.1 collective-permute-done.17.other
  30.4 0.7 %shard_map.104 = f32[256,256]{1,0:T(8,128)} custom-call(f32[8,128]{1,0:T(8,128)S(1)} %get-tuple-element.22.after, f32[128,256]{1,0:T(8,128)S(1)} %shard_map.103.own, f32[128,256]{1,0:T(8,128)S(1)} %collective-permute-done.17.other), custom_call_target="tpu_custom_call" | custom-call | bytes 528384 | tf_op jit(solution)/shard_map/pallas_call | solution.py:28
  (5 shorter events, 0.1 us)
Async XLA Ops:
  0.6 8.7 %copy-start = (bf16[1,1,6,128,128]{4,3,2,1,0:T(8,128)(2,1)S(1)}, bf16[1,1,6,128,128]{4,3,2,1,0:T(8,128)(2,1)}, u32[]{:S(2)}) copy-start(bf16[1,1,6,128,128]{4,3,2,1,0:T(8,128)(2,1)} %blocks.1) | copy-start | bytes 589828
  1.7 1.4 %collective-permute-start = (bf16[128,256]{1,0:T(8,128)(2,1)S(1)}, bf16[128,256]{1,0:T(8,128)(2,1)S(1)}, u32[]{:S(2)}, u32[]{:S(2)}) collective-permute-start(bf16[128,256]{1,0:T(8,128)(2,1)S(1)} %get-tuple-element.13.scaled), channel_id=1, source_target_pairs={{0,4},{4,0},{8,12},{12,8},{16,20},{20,16},{24,28},{28,24},{1,5},{5... | collective-permute-start | bytes 196616 | tf_op jit(solution)/shard_map/ppermute | solution.py:215
  3.1 6.2 %copy-start.1 = (s32[1,1,6]{2,1,0:T(1,128)S(1)}, s32[1,1,6]{2,1,0:T(1,128)}, u32[]{:S(2)}) copy-start(s32[1,1,6]{2,1,0:T(1,128)} %slots.1) | copy-start | bytes 76
  3.1 7.5 %collective-permute-start.5 = (bf16[128,256]{1,0:T(8,128)(2,1)S(1)}, bf16[128,256]{1,0:T(8,128)(2,1)S(1)}, u32[]{:S(2)}, u32[]{:S(2)}) collective-permute-start(bf16[128,256]{1,0:T(8,128)(2,1)S(1)} %get-tuple-element.14.after.refs_2_), channel_id=1, source_target_pairs={{0,7},{1,6},{2,5},{3,4},{4,24},{5,25},{6,26},{7,27},{8,15},{9,14},... | collective-permute-start | bytes 196616 | tf_op jit(solution)/shard_map/ppermute | solution.py:226
  7.9 3.7 %collective-permute-start.4 = (bf16[128,256]{1,0:T(8,128)(2,1)S(1)}, bf16[128,256]{1,0:T(8,128)(2,1)S(1)}, u32[]{:S(2)}, u32[]{:S(2)}) collective-permute-start(bf16[128,256]{1,0:T(8,128)(2,1)S(1)} %get-tuple-element.14.after.refs_2_), channel_id=1, source_target_pairs={{0,6},{1,7},{2,4},{3,5},{4,8},{5,9},{6,10},{7,11},{8,14},{9,15},{1... | collective-permute-start | bytes 196616 | tf_op jit(solution)/shard_map/ppermute | solution.py:226
  9.3 3.7 %collective-permute-start.2 = (bf16[128,256]{1,0:T(8,128)(2,1)S(1)}, bf16[128,256]{1,0:T(8,128)(2,1)S(1)}, u32[]{:S(2)}, u32[]{:S(2)}) collective-permute-start(bf16[128,256]{1,0:T(8,128)(2,1)S(1)} %get-tuple-element.14.after.refs_2_), channel_id=1, source_target_pairs={{0,5},{1,4},{2,7},{3,6},{4,16},{5,17},{6,18},{7,19},{8,13},{9,12},... | collective-permute-start | bytes 196616 | tf_op jit(solution)/shard_map/ppermute | solution.py:226
  10.0 4.2 %collective-permute-start.1 = (bf16[512,256]{1,0:T(8,128)(2,1)S(1)}, bf16[512,256]{1,0:T(8,128)(2,1)S(1)}, u32[]{:S(2)}, u32[]{:S(2)}) collective-permute-start(bf16[512,256]{1,0:T(8,128)(2,1)S(1)} %shard_map.97.refs_2_.refs_0_), channel_id=1, source_target_pairs={{0,4},{4,0},{8,12},{12,8},{16,20},{20,16},{24,28},{28,24},{1,5},{5... | collective-permute-start | bytes 786440 | tf_op jit(solution)/shard_map/ppermute | solution.py:215
  11.6 2.6 %collective-permute-start.6 = (bf16[256,256]{1,0:T(8,128)(2,1)S(1)}, bf16[256,256]{1,0:T(8,128)(2,1)S(1)}, u32[]{:S(2)}, u32[]{:S(2)}) collective-permute-start(bf16[256,256]{1,0:T(8,128)(2,1)S(1)} %shard_map.98), channel_id=1, source_target_pairs={{0,4},{4,0},{8,12},{12,8},{16,20},{20,16},{24,28},{28,24},{1,5},{5... | collective-permute-start | bytes 393224 | tf_op jit(solution)/shard_map/ppermute | solution.py:215
  13.0 1.3 %collective-permute-start.3 = (bf16[128,256]{1,0:T(8,128)(2,1)S(1)}, bf16[128,256]{1,0:T(8,128)(2,1)S(1)}, u32[]{:S(2)}, u32[]{:S(2)}) collective-permute-start(bf16[128,256]{1,0:T(8,128)(2,1)S(1)} %collective-permute-done.2.refs_6_), channel_id=1, source_target_pairs={{0,4},{4,0},{8,12},{12,8},{16,20},{20,16},{24,28},{28,24},{1,5},{5... | collective-permute-start | bytes 196616 | tf_op jit(solution)/shard_map/ppermute | solution.py:215
  14.9 4.7 %collective-permute-start.12 = (bf16[128,256]{1,0:T(8,128)(2,1)S(1)}, bf16[128,256]{1,0:T(8,128)(2,1)S(1)}, u32[]{:S(2)}, u32[]{:S(2)}) collective-permute-start(bf16[128,256]{1,0:T(8,128)(2,1)S(1)} %get-tuple-element.23), channel_id=1, source_target_pairs={{0,7},{1,6},{2,5},{3,4},{4,24},{5,25},{6,26},{7,27},{8,15},{9,14},... | collective-permute-start | bytes 196616 | tf_op jit(solution)/shard_map/ppermute | solution.py:226
  17.7 3.7 %collective-permute-start.11 = (bf16[128,256]{1,0:T(8,128)(2,1)S(1)}, bf16[128,256]{1,0:T(8,128)(2,1)S(1)}, u32[]{:S(2)}, u32[]{:S(2)}) collective-permute-start(bf16[128,256]{1,0:T(8,128)(2,1)S(1)} %get-tuple-element.23), channel_id=1, source_target_pairs={{0,6},{1,7},{2,4},{3,5},{4,8},{5,9},{6,10},{7,11},{8,14},{9,15},{1... | collective-permute-start | bytes 196616 | tf_op jit(solution)/shard_map/ppermute | solution.py:226
  17.9 3.7 %collective-permute-start.10 = (bf16[128,256]{1,0:T(8,128)(2,1)S(1)}, bf16[128,256]{1,0:T(8,128)(2,1)S(1)}, u32[]{:S(2)}, u32[]{:S(2)}) collective-permute-start(bf16[128,256]{1,0:T(8,128)(2,1)S(1)} %get-tuple-element.23), channel_id=1, source_target_pairs={{0,5},{1,4},{2,7},{3,6},{4,16},{5,17},{6,18},{7,19},{8,13},{9,12},... | collective-permute-start | bytes 196616 | tf_op jit(solution)/shard_map/ppermute | solution.py:226
  17.9 3.7 %collective-permute-start.9 = (bf16[128,256]{1,0:T(8,128)(2,1)S(1)}, bf16[128,256]{1,0:T(8,128)(2,1)S(1)}, u32[]{:S(2)}, u32[]{:S(2)}) collective-permute-start(bf16[128,256]{1,0:T(8,128)(2,1)S(1)} %get-tuple-element.23), channel_id=1, source_target_pairs={{0,4},{4,0},{8,12},{12,8},{16,20},{20,16},{24,28},{28,24},{1,5},{5... | collective-permute-start | bytes 196616 | tf_op jit(solution)/shard_map/ppermute | solution.py:215
  18.6 7.0 %collective-permute-start.7 = (bf16[128,256]{1,0:T(8,128)(2,1)S(1)}, bf16[128,256]{1,0:T(8,128)(2,1)S(1)}, u32[]{:S(2)}, u32[]{:S(2)}) collective-permute-start(bf16[128,256]{1,0:T(8,128)(2,1)S(1)} %get-tuple-element.17), channel_id=1, source_target_pairs={{0,12},{4,8},{8,4},{12,0},{16,28},{20,24},{24,20},{28,16},{1,13},{... | collective-permute-start | bytes 196616 | tf_op jit(solution)/shard_map/ppermute | solution.py:215
  21.6 5.0 %collective-permute-start.16 = (bf16[128,256]{1,0:T(8,128)(2,1)S(1)}, bf16[128,256]{1,0:T(8,128)(2,1)S(1)}, u32[]{:S(2)}, u32[]{:S(2)}) collective-permute-start(bf16[128,256]{1,0:T(8,128)(2,1)S(1)} %shard_map.102), channel_id=1, source_target_pairs={{0,7},{1,6},{2,5},{3,4},{4,24},{5,25},{6,26},{7,27},{8,15},{9,14},... | collective-permute-start | bytes 196616 | tf_op jit(solution)/shard_map/ppermute | solution.py:226
  24.7 3.7 %collective-permute-start.15 = (bf16[128,256]{1,0:T(8,128)(2,1)S(1)}, bf16[128,256]{1,0:T(8,128)(2,1)S(1)}, u32[]{:S(2)}, u32[]{:S(2)}) collective-permute-start(bf16[128,256]{1,0:T(8,128)(2,1)S(1)} %shard_map.102), channel_id=1, source_target_pairs={{0,6},{1,7},{2,4},{3,5},{4,8},{5,9},{6,10},{7,11},{8,14},{9,15},{1... | collective-permute-start | bytes 196616 | tf_op jit(solution)/shard_map/ppermute | solution.py:226
  24.7 3.7 %collective-permute-start.14 = (bf16[128,256]{1,0:T(8,128)(2,1)S(1)}, bf16[128,256]{1,0:T(8,128)(2,1)S(1)}, u32[]{:S(2)}, u32[]{:S(2)}) collective-permute-start(bf16[128,256]{1,0:T(8,128)(2,1)S(1)} %shard_map.102), channel_id=1, source_target_pairs={{0,5},{1,4},{2,7},{3,6},{4,16},{5,17},{6,18},{7,19},{8,13},{9,12},... | collective-permute-start | bytes 196616 | tf_op jit(solution)/shard_map/ppermute | solution.py:226
  24.7 3.7 %collective-permute-start.13 = (bf16[128,256]{1,0:T(8,128)(2,1)S(1)}, bf16[128,256]{1,0:T(8,128)(2,1)S(1)}, u32[]{:S(2)}, u32[]{:S(2)}) collective-permute-start(bf16[128,256]{1,0:T(8,128)(2,1)S(1)} %shard_map.102), channel_id=1, source_target_pairs={{0,4},{4,0},{8,12},{12,8},{16,20},{20,16},{24,28},{28,24},{1,5},{5... | collective-permute-start | bytes 196616 | tf_op jit(solution)/shard_map/ppermute | solution.py:215
  25.6 3.8 %copy-start.2 = (bf16[256,256]{1,0:T(8,128)(2,1)S(1)}, bf16[256,256]{1,0:T(8,128)(2,1)}, u32[]{:S(2)}) copy-start(bf16[256,256]{1,0:T(8,128)(2,1)} %weight.1) | copy-start | bytes 393220
  25.7 3.8 %collective-permute-start.8 = (bf16[64,256]{1,0:T(8,128)(2,1)S(1)}, bf16[64,256]{1,0:T(8,128)(2,1)S(1)}, u32[]{:S(2)}, u32[]{:S(2)}) collective-permute-start(bf16[64,256]{1,0:T(8,128)(2,1)S(1)} %get-tuple-element.19), channel_id=1, source_target_pairs={{0,20},{4,16},{8,28},{12,24},{16,4},{20,0},{24,12},{28,8},{1,21},{... | collective-permute-start | bytes 98312 | tf_op jit(solution)/shard_map/ppermute | solution.py:215
  28.4 2.0 %collective-permute-start.17 = (f32[128,256]{1,0:T(8,128)S(1)}, f32[128,256]{1,0:T(8,128)S(1)}, u32[]{:S(2)}, u32[]{:S(2)}) collective-permute-start(f32[128,256]{1,0:T(8,128)S(1)} %shard_map.103.own), channel_id=1, source_target_pairs={{0,4},{4,0},{8,12},{12,8},{16,20},{20,16},{24,28},{28,24},{1,5},{5... | collective-permute-start | bytes 393224 | tf_op jit(solution)/shard_map/ppermute | solution.py:215

commit v7 on v6

--- a/solution.py
+++ b/solution.py
@@ -54,12 +54,14 @@
     ]
     for c in copies:
         c.start()
-    for c in copies:
-        c.wait()
     nodes = vgrad.shape[0]
+    copies[0].wait()
     scale = column(lax.rsqrt(vdegree[...].astype(jnp.float32)))
+    copies[1].wait()
+    copies[2].wait()
     masked = vgrad[...] * vmask[...].astype(jnp.bfloat16)
     scaled[:nodes] = (masked.astype(jnp.float32) * scale).astype(jnp.bfloat16)
+    copies[3].wait()
     scaled[nodes:] = (vfeat[...].astype(jnp.float32) * scale).astype(jnp.bfloat16)
     scale_out[...] = scale
 
@@ -96,35 +98,55 @@
         dense[rows, columns] = value
 
 
-def multiply(nodes, chips, cols, refs):
-    own, other, pair, pair_left, near, far = refs[:6]
+def gathered(nodes, cols, refs):
+    pair, pair_left, near, far = refs[:4]
     rows = CORES * nodes
-    first = [pair_left] + list(refs[6 : 5 + cols])
+    first = [pair_left] + list(refs[4 : 3 + cols])
     second = [pair, near] + [far.at[n * rows : (n + 1) * rows] for n in range(cols - 2)]
-    leave, chunks, chunk_sends = refs[5 + cols :]
-    core = positions()[1]
-    width = leave.shape[1]
-    half = leave.shape[0]
+    core = positions()[1]
     grads = [jnp.where(core == 1, f[...], s[...]) for f, s in zip(first, second)]
-    feats = [jnp.where(core == 1, s[...], f[...]) for f, s in zip(first, second)]
     by_core = [
         jnp.concatenate([g[c * nodes : (c + 1) * nodes] for g in grads], axis=0)
         for c in range(CORES)
     ]
     mine = jnp.where(core == 1, by_core[1], by_core[0])
     theirs = jnp.where(core == 1, by_core[0], by_core[1])
+    return first, second, mine, theirs
+
+
+def weigh(nodes, chips, cols, refs):
+    own, other = refs[:2]
+    leave = refs[-1]
+    half = leave.shape[0]
+    first, second, mine, theirs = gathered(nodes, cols, refs[2:])
+    core = positions()[1]
+    feats = [
+        jnp.where(core == 1, s[:, half:], f[:, :half]) for f, s in zip(first, second)
+    ]
+    features = jnp.concatenate([feats[turned(k)] for k in range(chips)], axis=0)
+    first_rows = (((0,), (0,)), ((), ()))
+    part = jnp.zeros(leave.shape, jnp.float32)
+    for tile, rows in ((own, mine), (other, theirs)):
+        ahead = lax.dot_general(
+            features, tile[...], first_rows, preferred_element_type=jnp.float32
+        )
+        high = ahead.astype(jnp.bfloat16)
+        low = (ahead - high.astype(jnp.float32)).astype(jnp.bfloat16)
+        both = jnp.concatenate([high, low], axis=0)
+        both = jnp.dot(both, rows, preferred_element_type=jnp.float32)
+        part = part + both[:half] + both[half:]
+    leave[...] = part.astype(jnp.bfloat16)
+
+
+def pull(nodes, chips, cols, refs):
+    own, other = refs[:2]
+    chunks, chunk_sends = refs[-2:]
+    core = positions()[1]
+    _, _, mine, theirs = gathered(nodes, cols, refs[2:])
     total = jnp.dot(own[...], mine, preferred_element_type=jnp.float32) + jnp.dot(
         other[...], theirs, preferred_element_type=jnp.float32
     )
-    feats = [jnp.where(core == 0, x[:, :half], x[:, half:]) for x in feats]
-    features = jnp.concatenate([feats[turned(k)] for k in range(chips)], axis=0)
     high = total.astype(jnp.bfloat16)
-    low = (total - high.astype(jnp.float32)).astype(jnp.bfloat16)
-    first_rows = (((0,), (0,)), ((), ()))
-    part = lax.dot_general(features, high, first_rows, preferred_element_type=jnp.float32)
-    part = part + lax.dot_general(features, low, first_rows, preferred_element_type=jnp.float32)
-    part = part.astype(jnp.bfloat16)
-    leave[...] = part
 
     def chunk(x, k, other):
         at = k * CORES * nodes
@@ -260,15 +282,20 @@
         pack, [shape(((cols - 2) * CORES * nodes, width), bf16)], moved[1:] + [dense], flops=HEAVY
     )
     brought = [partner(moved[0]), partner(packed)]
-    leave, kept, leaving = call(
-        lambda *refs: multiply(nodes, chips, cols, refs),
-        [
-            shape((half, width), bf16),
-            shape((chips // 2 * nodes, width), f32), shape((chips // 2 * nodes, width), bf16),
-        ],
-        [dense, partner(dense), pair, pair_left] + brought + moved,
+    operands = [dense, partner(dense), pair, pair_left] + brought + moved
+    (leave,) = call(
+        lambda *refs: weigh(nodes, chips, cols, refs),
+        [shape((half, width), bf16)],
+        operands,
         limit=8 * 2**20 + 4 * size,
-        flops=4 * targets * sources * width + 4 * targets * width * width,
+        flops=4 * targets * sources * half + 8 * sources * half * width,
+    )
+    kept, leaving = call(
+        lambda *refs: pull(nodes, chips, cols, refs),
+        [shape((chips // 2 * nodes, width), f32), shape((chips // 2 * nodes, width), bf16)],
+        operands,
+        limit=8 * 2**20 + 4 * size,
+        flops=4 * targets * sources * width,
     )
     bit = 1
     while 2 * bit < chips:

time: 31.3 us -> 31.1 us (level)
  waiting for transfers between devices: 7.59 us -> 6.81 us
  starting transfers between devices: 18.1 us -> 18.7 us
    ppermute x9, waiting for transfers between devices: 6.15 us -> 5.36 us  [cross(): return lax.ppermute(x, ('row', 'col'), pairs)]
    ppermute x9, starting transfers between devices: 5.9 us -> 6.45 us  [swap(): return lax.ppermute(x, 'row', [(d, d ^ k) for d in range(rows)])]
    pallas_call x10 -> x11, Pallas kernels: 4.03 us -> 4.05 us  [call(): pl.pallas_call(body, out_shape=outs, in_specs=[pl.BlockSpec(memory_space=...]
  transfers between devices with their start and end apart: 18 -> 18, of which waited for: 10 -> 9; matrix products, arithmetic and copies ran while one was open for 0% -> 0% of each run, Pallas kernels for 5% -> 6%
where the time goes in v7:
time: 31.1 us; the launch traced here: 30.9 us
  starting transfers between devices  18.7 us (60%)
  waiting for transfers between devices  6.81 us (22%)
  Pallas kernels  4.05 us (13%)
  between operations  1.38 us (4%)
    ppermute x9, starting transfers between devices, cross(): return lax.ppermute(x, ('row', 'col'), pairs)  12.2 us
    ppermute x9, starting transfers between devices, swap(): return lax.ppermute(x, 'row', [(d, d ^ k) for d in range(rows)])  6.45 us
    ppermute x9, waiting for transfers between devices, cross(): return lax.ppermute(x, ('row', 'col'), pairs)  5.36 us
    pallas_call x11, Pallas kernels, call(): pl.pallas_call(body, out_shape=outs, in_specs=[pl.BlockSpec(memory_space=...  4.05 us
    ppermute x9, waiting for transfers between devices, swap(): return lax.ppermute(x, 'row', [(d, d ^ k) for d in range(rows)])  1.45 us
  transfers between devices with their start and end apart: 18, of which 9 were waited for; matrix products, arithmetic and copies ran while one was open for 0% of the time, Pallas kernels for 6%

profile of v7, /device:TPU:0, one launch (start us, length us, event | category | flops | bytes accessed | tf_op | source)
XLA Modules:
  0.0 30.9 jit_solution(1191289456362514714)
XLA Ops:
  0.6 0.0 copy-start
  0.6 1.0 %shard_map.95 = (bf16[128,256]{1,0:T(8,128)(2,1)S(1)}, f32[64,1]{1,0:T(8,128)S(1)}) custom-call(bf16[64,256]{1,0:T(8,128)(2,1)} %features.1, bf16[64,256]{1,0:T(8,128)(2,1)} %grad_out.1, s32[64,256]{1,0:T(8,128)} %relu_mask.1, s32[1,64]{1,0:T(1,128)} %bitcast.1), custom_call_target="tpu_custom_call" | custom-call | bytes 197120 | tf_op jit(solution)/shard_map/pallas_call | solution.py:28
  1.6 0.5 %collective-permute-start = (bf16[128,256]{1,0:T(8,128)(2,1)S(1)}, bf16[128,256]{1,0:T(8,128)(2,1)S(1)}, u32[]{:S(2)}, u32[]{:S(2)}) collective-permute-start(bf16[128,256]{1,0:T(8,128)(2,1)S(1)} %get-tuple-element.12.scaled), channel_id=1, source_target_pairs={{0,4},{4,0},{8,12},{12,8},{16,20},{20,16},{24,28},{28,24},{1,5},{5... | collective-permute-start | bytes 196616 | tf_op jit(solution)/shard_map/ppermute | solution.py:237
  2.8 0.3 collective-permute-done.other
  3.1 0.0 copy-start.1
  3.1 4.8 %collective-permute-start.5 = (bf16[128,256]{1,0:T(8,128)(2,1)S(1)}, bf16[128,256]{1,0:T(8,128)(2,1)S(1)}, u32[]{:S(2)}, u32[]{:S(2)}) collective-permute-start(bf16[128,256]{1,0:T(8,128)(2,1)S(1)} %get-tuple-element.13.after.refs_2_), channel_id=1, source_target_pairs={{0,7},{1,6},{2,5},{3,4},{4,24},{5,25},{6,26},{7,27},{8,15},{9,14},... | collective-permute-start | bytes 196616 | tf_op jit(solution)/shard_map/ppermute | solution.py:248
  7.8 1.4 %collective-permute-start.4 = (bf16[128,256]{1,0:T(8,128)(2,1)S(1)}, bf16[128,256]{1,0:T(8,128)(2,1)S(1)}, u32[]{:S(2)}, u32[]{:S(2)}) collective-permute-start(bf16[128,256]{1,0:T(8,128)(2,1)S(1)} %get-tuple-element.13.after.refs_2_), channel_id=1, source_target_pairs={{0,6},{1,7},{2,4},{3,5},{4,8},{5,9},{6,10},{7,11},{8,14},{9,15},{1... | collective-permute-start | bytes 196616 | tf_op jit(solution)/shard_map/ppermute | solution.py:248
  9.2 0.0 collective-permute-start.2
  9.2 0.0 copy-done
  9.2 0.0 copy-done.1
  9.2 0.6 %shard_map.97.refs_2_.refs_0_ = bf16[512,256]{1,0:T(8,128)(2,1)S(1)} custom-call(bf16[1,1,6,128,128]{4,3,2,1,0:T(8,128)(2,1)S(1)} %copy-done, s32[1,1,6]{2,1,0:T(1,128)S(1)} %copy-done.1, s32[1,1]{1,0:T(1,128)S(6)} %copy.10.count, bf16[128,256]{1,0:T(8,128)(2,1)S(1)} %get-tuple-element.13.after.refs_2_), custom_call_target="tpu_custom_call" | custom-call | bytes 524316 | tf_op jit(solution)/shard_map/pallas_call | solution.py:28
  9.9 1.1 %collective-permute-start.1 = (bf16[512,256]{1,0:T(8,128)(2,1)S(1)}, bf16[512,256]{1,0:T(8,128)(2,1)S(1)}, u32[]{:S(2)}, u32[]{:S(2)}) collective-permute-start(bf16[512,256]{1,0:T(8,128)(2,1)S(1)} %shard_map.97.refs_2_.refs_0_), channel_id=1, source_target_pairs={{0,4},{4,0},{8,12},{12,8},{16,20},{20,16},{24,28},{28,24},{1,5},{5... | collective-permute-start | bytes 786440 | tf_op jit(solution)/shard_map/ppermute | solution.py:237
  11.0 0.0 collective-permute-done.5.refs_1_.refs_8_
  11.0 0.6 %collective-permute-done.4.refs_0_.refs_7_ = bf16[128,256]{1,0:T(8,128)(2,1)S(1)} collective-permute-done((bf16[128,256]{1,0:T(8,128)(2,1)S(1)}, bf16[128,256]{1,0:T(8,128)(2,1)S(1)}, u32[]{:S(2)}, u32[]{:S(2)}) %collective-permute-start.4) | collective-permute-done | bytes 65568 | tf_op jit(solution)/shard_map/ppermute | solution.py:248
  11.5 0.2 collective-permute-start.6
  11.7 1.2 %collective-permute-done.2.refs_6_ = bf16[128,256]{1,0:T(8,128)(2,1)S(1)} collective-permute-done((bf16[128,256]{1,0:T(8,128)(2,1)S(1)}, bf16[128,256]{1,0:T(8,128)(2,1)S(1)}, u32[]{:S(2)}, u32[]{:S(2)}) %collective-permute-start.2) | collective-permute-done | bytes 65568 | tf_op jit(solution)/shard_map/ppermute | solution.py:248
  12.9 0.2 collective-permute-start.3
  13.1 1.0 %collective-permute-done.3.refs_4_ = bf16[128,256]{1,0:T(8,128)(2,1)S(1)} collective-permute-done((bf16[128,256]{1,0:T(8,128)(2,1)S(1)}, bf16[128,256]{1,0:T(8,128)(2,1)S(1)}, u32[]{:S(2)}, u32[]{:S(2)}) %collective-permute-start.3) | collective-permute-done | bytes 65568 | tf_op jit(solution)/shard_map/ppermute | solution.py:237
  14.2 0.0 collective-permute-done.6.refs_5_
  14.2 0.0 collective-permute-done.1.refs_1_
  14.2 0.5 %shard_map.102 = bf16[128,256]{1,0:T(8,128)(2,1)S(1)} custom-call(bf16[512,256]{1,0:T(8,128)(2,1)S(1)} %shard_map.97.refs_2_.refs_0_, bf16[512,256]{1,0:T(8,128)(2,1)S(1)} %collective-permute-done.1.refs_1_, bf16[128,256]{1,0:T(8,128)(2,1)S(1)} %get-tuple-element.13.after.refs_2_, bf16[128,256]{1,0:T(8,128)(2,1)S(1)} %get-tuple-element.14.refs_3_, ...), custom_call_target="tpu_custom_call" | custom-call | flops 134217728 | bytes 1114112 | tf_op jit(solution)/shard_map/pallas_call | solution.py:28
  14.7 2.8 %collective-permute-start.12 = (bf16[128,256]{1,0:T(8,128)(2,1)S(1)}, bf16[128,256]{1,0:T(8,128)(2,1)S(1)}, u32[]{:S(2)}, u32[]{:S(2)}) collective-permute-start(bf16[128,256]{1,0:T(8,128)(2,1)S(1)} %shard_map.102), channel_id=1, source_target_pairs={{0,7},{1,6},{2,5},{3,4},{4,24},{5,25},{6,26},{7,27},{8,15},{9,14},... | collective-permute-start | bytes 196616 | tf_op jit(solution)/shard_map/ppermute | solution.py:248
  17.5 0.2 collective-permute-start.11
  17.7 0.0 collective-permute-start.10
  17.7 0.8 %collective-permute-start.9 = (bf16[128,256]{1,0:T(8,128)(2,1)S(1)}, bf16[128,256]{1,0:T(8,128)(2,1)S(1)}, u32[]{:S(2)}, u32[]{:S(2)}) collective-permute-start(bf16[128,256]{1,0:T(8,128)(2,1)S(1)} %shard_map.102), channel_id=1, source_target_pairs={{0,4},{4,0},{8,12},{12,8},{16,20},{20,16},{24,28},{28,24},{1,5},{5... | collective-permute-start | bytes 196616 | tf_op jit(solution)/shard_map/ppermute | solution.py:237
  18.4 0.3 shard_map.99
  18.7 0.9 %collective-permute-start.7 = (bf16[128,256]{1,0:T(8,128)(2,1)S(1)}, bf16[128,256]{1,0:T(8,128)(2,1)S(1)}, u32[]{:S(2)}, u32[]{:S(2)}) collective-permute-start(bf16[128,256]{1,0:T(8,128)(2,1)S(1)} %get-tuple-element.16), channel_id=1, source_target_pairs={{0,12},{4,8},{8,4},{12,0},{16,28},{20,24},{24,20},{28,16},{1,13},{... | collective-permute-start | bytes 196616 | tf_op jit(solution)/shard_map/ppermute | solution.py:237
  19.6 0.0 collective-permute-done.12.refs_3_
  19.6 1.5 %collective-permute-done.11.refs_2_ = bf16[128,256]{1,0:T(8,128)(2,1)S(1)} collective-permute-done((bf16[128,256]{1,0:T(8,128)(2,1)S(1)}, bf16[128,256]{1,0:T(8,128)(2,1)S(1)}, u32[]{:S(2)}, u32[]{:S(2)}) %collective-permute-start.11) | collective-permute-done | bytes 65568 | tf_op jit(solution)/shard_map/ppermute | solution.py:248
  21.2 0.2 collective-permute-done.10.refs_1_
  21.4 0.0 collective-permute-done.9.refs_0_
  21.4 3.1 %collective-permute-start.16 = (bf16[128,256]{1,0:T(8,128)(2,1)S(1)}, bf16[128,256]{1,0:T(8,128)(2,1)S(1)}, u32[]{:S(2)}, u32[]{:S(2)}) collective-permute-start(bf16[128,256]{1,0:T(8,128)(2,1)S(1)} %shard_map.103), channel_id=1, source_target_pairs={{0,7},{1,6},{2,5},{3,4},{4,24},{5,25},{6,26},{7,27},{8,15},{9,14},... | collective-permute-start | bytes 196616 | tf_op jit(solution)/shard_map/ppermute | solution.py:248
  24.5 0.0 collective-permute-start.15
  24.5 0.0 collective-permute-start.14
  24.5 0.9 %collective-permute-start.13 = (bf16[128,256]{1,0:T(8,128)(2,1)S(1)}, bf16[128,256]{1,0:T(8,128)(2,1)S(1)}, u32[]{:S(2)}, u32[]{:S(2)}) collective-permute-start(bf16[128,256]{1,0:T(8,128)(2,1)S(1)} %shard_map.103), channel_id=1, source_target_pairs={{0,4},{4,0},{8,12},{12,8},{16,20},{20,16},{24,28},{28,24},{1,5},{5... | collective-permute-start | bytes 196616 | tf_op jit(solution)/shard_map/ppermute | solution.py:237
  25.4 0.0 collective-permute-done.7.received
  25.4 0.0 copy-start.2
  25.4 0.9 %collective-permute-start.8 = (bf16[64,256]{1,0:T(8,128)(2,1)S(1)}, bf16[64,256]{1,0:T(8,128)(2,1)S(1)}, u32[]{:S(2)}, u32[]{:S(2)}) collective-permute-start(bf16[64,256]{1,0:T(8,128)(2,1)S(1)} %get-tuple-element.18), channel_id=1, source_target_pairs={{0,20},{4,16},{8,28},{12,24},{16,4},{20,0},{24,12},{28,8},{1,21},{... | collective-permute-start | bytes 98312 | tf_op jit(solution)/shard_map/ppermute | solution.py:237
  26.3 0.1 collective-permute-done.16.refs_3_
  26.4 1.8 %collective-permute-done.15.refs_2_ = bf16[128,256]{1,0:T(8,128)(2,1)S(1)} collective-permute-done((bf16[128,256]{1,0:T(8,128)(2,1)S(1)}, bf16[128,256]{1,0:T(8,128)(2,1)S(1)}, u32[]{:S(2)}, u32[]{:S(2)}) %collective-permute-start.15) | collective-permute-done | bytes 65568 | tf_op jit(solution)/shard_map/ppermute | solution.py:248
  28.2 0.0 collective-permute-done.14.refs_1_
  28.2 0.0 collective-permute-done.13.refs_0_
  28.2 1.0 %collective-permute-start.17 = (f32[128,256]{1,0:T(8,128)S(1)}, f32[128,256]{1,0:T(8,128)S(1)}, u32[]{:S(2)}, u32[]{:S(2)}) collective-permute-start(f32[128,256]{1,0:T(8,128)S(1)} %shard_map.104.own), channel_id=1, source_target_pairs={{0,4},{4,0},{8,12},{12,8},{16,20},{20,16},{24,28},{28,24},{1,5},{5... | collective-permute-start | bytes 393224 | tf_op jit(solution)/shard_map/ppermute | solution.py:237
  29.2 0.0 collective-permute-done.8.received
  29.2 0.0 copy-done.2
  29.2 0.8 %shard_map.101 = (f32[64,256]{1,0:T(8,128)}, f32[8,128]{1,0:T(8,128)S(1)}) custom-call(f32[64,256]{1,0:T(8,128)S(1)} %get-tuple-element.17.kept, bf16[64,256]{1,0:T(8,128)(2,1)S(1)} %collective-permute-done.8.received, f32[64,1]{1,0:T(8,128)S(1)} %get-tuple-element.19.scale, bf16[256,256]{1,0:T(8,128)(2,1)S(1)} %copy-done.2), custom_call_target="tpu_custom_call" | custom-call | flops 4000000000 | bytes 299264 | tf_op jit(solution)/shard_map/pallas_call | solution.py:28
  30.1 0.1 collective-permute-done.17.other
  30.2 0.7 %shard_map.105 = f32[256,256]{1,0:T(8,128)} custom-call(f32[8,128]{1,0:T(8,128)S(1)} %get-tuple-element.21.after, f32[128,256]{1,0:T(8,128)S(1)} %shard_map.104.own, f32[128,256]{1,0:T(8,128)S(1)} %collective-permute-done.17.other), custom_call_target="tpu_custom_call" | custom-call | bytes 528384 | tf_op jit(solution)/shard_map/pallas_call | solution.py:28
  (5 shorter events, 0.1 us)
Async XLA Ops:
  0.6 8.6 %copy-start = (bf16[1,1,6,128,128]{4,3,2,1,0:T(8,128)(2,1)S(1)}, bf16[1,1,6,128,128]{4,3,2,1,0:T(8,128)(2,1)}, u32[]{:S(2)}) copy-start(bf16[1,1,6,128,128]{4,3,2,1,0:T(8,128)(2,1)} %blocks.1) | copy-start | bytes 589828
  1.6 1.4 %collective-permute-start = (bf16[128,256]{1,0:T(8,128)(2,1)S(1)}, bf16[128,256]{1,0:T(8,128)(2,1)S(1)}, u32[]{:S(2)}, u32[]{:S(2)}) collective-permute-start(bf16[128,256]{1,0:T(8,128)(2,1)S(1)} %get-tuple-element.12.scaled), channel_id=1, source_target_pairs={{0,4},{4,0},{8,12},{12,8},{16,20},{20,16},{24,28},{28,24},{1,5},{5... | collective-permute-start | bytes 196616 | tf_op jit(solution)/shard_map/ppermute | solution.py:237
  3.1 6.2 %copy-start.1 = (s32[1,1,6]{2,1,0:T(1,128)S(1)}, s32[1,1,6]{2,1,0:T(1,128)}, u32[]{:S(2)}) copy-start(s32[1,1,6]{2,1,0:T(1,128)} %slots.1) | copy-start | bytes 76
  3.1 7.9 %collective-permute-start.5 = (bf16[128,256]{1,0:T(8,128)(2,1)S(1)}, bf16[128,256]{1,0:T(8,128)(2,1)S(1)}, u32[]{:S(2)}, u32[]{:S(2)}) collective-permute-start(bf16[128,256]{1,0:T(8,128)(2,1)S(1)} %get-tuple-element.13.after.refs_2_), channel_id=1, source_target_pairs={{0,7},{1,6},{2,5},{3,4},{4,24},{5,25},{6,26},{7,27},{8,15},{9,14},... | collective-permute-start | bytes 196616 | tf_op jit(solution)/shard_map/ppermute | solution.py:248
  7.8 3.7 %collective-permute-start.4 = (bf16[128,256]{1,0:T(8,128)(2,1)S(1)}, bf16[128,256]{1,0:T(8,128)(2,1)S(1)}, u32[]{:S(2)}, u32[]{:S(2)}) collective-permute-start(bf16[128,256]{1,0:T(8,128)(2,1)S(1)} %get-tuple-element.13.after.refs_2_), channel_id=1, source_target_pairs={{0,6},{1,7},{2,4},{3,5},{4,8},{5,9},{6,10},{7,11},{8,14},{9,15},{1... | collective-permute-start | bytes 196616 | tf_op jit(solution)/shard_map/ppermute | solution.py:248
  9.2 3.7 %collective-permute-start.2 = (bf16[128,256]{1,0:T(8,128)(2,1)S(1)}, bf16[128,256]{1,0:T(8,128)(2,1)S(1)}, u32[]{:S(2)}, u32[]{:S(2)}) collective-permute-start(bf16[128,256]{1,0:T(8,128)(2,1)S(1)} %get-tuple-element.13.after.refs_2_), channel_id=1, source_target_pairs={{0,5},{1,4},{2,7},{3,6},{4,16},{5,17},{6,18},{7,19},{8,13},{9,12},... | collective-permute-start | bytes 196616 | tf_op jit(solution)/shard_map/ppermute | solution.py:248
  9.9 4.3 %collective-permute-start.1 = (bf16[512,256]{1,0:T(8,128)(2,1)S(1)}, bf16[512,256]{1,0:T(8,128)(2,1)S(1)}, u32[]{:S(2)}, u32[]{:S(2)}) collective-permute-start(bf16[512,256]{1,0:T(8,128)(2,1)S(1)} %shard_map.97.refs_2_.refs_0_), channel_id=1, source_target_pairs={{0,4},{4,0},{8,12},{12,8},{16,20},{20,16},{24,28},{28,24},{1,5},{5... | collective-permute-start | bytes 786440 | tf_op jit(solution)/shard_map/ppermute | solution.py:237
  11.5 2.6 %collective-permute-start.6 = (bf16[256,256]{1,0:T(8,128)(2,1)S(1)}, bf16[256,256]{1,0:T(8,128)(2,1)S(1)}, u32[]{:S(2)}, u32[]{:S(2)}) collective-permute-start(bf16[256,256]{1,0:T(8,128)(2,1)S(1)} %shard_map.98), channel_id=1, source_target_pairs={{0,4},{4,0},{8,12},{12,8},{16,20},{20,16},{24,28},{28,24},{1,5},{5... | collective-permute-start | bytes 393224 | tf_op jit(solution)/shard_map/ppermute | solution.py:237
  12.9 1.3 %collective-permute-start.3 = (bf16[128,256]{1,0:T(8,128)(2,1)S(1)}, bf16[128,256]{1,0:T(8,128)(2,1)S(1)}, u32[]{:S(2)}, u32[]{:S(2)}) collective-permute-start(bf16[128,256]{1,0:T(8,128)(2,1)S(1)} %collective-permute-done.2.refs_6_), channel_id=1, source_target_pairs={{0,4},{4,0},{8,12},{12,8},{16,20},{20,16},{24,28},{28,24},{1,5},{5... | collective-permute-start | bytes 196616 | tf_op jit(solution)/shard_map/ppermute | solution.py:237
  14.7 5.0 %collective-permute-start.12 = (bf16[128,256]{1,0:T(8,128)(2,1)S(1)}, bf16[128,256]{1,0:T(8,128)(2,1)S(1)}, u32[]{:S(2)}, u32[]{:S(2)}) collective-permute-start(bf16[128,256]{1,0:T(8,128)(2,1)S(1)} %shard_map.102), channel_id=1, source_target_pairs={{0,7},{1,6},{2,5},{3,4},{4,24},{5,25},{6,26},{7,27},{8,15},{9,14},... | collective-permute-start | bytes 196616 | tf_op jit(solution)/shard_map/ppermute | solution.py:248
  17.5 3.7 %collective-permute-start.11 = (bf16[128,256]{1,0:T(8,128)(2,1)S(1)}, bf16[128,256]{1,0:T(8,128)(2,1)S(1)}, u32[]{:S(2)}, u32[]{:S(2)}) collective-permute-start(bf16[128,256]{1,0:T(8,128)(2,1)S(1)} %shard_map.102), channel_id=1, source_target_pairs={{0,6},{1,7},{2,4},{3,5},{4,8},{5,9},{6,10},{7,11},{8,14},{9,15},{1... | collective-permute-start | bytes 196616 | tf_op jit(solution)/shard_map/ppermute | solution.py:248
  17.7 3.7 %collective-permute-start.10 = (bf16[128,256]{1,0:T(8,128)(2,1)S(1)}, bf16[128,256]{1,0:T(8,128)(2,1)S(1)}, u32[]{:S(2)}, u32[]{:S(2)}) collective-permute-start(bf16[128,256]{1,0:T(8,128)(2,1)S(1)} %shard_map.102), channel_id=1, source_target_pairs={{0,5},{1,4},{2,7},{3,6},{4,16},{5,17},{6,18},{7,19},{8,13},{9,12},... | collective-permute-start | bytes 196616 | tf_op jit(solution)/shard_map/ppermute | solution.py:248
  17.7 3.7 %collective-permute-start.9 = (bf16[128,256]{1,0:T(8,128)(2,1)S(1)}, bf16[128,256]{1,0:T(8,128)(2,1)S(1)}, u32[]{:S(2)}, u32[]{:S(2)}) collective-permute-start(bf16[128,256]{1,0:T(8,128)(2,1)S(1)} %shard_map.102), channel_id=1, source_target_pairs={{0,4},{4,0},{8,12},{12,8},{16,20},{20,16},{24,28},{28,24},{1,5},{5... | collective-permute-start | bytes 196616 | tf_op jit(solution)/shard_map/ppermute | solution.py:237
  18.7 6.7 %collective-permute-start.7 = (bf16[128,256]{1,0:T(8,128)(2,1)S(1)}, bf16[128,256]{1,0:T(8,128)(2,1)S(1)}, u32[]{:S(2)}, u32[]{:S(2)}) collective-permute-start(bf16[128,256]{1,0:T(8,128)(2,1)S(1)} %get-tuple-element.16), channel_id=1, source_target_pairs={{0,12},{4,8},{8,4},{12,0},{16,28},{20,24},{24,20},{28,16},{1,13},{... | collective-permute-start | bytes 196616 | tf_op jit(solution)/shard_map/ppermute | solution.py:237
  21.4 5.0 %collective-permute-start.16 = (bf16[128,256]{1,0:T(8,128)(2,1)S(1)}, bf16[128,256]{1,0:T(8,128)(2,1)S(1)}, u32[]{:S(2)}, u32[]{:S(2)}) collective-permute-start(bf16[128,256]{1,0:T(8,128)(2,1)S(1)} %shard_map.103), channel_id=1, source_target_pairs={{0,7},{1,6},{2,5},{3,4},{4,24},{5,25},{6,26},{7,27},{8,15},{9,14},... | collective-permute-start | bytes 196616 | tf_op jit(solution)/shard_map/ppermute | solution.py:248
  24.5 3.7 %collective-permute-start.15 = (bf16[128,256]{1,0:T(8,128)(2,1)S(1)}, bf16[128,256]{1,0:T(8,128)(2,1)S(1)}, u32[]{:S(2)}, u32[]{:S(2)}) collective-permute-start(bf16[128,256]{1,0:T(8,128)(2,1)S(1)} %shard_map.103), channel_id=1, source_target_pairs={{0,6},{1,7},{2,4},{3,5},{4,8},{5,9},{6,10},{7,11},{8,14},{9,15},{1... | collective-permute-start | bytes 196616 | tf_op jit(solution)/shard_map/ppermute | solution.py:248
  24.5 3.7 %collective-permute-start.14 = (bf16[128,256]{1,0:T(8,128)(2,1)S(1)}, bf16[128,256]{1,0:T(8,128)(2,1)S(1)}, u32[]{:S(2)}, u32[]{:S(2)}) collective-permute-start(bf16[128,256]{1,0:T(8,128)(2,1)S(1)} %shard_map.103), channel_id=1, source_target_pairs={{0,5},{1,4},{2,7},{3,6},{4,16},{5,17},{6,18},{7,19},{8,13},{9,12},... | collective-permute-start | bytes 196616 | tf_op jit(solution)/shard_map/ppermute | solution.py:248
  24.5 3.7 %collective-permute-start.13 = (bf16[128,256]{1,0:T(8,128)(2,1)S(1)}, bf16[128,256]{1,0:T(8,128)(2,1)S(1)}, u32[]{:S(2)}, u32[]{:S(2)}) collective-permute-start(bf16[128,256]{1,0:T(8,128)(2,1)S(1)} %shard_map.103), channel_id=1, source_target_pairs={{0,4},{4,0},{8,12},{12,8},{16,20},{20,16},{24,28},{28,24},{1,5},{5... | collective-permute-start | bytes 196616 | tf_op jit(solution)/shard_map/ppermute | solution.py:237
  25.4 3.8 %copy-start.2 = (bf16[256,256]{1,0:T(8,128)(2,1)S(1)}, bf16[256,256]{1,0:T(8,128)(2,1)}, u32[]{:S(2)}) copy-start(bf16[256,256]{1,0:T(8,128)(2,1)} %weight.1) | copy-start | bytes 393220
  25.4 3.8 %collective-permute-start.8 = (bf16[64,256]{1,0:T(8,128)(2,1)S(1)}, bf16[64,256]{1,0:T(8,128)(2,1)S(1)}, u32[]{:S(2)}, u32[]{:S(2)}) collective-permute-start(bf16[64,256]{1,0:T(8,128)(2,1)S(1)} %get-tuple-element.18), channel_id=1, source_target_pairs={{0,20},{4,16},{8,28},{12,24},{16,4},{20,0},{24,12},{28,8},{1,21},{... | collective-permute-start | bytes 98312 | tf_op jit(solution)/shard_map/ppermute | solution.py:237
  28.2 2.0 %collective-permute-start.17 = (f32[128,256]{1,0:T(8,128)S(1)}, f32[128,256]{1,0:T(8,128)S(1)}, u32[]{:S(2)}, u32[]{:S(2)}) collective-permute-start(f32[128,256]{1,0:T(8,128)S(1)} %shard_map.104.own), channel_id=1, source_target_pairs={{0,4},{4,0},{8,12},{12,8},{16,20},{20,16},{24,28},{28,24},{1,5},{5... | collective-permute-start | bytes 393224 | tf_op jit(solution)/shard_map/ppermute | solution.py:237

commit v8 on v7

--- a/solution.py
+++ b/solution.py
@@ -71,7 +71,7 @@
     core = positions()[1]
     mine = pl.ds(pl.multiple_of(core * nodes, nodes), nodes)
     theirs = pl.ds(pl.multiple_of((1 - core) * nodes, nodes), nodes)
-    sends, stays = jnp.where(core == 0, 0, nodes), jnp.where(core == 0, nodes, 0)
+    sends, stays = jnp.where(core == 1, 0, nodes), jnp.where(core == 1, nodes, 0)
     for out, at in ((pair, sends), (pair_left, stays)):
         rows = pl.ds(pl.multiple_of(at, nodes), nodes)
         out[mine] = scaled[rows]
@@ -101,8 +101,8 @@
 def gathered(nodes, cols, refs):
     pair, pair_left, near, far = refs[:4]
     rows = CORES * nodes
-    first = [pair_left] + list(refs[4 : 3 + cols])
-    second = [pair, near] + [far.at[n * rows : (n + 1) * rows] for n in range(cols - 2)]
+    first = [pair] + list(refs[4 : 3 + cols])
+    second = [pair_left, near] + [far.at[n * rows : (n + 1) * rows] for n in range(cols - 2)]
     core = positions()[1]
     grads = [jnp.where(core == 1, f[...], s[...]) for f, s in zip(first, second)]
     by_core = [
@@ -121,7 +121,7 @@
     first, second, mine, theirs = gathered(nodes, cols, refs[2:])
     core = positions()[1]
     feats = [
-        jnp.where(core == 1, s[:, half:], f[:, :half]) for f, s in zip(first, second)
+        jnp.where(core == 1, s[:, :half], f[:, half:]) for f, s in zip(first, second)
     ]
     features = jnp.concatenate([feats[turned(k)] for k in range(chips)], axis=0)
     first_rows = (((0,), (0,)), ((), ()))
@@ -250,6 +250,17 @@
     def spread(x):
         return [cross(x, k) for k in range(1, cols)]
 
+    def along(x):
+        out = []
+        for k in range(1, cols):
+            pairs = []
+            for r in range(rows):
+                for j in range(cols):
+                    to = (r, j ^ k) if r % CORES == 1 else (r ^ (CORES * turned(k)), j)
+                    pairs.append((r * cols + j, to[0] * cols + to[1]))
+            out.append(lax.ppermute(x, ("row", "col"), pairs))
+        return out
+
     scaled, scale = call(
         scale_nodes,
         [shape((2 * nodes, width), bf16), shape((nodes, 1), f32)],
@@ -268,7 +279,7 @@
         pair_up, [shape((CORES * nodes, width), bf16)] * 2,
         [scaled, partner(scaled), block_count], [VMEM, VMEM, SMEM],
     )
-    moved = spread(pair)
+    moved = along(pair)
     targets, sources = rows * nodes, cols * nodes
     size = targets * sources * 2
     (dense,) = call(
@@ -314,7 +325,7 @@
         [kept, received, scale, weight],
         flops=HEAVY,
     )
-    (once,) = call(sum_parts, [shape((half, width), bf16)], [partner(leave)] + spread(leave))
+    (once,) = call(sum_parts, [shape((half, width), bf16)], [leave] + along(leave))
     factor = (nodes * rows * cols) ** (-0.5)
     (own_half,) = call(
         functools.partial(finish_weight, factor),

time: 31.1 us -> 30.6 us (0.984)
  starting transfers between devices: 18.7 us -> 17.4 us
  waiting for transfers between devices: 6.81 us -> 7.29 us
  Pallas kernels: 4.05 us -> 4.44 us
    ppermute x9 -> x3, starting transfers between devices: 12.2 us -> 3.47 us  [cross(): return lax.ppermute(x, ('row', 'col'), pairs)]
    ppermute x0 -> x6, starting transfers between devices: none -> 8.06 us  [along(): out.append(lax.ppermute(x, ('row', 'col'), pairs))]
    ppermute x0 -> x6, waiting for transfers between devices: none -> 3.8 us  [along(): out.append(lax.ppermute(x, ('row', 'col'), pairs))]
    ppermute x9 -> x3, waiting for transfers between devices: 5.36 us -> 1.84 us  [cross(): return lax.ppermute(x, ('row', 'col'), pairs)]
    ppermute x9 -> x8, starting transfers between devices: 6.45 us -> 5.84 us  [swap(): return lax.ppermute(x, 'row', [(d, d ^ k) for d in range(rows)])]
    pallas_call x11, Pallas kernels: 4.05 us -> 4.44 us  [call(): pl.pallas_call(body, out_shape=outs, in_specs=[pl.BlockSpec(memory_space=...]
    ppermute x9 -> x8, waiting for transfers between devices: 1.45 us -> 1.65 us  [swap(): return lax.ppermute(x, 'row', [(d, d ^ k) for d in range(rows)])]
  transfers between devices with their start and end apart: 18 -> 17, of which waited for: 9 -> 8; matrix products, arithmetic and copies ran while one was open for 0% -> 0% of each run, Pallas kernels for 6% -> 7%
where the time goes in v8:
time: 30.6 us; the launch traced here: 30.5 us
  starting transfers between devices  17.4 us (57%)
  waiting for transfers between devices  7.29 us (24%)
  Pallas kernels  4.44 us (15%)
  between operations  1.37 us (4%)
    ppermute x6, starting transfers between devices, along(): out.append(lax.ppermute(x, ('row', 'col'), pairs))  8.06 us
    ppermute x8, starting transfers between devices, swap(): return lax.ppermute(x, 'row', [(d, d ^ k) for d in range(rows)])  5.84 us
    pallas_call x11, Pallas kernels, call(): pl.pallas_call(body, out_shape=outs, in_specs=[pl.BlockSpec(memory_space=...  4.44 us
    ppermute x6, waiting for transfers between devices, along(): out.append(lax.ppermute(x, ('row', 'col'), pairs))  3.8 us
    ppermute x3, starting transfers between devices, cross(): return lax.ppermute(x, ('row', 'col'), pairs)  3.47 us
    ppermute x3, waiting for transfers between devices, cross(): return lax.ppermute(x, ('row', 'col'), pairs)  1.84 us
    ppermute x8, waiting for transfers between devices, swap(): return lax.ppermute(x, 'row', [(d, d ^ k) for d in range(rows)])  1.65 us
  transfers between devices with their start and end apart: 17, of which 8 were waited for; matrix products, arithmetic and copies ran while one was open for 0% of the time, Pallas kernels for 7%

profile of v8, /device:TPU:0, one launch (start us, length us, event | category | flops | bytes accessed | tf_op | source)
XLA Modules:
  0.0 30.5 jit_solution(3445529242607541096)
XLA Ops:
  0.6 0.0 copy-start
  0.6 1.0 %shard_map.95 = (bf16[128,256]{1,0:T(8,128)(2,1)S(1)}, f32[64,1]{1,0:T(8,128)S(1)}) custom-call(bf16[64,256]{1,0:T(8,128)(2,1)} %features.1, bf16[64,256]{1,0:T(8,128)(2,1)} %grad_out.1, s32[64,256]{1,0:T(8,128)} %relu_mask.1, s32[1,64]{1,0:T(1,128)} %bitcast.1), custom_call_target="tpu_custom_call" | custom-call | bytes 197120 | tf_op jit(solution)/shard_map/pallas_call | solution.py:28
  1.6 0.5 %collective-permute-start = (bf16[128,256]{1,0:T(8,128)(2,1)S(1)}, bf16[128,256]{1,0:T(8,128)(2,1)S(1)}, u32[]{:S(2)}, u32[]{:S(2)}) collective-permute-start(bf16[128,256]{1,0:T(8,128)(2,1)S(1)} %get-tuple-element.12.scaled), channel_id=1, source_target_pairs={{0,4},{4,0},{8,12},{12,8},{16,20},{20,16},{24,28},{28,24},{1,5},{5... | collective-permute-start | bytes 196616 | tf_op jit(solution)/shard_map/ppermute | solution.py:237
  2.8 0.3 collective-permute-done.other
  3.1 0.0 copy-start.1
  3.1 3.9 %collective-permute-start.5 = (bf16[128,256]{1,0:T(8,128)(2,1)S(1)}, bf16[128,256]{1,0:T(8,128)(2,1)S(1)}, u32[]{:S(2)}, u32[]{:S(2)}) collective-permute-start(bf16[128,256]{1,0:T(8,128)(2,1)S(1)} %get-tuple-element.13.after.refs_2_), channel_id=1, source_target_pairs={{0,24},{1,25},{2,26},{3,27},{4,7},{5,6},{6,5},{7,4},{8,16},{9,17},... | collective-permute-start | bytes 196616 | tf_op jit(solution)/shard_map/ppermute | solution.py:261
  6.9 0.5 %collective-permute-start.4 = (bf16[128,256]{1,0:T(8,128)(2,1)S(1)}, bf16[128,256]{1,0:T(8,128)(2,1)S(1)}, u32[]{:S(2)}, u32[]{:S(2)}) collective-permute-start(bf16[128,256]{1,0:T(8,128)(2,1)S(1)} %get-tuple-element.13.after.refs_2_), channel_id=1, source_target_pairs={{0,8},{1,9},{2,10},{3,11},{4,6},{5,7},{6,4},{7,5},{8,0},{9,1},{10,... | collective-permute-start | bytes 196616 | tf_op jit(solution)/shard_map/ppermute | solution.py:261
  7.5 0.1 collective-permute-start.2
  7.6 0.0 copy-done
  7.6 0.0 copy-done.1
  7.6 1.0 %shard_map.97.refs_2_.refs_0_ = bf16[512,256]{1,0:T(8,128)(2,1)S(1)} custom-call(bf16[1,1,6,128,128]{4,3,2,1,0:T(8,128)(2,1)S(1)} %copy-done, s32[1,1,6]{2,1,0:T(1,128)S(1)} %copy-done.1, s32[1,1]{1,0:T(1,128)S(6)} %copy.10.count, bf16[128,256]{1,0:T(8,128)(2,1)S(1)} %get-tuple-element.13.after.refs_2_), custom_call_target="tpu_custom_call" | custom-call | bytes 524316 | tf_op jit(solution)/shard_map/pallas_call | solution.py:28
  8.6 0.8 %collective-permute-start.1 = (bf16[512,256]{1,0:T(8,128)(2,1)S(1)}, bf16[512,256]{1,0:T(8,128)(2,1)S(1)}, u32[]{:S(2)}, u32[]{:S(2)}) collective-permute-start(bf16[512,256]{1,0:T(8,128)(2,1)S(1)} %shard_map.97.refs_2_.refs_0_), channel_id=1, source_target_pairs={{0,4},{4,0},{8,12},{12,8},{16,20},{20,16},{24,28},{28,24},{1,5},{5... | collective-permute-start | bytes 786440 | tf_op jit(solution)/shard_map/ppermute | solution.py:237
  9.4 0.0 collective-permute-done.5.refs_1_.refs_8_
  9.4 1.8 %collective-permute-done.4.refs_0_.refs_7_ = bf16[128,256]{1,0:T(8,128)(2,1)S(1)} collective-permute-done((bf16[128,256]{1,0:T(8,128)(2,1)S(1)}, bf16[128,256]{1,0:T(8,128)(2,1)S(1)}, u32[]{:S(2)}, u32[]{:S(2)}) %collective-permute-start.4) | collective-permute-done | bytes 65568 | tf_op jit(solution)/shard_map/ppermute | solution.py:261
  11.2 0.8 %collective-permute-start.6 = (bf16[256,256]{1,0:T(8,128)(2,1)S(1)}, bf16[256,256]{1,0:T(8,128)(2,1)S(1)}, u32[]{:S(2)}, u32[]{:S(2)}) collective-permute-start(bf16[256,256]{1,0:T(8,128)(2,1)S(1)} %shard_map.98), channel_id=1, source_target_pairs={{0,4},{4,0},{8,12},{12,8},{16,20},{20,16},{24,28},{28,24},{1,5},{5... | collective-permute-start | bytes 393224 | tf_op jit(solution)/shard_map/ppermute | solution.py:237
  12.1 0.0 collective-permute-done.2.refs_6_
  12.1 0.1 collective-permute-start.3
  12.1 1.2 %collective-permute-done.3.refs_4_ = bf16[128,256]{1,0:T(8,128)(2,1)S(1)} collective-permute-done((bf16[128,256]{1,0:T(8,128)(2,1)S(1)}, bf16[128,256]{1,0:T(8,128)(2,1)S(1)}, u32[]{:S(2)}, u32[]{:S(2)}) %collective-permute-start.3) | collective-permute-done | bytes 65568 | tf_op jit(solution)/shard_map/ppermute | solution.py:237
  13.3 0.0 collective-permute-done.6.refs_5_
  13.3 0.0 collective-permute-done.1.refs_1_
  13.3 0.5 %shard_map.102.refs_0_ = bf16[128,256]{1,0:T(8,128)(2,1)S(1)} custom-call(bf16[512,256]{1,0:T(8,128)(2,1)S(1)} %shard_map.97.refs_2_.refs_0_, bf16[512,256]{1,0:T(8,128)(2,1)S(1)} %collective-permute-done.1.refs_1_, bf16[128,256]{1,0:T(8,128)(2,1)S(1)} %get-tuple-element.13.after.refs_2_, bf16[128,256]{1,0:T(8,128)(2,1)S(1)} %get-tuple-element.14.refs_3_, ...), custom_call_target="tpu_custom_call" | custom-call | flops 134217728 | bytes 1114112 | tf_op jit(solution)/shard_map/pallas_call | solution.py:28
  13.8 2.5 %collective-permute-start.11 = (bf16[128,256]{1,0:T(8,128)(2,1)S(1)}, bf16[128,256]{1,0:T(8,128)(2,1)S(1)}, u32[]{:S(2)}, u32[]{:S(2)}) collective-permute-start(bf16[128,256]{1,0:T(8,128)(2,1)S(1)} %shard_map.102.refs_0_), channel_id=1, source_target_pairs={{0,24},{1,25},{2,26},{3,27},{4,7},{5,6},{6,5},{7,4},{8,16},{9,17},... | collective-permute-start | bytes 196616 | tf_op jit(solution)/shard_map/ppermute | solution.py:261
  16.3 0.5 %collective-permute-start.10 = (bf16[128,256]{1,0:T(8,128)(2,1)S(1)}, bf16[128,256]{1,0:T(8,128)(2,1)S(1)}, u32[]{:S(2)}, u32[]{:S(2)}) collective-permute-start(bf16[128,256]{1,0:T(8,128)(2,1)S(1)} %shard_map.102.refs_0_), channel_id=1, source_target_pairs={{0,8},{1,9},{2,10},{3,11},{4,6},{5,7},{6,4},{7,5},{8,0},{9,1},{10,... | collective-permute-start | bytes 196616 | tf_op jit(solution)/shard_map/ppermute | solution.py:261
  16.8 0.5 %collective-permute-start.9 = (bf16[128,256]{1,0:T(8,128)(2,1)S(1)}, bf16[128,256]{1,0:T(8,128)(2,1)S(1)}, u32[]{:S(2)}, u32[]{:S(2)}) collective-permute-start(bf16[128,256]{1,0:T(8,128)(2,1)S(1)} %shard_map.102.refs_0_), channel_id=1, source_target_pairs={{0,16},{1,17},{2,18},{3,19},{4,5},{5,4},{6,7},{7,6},{8,24},{9,25},... | collective-permute-start | bytes 196616 | tf_op jit(solution)/shard_map/ppermute | solution.py:261
  17.4 0.3 shard_map.99
  17.7 1.4 %collective-permute-start.7 = (bf16[128,256]{1,0:T(8,128)(2,1)S(1)}, bf16[128,256]{1,0:T(8,128)(2,1)S(1)}, u32[]{:S(2)}, u32[]{:S(2)}) collective-permute-start(bf16[128,256]{1,0:T(8,128)(2,1)S(1)} %get-tuple-element.16), channel_id=1, source_target_pairs={{0,12},{4,8},{8,4},{12,0},{16,28},{20,24},{24,20},{28,16},{1,13},{... | collective-permute-start | bytes 196616 | tf_op jit(solution)/shard_map/ppermute | solution.py:237
  19.1 0.0 collective-permute-done.11.refs_3_
  19.1 1.5 %collective-permute-done.10.refs_2_ = bf16[128,256]{1,0:T(8,128)(2,1)S(1)} collective-permute-done((bf16[128,256]{1,0:T(8,128)(2,1)S(1)}, bf16[128,256]{1,0:T(8,128)(2,1)S(1)}, u32[]{:S(2)}, u32[]{:S(2)}) %collective-permute-start.10) | collective-permute-done | bytes 65568 | tf_op jit(solution)/shard_map/ppermute | solution.py:261
  20.6 0.5 %collective-permute-done.9.refs_1_ = bf16[128,256]{1,0:T(8,128)(2,1)S(1)} collective-permute-done((bf16[128,256]{1,0:T(8,128)(2,1)S(1)}, bf16[128,256]{1,0:T(8,128)(2,1)S(1)}, u32[]{:S(2)}, u32[]{:S(2)}) %collective-permute-start.9) | collective-permute-done | bytes 65568 | tf_op jit(solution)/shard_map/ppermute | solution.py:261
  21.1 1.9 %collective-permute-start.15 = (bf16[128,256]{1,0:T(8,128)(2,1)S(1)}, bf16[128,256]{1,0:T(8,128)(2,1)S(1)}, u32[]{:S(2)}, u32[]{:S(2)}) collective-permute-start(bf16[128,256]{1,0:T(8,128)(2,1)S(1)} %shard_map.103), channel_id=1, source_target_pairs={{0,7},{1,6},{2,5},{3,4},{4,24},{5,25},{6,26},{7,27},{8,15},{9,14},... | collective-permute-start | bytes 196616 | tf_op jit(solution)/shard_map/ppermute | solution.py:248
  23.0 1.6 %collective-permute-start.14 = (bf16[128,256]{1,0:T(8,128)(2,1)S(1)}, bf16[128,256]{1,0:T(8,128)(2,1)S(1)}, u32[]{:S(2)}, u32[]{:S(2)}) collective-permute-start(bf16[128,256]{1,0:T(8,128)(2,1)S(1)} %shard_map.103), channel_id=1, source_target_pairs={{0,6},{1,7},{2,4},{3,5},{4,8},{5,9},{6,10},{7,11},{8,14},{9,15},{1... | collective-permute-start | bytes 196616 | tf_op jit(solution)/shard_map/ppermute | solution.py:248
  24.6 0.0 collective-permute-start.13
  24.6 0.7 %collective-permute-start.12 = (bf16[128,256]{1,0:T(8,128)(2,1)S(1)}, bf16[128,256]{1,0:T(8,128)(2,1)S(1)}, u32[]{:S(2)}, u32[]{:S(2)}) collective-permute-start(bf16[128,256]{1,0:T(8,128)(2,1)S(1)} %shard_map.103), channel_id=1, source_target_pairs={{0,4},{4,0},{8,12},{12,8},{16,20},{20,16},{24,28},{28,24},{1,5},{5... | collective-permute-start | bytes 196616 | tf_op jit(solution)/shard_map/ppermute | solution.py:237
  25.3 0.0 collective-permute-done.7.received
  25.3 0.0 copy-start.2
  25.3 1.1 %collective-permute-start.8 = (bf16[64,256]{1,0:T(8,128)(2,1)S(1)}, bf16[64,256]{1,0:T(8,128)(2,1)S(1)}, u32[]{:S(2)}, u32[]{:S(2)}) collective-permute-start(bf16[64,256]{1,0:T(8,128)(2,1)S(1)} %get-tuple-element.18), channel_id=1, source_target_pairs={{0,20},{4,16},{8,28},{12,24},{16,4},{20,0},{24,12},{28,8},{1,21},{... | collective-permute-start | bytes 98312 | tf_op jit(solution)/shard_map/ppermute | solution.py:237
  26.5 0.0 collective-permute-done.15.refs_3_
  26.5 0.2 collective-permute-done.14.refs_2_
  26.7 1.6 %collective-permute-done.13.refs_1_ = bf16[128,256]{1,0:T(8,128)(2,1)S(1)} collective-permute-done((bf16[128,256]{1,0:T(8,128)(2,1)S(1)}, bf16[128,256]{1,0:T(8,128)(2,1)S(1)}, u32[]{:S(2)}, u32[]{:S(2)}) %collective-permute-start.13) | collective-permute-done | bytes 65568 | tf_op jit(solution)/shard_map/ppermute | solution.py:248
  28.3 0.0 collective-permute-done.12.refs_0_
  28.4 0.3 %collective-permute-start.16 = (f32[128,256]{1,0:T(8,128)S(1)}, f32[128,256]{1,0:T(8,128)S(1)}, u32[]{:S(2)}, u32[]{:S(2)}) collective-permute-start(f32[128,256]{1,0:T(8,128)S(1)} %shard_map.104.own), channel_id=1, source_target_pairs={{0,4},{4,0},{8,12},{12,8},{16,20},{20,16},{24,28},{28,24},{1,5},{5... | collective-permute-start | bytes 393224 | tf_op jit(solution)/shard_map/ppermute | solution.py:237
  28.7 0.2 collective-permute-done.8.received
  28.9 0.0 copy-done.2
  28.9 0.8 %shard_map.101 = (f32[64,256]{1,0:T(8,128)}, f32[8,128]{1,0:T(8,128)S(1)}) custom-call(f32[64,256]{1,0:T(8,128)S(1)} %get-tuple-element.17.kept, bf16[64,256]{1,0:T(8,128)(2,1)S(1)} %collective-permute-done.8.received, f32[64,1]{1,0:T(8,128)S(1)} %get-tuple-element.19.scale, bf16[256,256]{1,0:T(8,128)(2,1)S(1)} %copy-done.2), custom_call_target="tpu_custom_call" | custom-call | flops 4000000000 | bytes 299264 | tf_op jit(solution)/shard_map/pallas_call | solution.py:28
  29.7 0.0 collective-permute-done.16.other
  29.8 0.7 %shard_map.105 = f32[256,256]{1,0:T(8,128)} custom-call(f32[8,128]{1,0:T(8,128)S(1)} %get-tuple-element.21.after, f32[128,256]{1,0:T(8,128)S(1)} %shard_map.104.own, f32[128,256]{1,0:T(8,128)S(1)} %collective-permute-done.16.other), custom_call_target="tpu_custom_call" | custom-call | bytes 528384 | tf_op jit(solution)/shard_map/pallas_call | solution.py:28
  (5 shorter events, 0.1 us)
Async XLA Ops:
  0.6 6.9 %copy-start = (bf16[1,1,6,128,128]{4,3,2,1,0:T(8,128)(2,1)S(1)}, bf16[1,1,6,128,128]{4,3,2,1,0:T(8,128)(2,1)}, u32[]{:S(2)}) copy-start(bf16[1,1,6,128,128]{4,3,2,1,0:T(8,128)(2,1)} %blocks.1) | copy-start | bytes 589828
  1.6 1.4 %collective-permute-start = (bf16[128,256]{1,0:T(8,128)(2,1)S(1)}, bf16[128,256]{1,0:T(8,128)(2,1)S(1)}, u32[]{:S(2)}, u32[]{:S(2)}) collective-permute-start(bf16[128,256]{1,0:T(8,128)(2,1)S(1)} %get-tuple-element.12.scaled), channel_id=1, source_target_pairs={{0,4},{4,0},{8,12},{12,8},{16,20},{20,16},{24,28},{28,24},{1,5},{5... | collective-permute-start | bytes 196616 | tf_op jit(solution)/shard_map/ppermute | solution.py:237
  3.1 4.5 %copy-start.1 = (s32[1,1,6]{2,1,0:T(1,128)S(1)}, s32[1,1,6]{2,1,0:T(1,128)}, u32[]{:S(2)}) copy-start(s32[1,1,6]{2,1,0:T(1,128)} %slots.1) | copy-start | bytes 76
  3.1 6.4 %collective-permute-start.5 = (bf16[128,256]{1,0:T(8,128)(2,1)S(1)}, bf16[128,256]{1,0:T(8,128)(2,1)S(1)}, u32[]{:S(2)}, u32[]{:S(2)}) collective-permute-start(bf16[128,256]{1,0:T(8,128)(2,1)S(1)} %get-tuple-element.13.after.refs_2_), channel_id=1, source_target_pairs={{0,24},{1,25},{2,26},{3,27},{4,7},{5,6},{6,5},{7,4},{8,16},{9,17},... | collective-permute-start | bytes 196616 | tf_op jit(solution)/shard_map/ppermute | solution.py:261
  6.9 4.3 %collective-permute-start.4 = (bf16[128,256]{1,0:T(8,128)(2,1)S(1)}, bf16[128,256]{1,0:T(8,128)(2,1)S(1)}, u32[]{:S(2)}, u32[]{:S(2)}) collective-permute-start(bf16[128,256]{1,0:T(8,128)(2,1)S(1)} %get-tuple-element.13.after.refs_2_), channel_id=1, source_target_pairs={{0,8},{1,9},{2,10},{3,11},{4,6},{5,7},{6,4},{7,5},{8,0},{9,1},{10,... | collective-permute-start | bytes 196616 | tf_op jit(solution)/shard_map/ppermute | solution.py:261
  7.5 4.6 %collective-permute-start.2 = (bf16[128,256]{1,0:T(8,128)(2,1)S(1)}, bf16[128,256]{1,0:T(8,128)(2,1)S(1)}, u32[]{:S(2)}, u32[]{:S(2)}) collective-permute-start(bf16[128,256]{1,0:T(8,128)(2,1)S(1)} %get-tuple-element.13.after.refs_2_), channel_id=1, source_target_pairs={{0,16},{1,17},{2,18},{3,19},{4,5},{5,4},{6,7},{7,6},{8,24},{9,25},... | collective-permute-start | bytes 196616 | tf_op jit(solution)/shard_map/ppermute | solution.py:261
  8.6 4.7 %collective-permute-start.1 = (bf16[512,256]{1,0:T(8,128)(2,1)S(1)}, bf16[512,256]{1,0:T(8,128)(2,1)S(1)}, u32[]{:S(2)}, u32[]{:S(2)}) collective-permute-start(bf16[512,256]{1,0:T(8,128)(2,1)S(1)} %shard_map.97.refs_2_.refs_0_), channel_id=1, source_target_pairs={{0,4},{4,0},{8,12},{12,8},{16,20},{20,16},{24,28},{28,24},{1,5},{5... | collective-permute-start | bytes 786440 | tf_op jit(solution)/shard_map/ppermute | solution.py:237
  11.2 2.1 %collective-permute-start.6 = (bf16[256,256]{1,0:T(8,128)(2,1)S(1)}, bf16[256,256]{1,0:T(8,128)(2,1)S(1)}, u32[]{:S(2)}, u32[]{:S(2)}) collective-permute-start(bf16[256,256]{1,0:T(8,128)(2,1)S(1)} %shard_map.98), channel_id=1, source_target_pairs={{0,4},{4,0},{8,12},{12,8},{16,20},{20,16},{24,28},{28,24},{1,5},{5... | collective-permute-start | bytes 393224 | tf_op jit(solution)/shard_map/ppermute | solution.py:237
  12.1 1.3 %collective-permute-start.3 = (bf16[128,256]{1,0:T(8,128)(2,1)S(1)}, bf16[128,256]{1,0:T(8,128)(2,1)S(1)}, u32[]{:S(2)}, u32[]{:S(2)}) collective-permute-start(bf16[128,256]{1,0:T(8,128)(2,1)S(1)} %collective-permute-done.2.refs_6_), channel_id=1, source_target_pairs={{0,4},{4,0},{8,12},{12,8},{16,20},{20,16},{24,28},{28,24},{1,5},{5... | collective-permute-start | bytes 196616 | tf_op jit(solution)/shard_map/ppermute | solution.py:237
  13.8 5.3 %collective-permute-start.11 = (bf16[128,256]{1,0:T(8,128)(2,1)S(1)}, bf16[128,256]{1,0:T(8,128)(2,1)S(1)}, u32[]{:S(2)}, u32[]{:S(2)}) collective-permute-start(bf16[128,256]{1,0:T(8,128)(2,1)S(1)} %shard_map.102.refs_0_), channel_id=1, source_target_pairs={{0,24},{1,25},{2,26},{3,27},{4,7},{5,6},{6,5},{7,4},{8,16},{9,17},... | collective-permute-start | bytes 196616 | tf_op jit(solution)/shard_map/ppermute | solution.py:261
  16.3 4.3 %collective-permute-start.10 = (bf16[128,256]{1,0:T(8,128)(2,1)S(1)}, bf16[128,256]{1,0:T(8,128)(2,1)S(1)}, u32[]{:S(2)}, u32[]{:S(2)}) collective-permute-start(bf16[128,256]{1,0:T(8,128)(2,1)S(1)} %shard_map.102.refs_0_), channel_id=1, source_target_pairs={{0,8},{1,9},{2,10},{3,11},{4,6},{5,7},{6,4},{7,5},{8,0},{9,1},{10,... | collective-permute-start | bytes 196616 | tf_op jit(solution)/shard_map/ppermute | solution.py:261
  16.8 4.3 %collective-permute-start.9 = (bf16[128,256]{1,0:T(8,128)(2,1)S(1)}, bf16[128,256]{1,0:T(8,128)(2,1)S(1)}, u32[]{:S(2)}, u32[]{:S(2)}) collective-permute-start(bf16[128,256]{1,0:T(8,128)(2,1)S(1)} %shard_map.102.refs_0_), channel_id=1, source_target_pairs={{0,16},{1,17},{2,18},{3,19},{4,5},{5,4},{6,7},{7,6},{8,24},{9,25},... | collective-permute-start | bytes 196616 | tf_op jit(solution)/shard_map/ppermute | solution.py:261
  17.7 7.6 %collective-permute-start.7 = (bf16[128,256]{1,0:T(8,128)(2,1)S(1)}, bf16[128,256]{1,0:T(8,128)(2,1)S(1)}, u32[]{:S(2)}, u32[]{:S(2)}) collective-permute-start(bf16[128,256]{1,0:T(8,128)(2,1)S(1)} %get-tuple-element.16), channel_id=1, source_target_pairs={{0,12},{4,8},{8,4},{12,0},{16,28},{20,24},{24,20},{28,16},{1,13},{... | collective-permute-start | bytes 196616 | tf_op jit(solution)/shard_map/ppermute | solution.py:237
  21.1 5.3 %collective-permute-start.15 = (bf16[128,256]{1,0:T(8,128)(2,1)S(1)}, bf16[128,256]{1,0:T(8,128)(2,1)S(1)}, u32[]{:S(2)}, u32[]{:S(2)}) collective-permute-start(bf16[128,256]{1,0:T(8,128)(2,1)S(1)} %shard_map.103), channel_id=1, source_target_pairs={{0,7},{1,6},{2,5},{3,4},{4,24},{5,25},{6,26},{7,27},{8,15},{9,14},... | collective-permute-start | bytes 196616 | tf_op jit(solution)/shard_map/ppermute | solution.py:248
  23.0 3.7 %collective-permute-start.14 = (bf16[128,256]{1,0:T(8,128)(2,1)S(1)}, bf16[128,256]{1,0:T(8,128)(2,1)S(1)}, u32[]{:S(2)}, u32[]{:S(2)}) collective-permute-start(bf16[128,256]{1,0:T(8,128)(2,1)S(1)} %shard_map.103), channel_id=1, source_target_pairs={{0,6},{1,7},{2,4},{3,5},{4,8},{5,9},{6,10},{7,11},{8,14},{9,15},{1... | collective-permute-start | bytes 196616 | tf_op jit(solution)/shard_map/ppermute | solution.py:248
  24.6 3.7 %collective-permute-start.13 = (bf16[128,256]{1,0:T(8,128)(2,1)S(1)}, bf16[128,256]{1,0:T(8,128)(2,1)S(1)}, u32[]{:S(2)}, u32[]{:S(2)}) collective-permute-start(bf16[128,256]{1,0:T(8,128)(2,1)S(1)} %shard_map.103), channel_id=1, source_target_pairs={{0,5},{1,4},{2,7},{3,6},{4,16},{5,17},{6,18},{7,19},{8,13},{9,12},... | collective-permute-start | bytes 196616 | tf_op jit(solution)/shard_map/ppermute | solution.py:248
  24.6 3.7 %collective-permute-start.12 = (bf16[128,256]{1,0:T(8,128)(2,1)S(1)}, bf16[128,256]{1,0:T(8,128)(2,1)S(1)}, u32[]{:S(2)}, u32[]{:S(2)}) collective-permute-start(bf16[128,256]{1,0:T(8,128)(2,1)S(1)} %shard_map.103), channel_id=1, source_target_pairs={{0,4},{4,0},{8,12},{12,8},{16,20},{20,16},{24,28},{28,24},{1,5},{5... | collective-permute-start | bytes 196616 | tf_op jit(solution)/shard_map/ppermute | solution.py:237
  25.3 3.6 %copy-start.2 = (bf16[256,256]{1,0:T(8,128)(2,1)S(1)}, bf16[256,256]{1,0:T(8,128)(2,1)}, u32[]{:S(2)}) copy-start(bf16[256,256]{1,0:T(8,128)(2,1)} %weight.1) | copy-start | bytes 393220
  25.3 3.6 %collective-permute-start.8 = (bf16[64,256]{1,0:T(8,128)(2,1)S(1)}, bf16[64,256]{1,0:T(8,128)(2,1)S(1)}, u32[]{:S(2)}, u32[]{:S(2)}) collective-permute-start(bf16[64,256]{1,0:T(8,128)(2,1)S(1)} %get-tuple-element.18), channel_id=1, source_target_pairs={{0,20},{4,16},{8,28},{12,24},{16,4},{20,0},{24,12},{28,8},{1,21},{... | collective-permute-start | bytes 98312 | tf_op jit(solution)/shard_map/ppermute | solution.py:237
  28.4 1.4 %collective-permute-start.16 = (f32[128,256]{1,0:T(8,128)S(1)}, f32[128,256]{1,0:T(8,128)S(1)}, u32[]{:S(2)}, u32[]{:S(2)}) collective-permute-start(f32[128,256]{1,0:T(8,128)S(1)} %shard_map.104.own), channel_id=1, source_target_pairs={{0,4},{4,0},{8,12},{12,8},{16,20},{20,16},{24,28},{28,24},{1,5},{5... | collective-permute-start | bytes 393224 | tf_op jit(solution)/shard_map/ppermute | solution.py:237

commit v9 on v8

--- a/solution.py
+++ b/solution.py
@@ -99,10 +99,9 @@
 
 
 def gathered(nodes, cols, refs):
-    pair, pair_left, near, far = refs[:4]
-    rows = CORES * nodes
-    first = [pair] + list(refs[4 : 3 + cols])
-    second = [pair_left, near] + [far.at[n * rows : (n + 1) * rows] for n in range(cols - 2)]
+    pair, pair_left = refs[:2]
+    first = [pair] + list(refs[1 + cols : 2 * cols])
+    second = [pair_left] + list(refs[2 : 1 + cols])
     core = positions()[1]
     grads = [jnp.where(core == 1, f[...], s[...]) for f, s in zip(first, second)]
     by_core = [
@@ -114,26 +113,45 @@
     return first, second, mine, theirs
 
 
+def half_features(core, received, brought, half):
+    return jnp.where(core == 1, brought[:, :half], received[:, half:])
+
+
+def look_ahead(nodes, chips, cols, refs):
+    own, other, pair, pair_left = refs[:4]
+    far, moved, outs = refs[4 : 2 + cols], refs[2 + cols : 2 * cols], refs[-2:]
+    rows = CORES * nodes
+    core = positions()[1]
+    half = outs[0].shape[0]
+    feats = {turned(0): half_features(core, pair, pair_left, half)}
+    for n, (piece, brought) in enumerate(zip(moved, far)):
+        feats[turned(n + 2)] = half_features(core, piece, brought, half)
+    order = sorted(feats)
+    features = jnp.concatenate([feats[k] for k in order], axis=0)
+    for tile, out in zip((own, other), outs):
+        tiles = jnp.concatenate([tile[k * rows : (k + 1) * rows] for k in order], axis=0)
+        out[...] = lax.dot_general(
+            features, tiles, (((0,), (0,)), ((), ())), preferred_element_type=jnp.float32
+        )
+
+
 def weigh(nodes, chips, cols, refs):
     own, other = refs[:2]
-    leave = refs[-1]
+    near, piece = refs[4], refs[3 + cols]
+    aheads, leave = refs[-3:-1], refs[-1]
     half = leave.shape[0]
-    first, second, mine, theirs = gathered(nodes, cols, refs[2:])
-    core = positions()[1]
-    feats = [
-        jnp.where(core == 1, s[:, :half], f[:, half:]) for f, s in zip(first, second)
-    ]
-    features = jnp.concatenate([feats[turned(k)] for k in range(chips)], axis=0)
-    first_rows = (((0,), (0,)), ((), ()))
+    _, _, mine, theirs = gathered(nodes, cols, refs[2:-3])
+    features = half_features(positions()[1], piece, near, half)
+    rows = pl.ds(turned(1) * CORES * nodes, CORES * nodes)
     part = jnp.zeros(leave.shape, jnp.float32)
-    for tile, rows in ((own, mine), (other, theirs)):
-        ahead = lax.dot_general(
-            features, tile[...], first_rows, preferred_element_type=jnp.float32
-        )
-        high = ahead.astype(jnp.bfloat16)
-        low = (ahead - high.astype(jnp.float32)).astype(jnp.bfloat16)
+    for tile, ahead, grads in ((own, aheads[0], mine), (other, aheads[1], theirs)):
+        full = ahead[...] + lax.dot_general(
+            features, tile[rows], (((0,), (0,)), ((), ())), preferred_element_type=jnp.float32
+        )
+        high = full.astype(jnp.bfloat16)
+        low = (full - high.astype(jnp.float32)).astype(jnp.bfloat16)
         both = jnp.concatenate([high, low], axis=0)
-        both = jnp.dot(both, rows, preferred_element_type=jnp.float32)
+        both = jnp.dot(both, grads, preferred_element_type=jnp.float32)
         part = part + both[:half] + both[half:]
     leave[...] = part.astype(jnp.bfloat16)
 
@@ -162,10 +180,9 @@
 
 
 def pack(*refs):
-    out = refs[-1]
-    rows = refs[0].shape[0]
-    for n, r in enumerate(refs[:-2]):
-        out[n * rows : (n + 1) * rows] = r[...]
+    count = len(refs) // 2
+    for piece, out in zip(refs[:count], refs[count + 1 :]):
+        out[...] = piece[...]
 
 
 def halving(n):
@@ -289,17 +306,25 @@
         [VMEM, SMEM, SMEM, VMEM],
         limit=8 * 2**20 + 3 * size,
     )
-    (packed,) = call(
-        pack, [shape(((cols - 2) * CORES * nodes, width), bf16)], moved[1:] + [dense], flops=HEAVY
-    )
-    brought = [partner(moved[0]), partner(packed)]
-    operands = [dense, partner(dense), pair, pair_left] + brought + moved
+    packed = call(
+        pack, [shape((CORES * nodes, width), bf16)] * (cols - 2), moved[1:] + [dense], flops=HEAVY
+    )
+    brought = [partner(moved[0])] + [partner(x) for x in packed]
+    their_dense = partner(dense)
+    operands = [dense, their_dense, pair, pair_left] + brought + moved
+    aheads = call(
+        lambda *refs: look_ahead(nodes, chips, cols, refs),
+        [shape((half, sources), f32)] * 2,
+        [dense, their_dense, pair, pair_left, *brought[1:]] + moved[1:],
+        limit=8 * 2**20 + 4 * size,
+        flops=4 * targets * sources * half,
+    )
     (leave,) = call(
         lambda *refs: weigh(nodes, chips, cols, refs),
         [shape((half, width), bf16)],
-        operands,
+        operands + list(aheads),
         limit=8 * 2**20 + 4 * size,
-        flops=4 * targets * sources * half + 8 * sources * half * width,
+        flops=8 * sources * half * width,
     )
     kept, leaving = call(
         lambda *refs: pull(nodes, chips, cols, refs),

time: 30.6 us -> 30.7 us (level)
  starting transfers between devices: 17.4 us -> 17.9 us
    ppermute x8 -> x9, starting transfers between devices: 5.84 us -> 6.63 us  [swap(): return lax.ppermute(x, 'row', [(d, d ^ k) for d in range(rows)])]
    ppermute x8 -> x9, waiting for transfers between devices: 1.65 us -> 1.14 us  [swap(): return lax.ppermute(x, 'row', [(d, d ^ k) for d in range(rows)])]
    pallas_call x11 -> x12, Pallas kernels: 4.44 us -> 4.23 us  [call(): pl.pallas_call(body, out_shape=outs, in_specs=[pl.BlockSpec(memory_space=...]
  transfers between devices with their start and end apart: 17 -> 18, of which waited for: 8 -> 10; matrix products, arithmetic and copies ran while one was open for 0% -> 0% of each run, Pallas kernels for 7% -> 7%
where the time goes in v9:
time: 30.7 us; the launch traced here: 30.6 us
  starting transfers between devices  17.9 us (58%)
  waiting for transfers between devices  7.06 us (23%)
  Pallas kernels  4.23 us (14%)
  between operations  1.39 us (5%)
    ppermute x6, starting transfers between devices, along(): out.append(lax.ppermute(x, ('row', 'col'), pairs))  8.06 us
    ppermute x9, starting transfers between devices, swap(): return lax.ppermute(x, 'row', [(d, d ^ k) for d in range(rows)])  6.63 us
    pallas_call x12, Pallas kernels, call(): pl.pallas_call(body, out_shape=outs, in_specs=[pl.BlockSpec(memory_space=...  4.23 us
    ppermute x6, waiting for transfers between devices, along(): out.append(lax.ppermute(x, ('row', 'col'), pairs))  4.07 us
    ppermute x3, starting transfers between devices, cross(): return lax.ppermute(x, ('row', 'col'), pairs)  3.19 us
    ppermute x3, waiting for transfers between devices, cross(): return lax.ppermute(x, ('row', 'col'), pairs)  1.84 us
    ppermute x9, waiting for transfers between devices, swap(): return lax.ppermute(x, 'row', [(d, d ^ k) for d in range(rows)])  1.14 us
  transfers between devices with their start and end apart: 18, of which 10 were waited for; matrix products, arithmetic and copies ran while one was open for 0% of the time, Pallas kernels for 7%

profile of v9, /device:TPU:0, one launch (start us, length us, event | category | flops | bytes accessed | tf_op | source)
XLA Modules:
  0.0 30.6 jit_solution(16138622150530493494)
XLA Ops:
  0.6 0.0 copy-start
  0.6 1.0 %shard_map.95 = (bf16[128,256]{1,0:T(8,128)(2,1)S(1)}, f32[64,1]{1,0:T(8,128)S(1)}) custom-call(bf16[64,256]{1,0:T(8,128)(2,1)} %features.1, bf16[64,256]{1,0:T(8,128)(2,1)} %grad_out.1, s32[64,256]{1,0:T(8,128)} %relu_mask.1, s32[1,64]{1,0:T(1,128)} %bitcast.1), custom_call_target="tpu_custom_call" | custom-call | bytes 197120 | tf_op jit(solution)/shard_map/pallas_call | solution.py:28
  1.6 0.5 %collective-permute-start = (bf16[128,256]{1,0:T(8,128)(2,1)S(1)}, bf16[128,256]{1,0:T(8,128)(2,1)S(1)}, u32[]{:S(2)}, u32[]{:S(2)}) collective-permute-start(bf16[128,256]{1,0:T(8,128)(2,1)S(1)} %get-tuple-element.16.scaled), channel_id=1, source_target_pairs={{0,4},{4,0},{8,12},{12,8},{16,20},{20,16},{24,28},{28,24},{1,5},{5... | collective-permute-start | bytes 196616 | tf_op jit(solution)/shard_map/ppermute | solution.py:254
  2.8 0.3 collective-permute-done.other
  3.1 0.0 copy-start.1
  3.1 3.9 %collective-permute-start.5 = (bf16[128,256]{1,0:T(8,128)(2,1)S(1)}, bf16[128,256]{1,0:T(8,128)(2,1)S(1)}, u32[]{:S(2)}, u32[]{:S(2)}) collective-permute-start(bf16[128,256]{1,0:T(8,128)(2,1)S(1)} %get-tuple-element.17.after.refs_2_), channel_id=1, source_target_pairs={{0,24},{1,25},{2,26},{3,27},{4,7},{5,6},{6,5},{7,4},{8,16},{9,17},... | collective-permute-start | bytes 196616 | tf_op jit(solution)/shard_map/ppermute | solution.py:278
  6.9 0.5 %collective-permute-start.4 = (bf16[128,256]{1,0:T(8,128)(2,1)S(1)}, bf16[128,256]{1,0:T(8,128)(2,1)S(1)}, u32[]{:S(2)}, u32[]{:S(2)}) collective-permute-start(bf16[128,256]{1,0:T(8,128)(2,1)S(1)} %get-tuple-element.17.after.refs_2_), channel_id=1, source_target_pairs={{0,8},{1,9},{2,10},{3,11},{4,6},{5,7},{6,4},{7,5},{8,0},{9,1},{10,... | collective-permute-start | bytes 196616 | tf_op jit(solution)/shard_map/ppermute | solution.py:278
  7.5 0.1 collective-permute-start.2
  7.6 0.0 copy-done
  7.6 0.0 copy-done.1
  7.6 0.6 %shard_map.97.refs_2_.refs_0_ = bf16[512,256]{1,0:T(8,128)(2,1)S(1)} custom-call(bf16[1,1,6,128,128]{4,3,2,1,0:T(8,128)(2,1)S(1)} %copy-done, s32[1,1,6]{2,1,0:T(1,128)S(1)} %copy-done.1, s32[1,1]{1,0:T(1,128)S(6)} %copy.10.count, bf16[128,256]{1,0:T(8,128)(2,1)S(1)} %get-tuple-element.17.after.refs_2_), custom_call_target="tpu_custom_call" | custom-call | bytes 524316 | tf_op jit(solution)/shard_map/pallas_call | solution.py:28
  8.2 0.9 %collective-permute-start.1 = (bf16[512,256]{1,0:T(8,128)(2,1)S(1)}, bf16[512,256]{1,0:T(8,128)(2,1)S(1)}, u32[]{:S(2)}, u32[]{:S(2)}) collective-permute-start(bf16[512,256]{1,0:T(8,128)(2,1)S(1)} %shard_map.97.refs_2_.refs_0_), channel_id=1, source_target_pairs={{0,4},{4,0},{8,12},{12,8},{16,20},{20,16},{24,28},{28,24},{1,5},{5... | collective-permute-start | bytes 786440 | tf_op jit(solution)/shard_map/ppermute | solution.py:254
  9.1 0.1 collective-permute-done.5.refs_1_.refs_9_.refs_7_
  9.2 2.0 %collective-permute-done.4.refs_0_.refs_8_.refs_6_ = bf16[128,256]{1,0:T(8,128)(2,1)S(1)} collective-permute-done((bf16[128,256]{1,0:T(8,128)(2,1)S(1)}, bf16[128,256]{1,0:T(8,128)(2,1)S(1)}, u32[]{:S(2)}, u32[]{:S(2)}) %collective-permute-start.4) | collective-permute-done | bytes 65568 | tf_op jit(solution)/shard_map/ppermute | solution.py:278
  11.2 0.8 %collective-permute-start.6 = (bf16[128,256]{1,0:T(8,128)(2,1)S(1)}, bf16[128,256]{1,0:T(8,128)(2,1)S(1)}, u32[]{:S(2)}, u32[]{:S(2)}) collective-permute-start(bf16[128,256]{1,0:T(8,128)(2,1)S(1)} %get-tuple-element.19), channel_id=1, source_target_pairs={{0,4},{4,0},{8,12},{12,8},{16,20},{20,16},{24,28},{28,24},{1,5},{5... | collective-permute-start | bytes 196616 | tf_op jit(solution)/shard_map/ppermute | solution.py:254
  12.1 0.1 collective-permute-start.7
  12.1 0.0 collective-permute-done.2.refs_7_
  12.1 0.4 %collective-permute-start.3 = (bf16[128,256]{1,0:T(8,128)(2,1)S(1)}, bf16[128,256]{1,0:T(8,128)(2,1)S(1)}, u32[]{:S(2)}, u32[]{:S(2)}) collective-permute-start(bf16[128,256]{1,0:T(8,128)(2,1)S(1)} %collective-permute-done.2.refs_7_), channel_id=1, source_target_pairs={{0,4},{4,0},{8,12},{12,8},{16,20},{20,16},{24,28},{28,24},{1,5},{5... | collective-permute-start | bytes 196616 | tf_op jit(solution)/shard_map/ppermute | solution.py:254
  12.6 0.4 %collective-permute-done.6.refs_5_.refs_4_ = bf16[128,256]{1,0:T(8,128)(2,1)S(1)} collective-permute-done((bf16[128,256]{1,0:T(8,128)(2,1)S(1)}, bf16[128,256]{1,0:T(8,128)(2,1)S(1)}, u32[]{:S(2)}, u32[]{:S(2)}) %collective-permute-start.6) | collective-permute-done | bytes 65568 | tf_op jit(solution)/shard_map/ppermute | solution.py:254
  13.0 0.4 %collective-permute-done.7.refs_6_.refs_5_ = bf16[128,256]{1,0:T(8,128)(2,1)S(1)} collective-permute-done((bf16[128,256]{1,0:T(8,128)(2,1)S(1)}, bf16[128,256]{1,0:T(8,128)(2,1)S(1)}, u32[]{:S(2)}, u32[]{:S(2)}) %collective-permute-start.7) | collective-permute-done | bytes 65568 | tf_op jit(solution)/shard_map/ppermute | solution.py:254
  13.3 0.0 collective-permute-done.1.refs_1_
  13.3 0.3 shard_map.102
  13.6 0.0 collective-permute-done.3.refs_4_
  13.6 0.4 %shard_map.103.refs_0_ = bf16[128,256]{1,0:T(8,128)(2,1)S(1)} custom-call(bf16[512,256]{1,0:T(8,128)(2,1)S(1)} %shard_map.97.refs_2_.refs_0_, bf16[512,256]{1,0:T(8,128)(2,1)S(1)} %collective-permute-done.1.refs_1_, bf16[128,256]{1,0:T(8,128)(2,1)S(1)} %get-tuple-element.17.after.refs_2_, bf16[128,256]{1,0:T(8,128)(2,1)S(1)} %get-tuple-element.18.refs_3_, ...), custom_call_target="tpu_custom_call" | custom-call | flops 67108864 | bytes 1376256 | tf_op jit(solution)/shard_map/pallas_call | solution.py:28
  14.0 2.5 %collective-permute-start.12 = (bf16[128,256]{1,0:T(8,128)(2,1)S(1)}, bf16[128,256]{1,0:T(8,128)(2,1)S(1)}, u32[]{:S(2)}, u32[]{:S(2)}) collective-permute-start(bf16[128,256]{1,0:T(8,128)(2,1)S(1)} %shard_map.103.refs_0_), channel_id=1, source_target_pairs={{0,24},{1,25},{2,26},{3,27},{4,7},{5,6},{6,5},{7,4},{8,16},{9,17},... | collective-permute-start | bytes 196616 | tf_op jit(solution)/shard_map/ppermute | solution.py:278
  16.5 0.5 %collective-permute-start.11 = (bf16[128,256]{1,0:T(8,128)(2,1)S(1)}, bf16[128,256]{1,0:T(8,128)(2,1)S(1)}, u32[]{:S(2)}, u32[]{:S(2)}) collective-permute-start(bf16[128,256]{1,0:T(8,128)(2,1)S(1)} %shard_map.103.refs_0_), channel_id=1, source_target_pairs={{0,8},{1,9},{2,10},{3,11},{4,6},{5,7},{6,4},{7,5},{8,0},{9,1},{10,... | collective-permute-start | bytes 196616 | tf_op jit(solution)/shard_map/ppermute | solution.py:278
  17.1 0.5 %collective-permute-start.10 = (bf16[128,256]{1,0:T(8,128)(2,1)S(1)}, bf16[128,256]{1,0:T(8,128)(2,1)S(1)}, u32[]{:S(2)}, u32[]{:S(2)}) collective-permute-start(bf16[128,256]{1,0:T(8,128)(2,1)S(1)} %shard_map.103.refs_0_), channel_id=1, source_target_pairs={{0,16},{1,17},{2,18},{3,19},{4,5},{5,4},{6,7},{7,6},{8,24},{9,25},... | collective-permute-start | bytes 196616 | tf_op jit(solution)/shard_map/ppermute | solution.py:278
  17.6 0.3 shard_map.99
  17.9 1.5 %collective-permute-start.8 = (bf16[128,256]{1,0:T(8,128)(2,1)S(1)}, bf16[128,256]{1,0:T(8,128)(2,1)S(1)}, u32[]{:S(2)}, u32[]{:S(2)}) collective-permute-start(bf16[128,256]{1,0:T(8,128)(2,1)S(1)} %get-tuple-element.22), channel_id=1, source_target_pairs={{0,12},{4,8},{8,4},{12,0},{16,28},{20,24},{24,20},{28,16},{1,13},{... | collective-permute-start | bytes 196616 | tf_op jit(solution)/shard_map/ppermute | solution.py:254
  19.3 0.0 collective-permute-done.12.refs_3_
  19.3 1.5 %collective-permute-done.11.refs_2_ = bf16[128,256]{1,0:T(8,128)(2,1)S(1)} collective-permute-done((bf16[128,256]{1,0:T(8,128)(2,1)S(1)}, bf16[128,256]{1,0:T(8,128)(2,1)S(1)}, u32[]{:S(2)}, u32[]{:S(2)}) %collective-permute-start.11) | collective-permute-done | bytes 65568 | tf_op jit(solution)/shard_map/ppermute | solution.py:278
  20.8 0.5 %collective-permute-done.10.refs_1_ = bf16[128,256]{1,0:T(8,128)(2,1)S(1)} collective-permute-done((bf16[128,256]{1,0:T(8,128)(2,1)S(1)}, bf16[128,256]{1,0:T(8,128)(2,1)S(1)}, u32[]{:S(2)}, u32[]{:S(2)}) %collective-permute-start.10) | collective-permute-done | bytes 65568 | tf_op jit(solution)/shard_map/ppermute | solution.py:278
  21.4 1.7 %collective-permute-start.16 = (bf16[128,256]{1,0:T(8,128)(2,1)S(1)}, bf16[128,256]{1,0:T(8,128)(2,1)S(1)}, u32[]{:S(2)}, u32[]{:S(2)}) collective-permute-start(bf16[128,256]{1,0:T(8,128)(2,1)S(1)} %shard_map.104), channel_id=1, source_target_pairs={{0,7},{1,6},{2,5},{3,4},{4,24},{5,25},{6,26},{7,27},{8,15},{9,14},... | collective-permute-start | bytes 196616 | tf_op jit(solution)/shard_map/ppermute | solution.py:265
  23.1 1.4 %collective-permute-start.15 = (bf16[128,256]{1,0:T(8,128)(2,1)S(1)}, bf16[128,256]{1,0:T(8,128)(2,1)S(1)}, u32[]{:S(2)}, u32[]{:S(2)}) collective-permute-start(bf16[128,256]{1,0:T(8,128)(2,1)S(1)} %shard_map.104), channel_id=1, source_target_pairs={{0,6},{1,7},{2,4},{3,5},{4,8},{5,9},{6,10},{7,11},{8,14},{9,15},{1... | collective-permute-start | bytes 196616 | tf_op jit(solution)/shard_map/ppermute | solution.py:265
  24.5 0.0 collective-permute-start.14
  24.5 0.7 %collective-permute-start.13 = (bf16[128,256]{1,0:T(8,128)(2,1)S(1)}, bf16[128,256]{1,0:T(8,128)(2,1)S(1)}, u32[]{:S(2)}, u32[]{:S(2)}) collective-permute-start(bf16[128,256]{1,0:T(8,128)(2,1)S(1)} %shard_map.104), channel_id=1, source_target_pairs={{0,4},{4,0},{8,12},{12,8},{16,20},{20,16},{24,28},{28,24},{1,5},{5... | collective-permute-start | bytes 196616 | tf_op jit(solution)/shard_map/ppermute | solution.py:254
  25.2 0.0 collective-permute-done.8.received
  25.3 0.0 copy-start.2
  25.3 1.1 %collective-permute-start.9 = (bf16[64,256]{1,0:T(8,128)(2,1)S(1)}, bf16[64,256]{1,0:T(8,128)(2,1)S(1)}, u32[]{:S(2)}, u32[]{:S(2)}) collective-permute-start(bf16[64,256]{1,0:T(8,128)(2,1)S(1)} %get-tuple-element.24), channel_id=1, source_target_pairs={{0,20},{4,16},{8,28},{12,24},{16,4},{20,0},{24,12},{28,8},{1,21},{... | collective-permute-start | bytes 98312 | tf_op jit(solution)/shard_map/ppermute | solution.py:254
  26.4 0.0 collective-permute-done.16.refs_3_
  26.4 0.4 %collective-permute-done.15.refs_2_ = bf16[128,256]{1,0:T(8,128)(2,1)S(1)} collective-permute-done((bf16[128,256]{1,0:T(8,128)(2,1)S(1)}, bf16[128,256]{1,0:T(8,128)(2,1)S(1)}, u32[]{:S(2)}, u32[]{:S(2)}) %collective-permute-start.15) | collective-permute-done | bytes 65568 | tf_op jit(solution)/shard_map/ppermute | solution.py:265
  26.8 1.4 %collective-permute-done.14.refs_1_ = bf16[128,256]{1,0:T(8,128)(2,1)S(1)} collective-permute-done((bf16[128,256]{1,0:T(8,128)(2,1)S(1)}, bf16[128,256]{1,0:T(8,128)(2,1)S(1)}, u32[]{:S(2)}, u32[]{:S(2)}) %collective-permute-start.14) | collective-permute-done | bytes 65568 | tf_op jit(solution)/shard_map/ppermute | solution.py:265
  28.2 0.0 collective-permute-done.13.refs_0_
  28.3 0.6 %collective-permute-start.17 = (f32[128,256]{1,0:T(8,128)S(1)}, f32[128,256]{1,0:T(8,128)S(1)}, u32[]{:S(2)}, u32[]{:S(2)}) collective-permute-start(f32[128,256]{1,0:T(8,128)S(1)} %shard_map.105.own), channel_id=1, source_target_pairs={{0,4},{4,0},{8,12},{12,8},{16,20},{20,16},{24,28},{28,24},{1,5},{5... | collective-permute-start | bytes 393224 | tf_op jit(solution)/shard_map/ppermute | solution.py:254
  28.9 0.0 collective-permute-done.9.received
  28.9 0.8 %shard_map.101 = (f32[64,256]{1,0:T(8,128)}, f32[8,128]{1,0:T(8,128)S(1)}) custom-call(f32[64,256]{1,0:T(8,128)S(1)} %get-tuple-element.23.kept, bf16[64,256]{1,0:T(8,128)(2,1)S(1)} %collective-permute-done.9.received, f32[64,1]{1,0:T(8,128)S(1)} %get-tuple-element.25.scale, bf16[256,256]{1,0:T(8,128)(2,1)S(1)} %copy-done.2), custom_call_target="tpu_custom_call" | custom-call | flops 4000000000 | bytes 299264 | tf_op jit(solution)/shard_map/pallas_call | solution.py:28
  29.7 0.1 collective-permute-done.17.other
  29.9 0.7 %shard_map.106 = f32[256,256]{1,0:T(8,128)} custom-call(f32[8,128]{1,0:T(8,128)S(1)} %get-tuple-element.27.after, f32[128,256]{1,0:T(8,128)S(1)} %shard_map.105.own, f32[128,256]{1,0:T(8,128)S(1)} %collective-permute-done.17.other), custom_call_target="tpu_custom_call" | custom-call | bytes 528384 | tf_op jit(solution)/shard_map/pallas_call | solution.py:28
  (6 shorter events, 0.1 us)
Async XLA Ops:
  0.6 6.9 %copy-start = (bf16[1,1,6,128,128]{4,3,2,1,0:T(8,128)(2,1)S(1)}, bf16[1,1,6,128,128]{4,3,2,1,0:T(8,128)(2,1)}, u32[]{:S(2)}) copy-start(bf16[1,1,6,128,128]{4,3,2,1,0:T(8,128)(2,1)} %blocks.1) | copy-start | bytes 589828
  1.6 1.4 %collective-permute-start = (bf16[128,256]{1,0:T(8,128)(2,1)S(1)}, bf16[128,256]{1,0:T(8,128)(2,1)S(1)}, u32[]{:S(2)}, u32[]{:S(2)}) collective-permute-start(bf16[128,256]{1,0:T(8,128)(2,1)S(1)} %get-tuple-element.16.scaled), channel_id=1, source_target_pairs={{0,4},{4,0},{8,12},{12,8},{16,20},{20,16},{24,28},{28,24},{1,5},{5... | collective-permute-start | bytes 196616 | tf_op jit(solution)/shard_map/ppermute | solution.py:254
  3.1 4.5 %copy-start.1 = (s32[1,1,6]{2,1,0:T(1,128)S(1)}, s32[1,1,6]{2,1,0:T(1,128)}, u32[]{:S(2)}) copy-start(s32[1,1,6]{2,1,0:T(1,128)} %slots.1) | copy-start | bytes 76
  3.1 6.1 %collective-permute-start.5 = (bf16[128,256]{1,0:T(8,128)(2,1)S(1)}, bf16[128,256]{1,0:T(8,128)(2,1)S(1)}, u32[]{:S(2)}, u32[]{:S(2)}) collective-permute-start(bf16[128,256]{1,0:T(8,128)(2,1)S(1)} %get-tuple-element.17.after.refs_2_), channel_id=1, source_target_pairs={{0,24},{1,25},{2,26},{3,27},{4,7},{5,6},{6,5},{7,4},{8,16},{9,17},... | collective-permute-start | bytes 196616 | tf_op jit(solution)/shard_map/ppermute | solution.py:278
  6.9 4.3 %collective-permute-start.4 = (bf16[128,256]{1,0:T(8,128)(2,1)S(1)}, bf16[128,256]{1,0:T(8,128)(2,1)S(1)}, u32[]{:S(2)}, u32[]{:S(2)}) collective-permute-start(bf16[128,256]{1,0:T(8,128)(2,1)S(1)} %get-tuple-element.17.after.refs_2_), channel_id=1, source_target_pairs={{0,8},{1,9},{2,10},{3,11},{4,6},{5,7},{6,4},{7,5},{8,0},{9,1},{10,... | collective-permute-start | bytes 196616 | tf_op jit(solution)/shard_map/ppermute | solution.py:278
  7.5 4.7 %collective-permute-start.2 = (bf16[128,256]{1,0:T(8,128)(2,1)S(1)}, bf16[128,256]{1,0:T(8,128)(2,1)S(1)}, u32[]{:S(2)}, u32[]{:S(2)}) collective-permute-start(bf16[128,256]{1,0:T(8,128)(2,1)S(1)} %get-tuple-element.17.after.refs_2_), channel_id=1, source_target_pairs={{0,16},{1,17},{2,18},{3,19},{4,5},{5,4},{6,7},{7,6},{8,24},{9,25},... | collective-permute-start | bytes 196616 | tf_op jit(solution)/shard_map/ppermute | solution.py:278
  8.2 5.1 %collective-permute-start.1 = (bf16[512,256]{1,0:T(8,128)(2,1)S(1)}, bf16[512,256]{1,0:T(8,128)(2,1)S(1)}, u32[]{:S(2)}, u32[]{:S(2)}) collective-permute-start(bf16[512,256]{1,0:T(8,128)(2,1)S(1)} %shard_map.97.refs_2_.refs_0_), channel_id=1, source_target_pairs={{0,4},{4,0},{8,12},{12,8},{16,20},{20,16},{24,28},{28,24},{1,5},{5... | collective-permute-start | bytes 786440 | tf_op jit(solution)/shard_map/ppermute | solution.py:254
  11.2 1.7 %collective-permute-start.6 = (bf16[128,256]{1,0:T(8,128)(2,1)S(1)}, bf16[128,256]{1,0:T(8,128)(2,1)S(1)}, u32[]{:S(2)}, u32[]{:S(2)}) collective-permute-start(bf16[128,256]{1,0:T(8,128)(2,1)S(1)} %get-tuple-element.19), channel_id=1, source_target_pairs={{0,4},{4,0},{8,12},{12,8},{16,20},{20,16},{24,28},{28,24},{1,5},{5... | collective-permute-start | bytes 196616 | tf_op jit(solution)/shard_map/ppermute | solution.py:254
  12.1 1.3 %collective-permute-start.7 = (bf16[128,256]{1,0:T(8,128)(2,1)S(1)}, bf16[128,256]{1,0:T(8,128)(2,1)S(1)}, u32[]{:S(2)}, u32[]{:S(2)}) collective-permute-start(bf16[128,256]{1,0:T(8,128)(2,1)S(1)} %get-tuple-element.20), channel_id=1, source_target_pairs={{0,4},{4,0},{8,12},{12,8},{16,20},{20,16},{24,28},{28,24},{1,5},{5... | collective-permute-start | bytes 196616 | tf_op jit(solution)/shard_map/ppermute | solution.py:254
  12.1 1.4 %collective-permute-start.3 = (bf16[128,256]{1,0:T(8,128)(2,1)S(1)}, bf16[128,256]{1,0:T(8,128)(2,1)S(1)}, u32[]{:S(2)}, u32[]{:S(2)}) collective-permute-start(bf16[128,256]{1,0:T(8,128)(2,1)S(1)} %collective-permute-done.2.refs_7_), channel_id=1, source_target_pairs={{0,4},{4,0},{8,12},{12,8},{16,20},{20,16},{24,28},{28,24},{1,5},{5... | collective-permute-start | bytes 196616 | tf_op jit(solution)/shard_map/ppermute | solution.py:254
  14.0 5.3 %collective-permute-start.12 = (bf16[128,256]{1,0:T(8,128)(2,1)S(1)}, bf16[128,256]{1,0:T(8,128)(2,1)S(1)}, u32[]{:S(2)}, u32[]{:S(2)}) collective-permute-start(bf16[128,256]{1,0:T(8,128)(2,1)S(1)} %shard_map.103.refs_0_), channel_id=1, source_target_pairs={{0,24},{1,25},{2,26},{3,27},{4,7},{5,6},{6,5},{7,4},{8,16},{9,17},... | collective-permute-start | bytes 196616 | tf_op jit(solution)/shard_map/ppermute | solution.py:278
  16.5 4.3 %collective-permute-start.11 = (bf16[128,256]{1,0:T(8,128)(2,1)S(1)}, bf16[128,256]{1,0:T(8,128)(2,1)S(1)}, u32[]{:S(2)}, u32[]{:S(2)}) collective-permute-start(bf16[128,256]{1,0:T(8,128)(2,1)S(1)} %shard_map.103.refs_0_), channel_id=1, source_target_pairs={{0,8},{1,9},{2,10},{3,11},{4,6},{5,7},{6,4},{7,5},{8,0},{9,1},{10,... | collective-permute-start | bytes 196616 | tf_op jit(solution)/shard_map/ppermute | solution.py:278
  17.1 4.3 %collective-permute-start.10 = (bf16[128,256]{1,0:T(8,128)(2,1)S(1)}, bf16[128,256]{1,0:T(8,128)(2,1)S(1)}, u32[]{:S(2)}, u32[]{:S(2)}) collective-permute-start(bf16[128,256]{1,0:T(8,128)(2,1)S(1)} %shard_map.103.refs_0_), channel_id=1, source_target_pairs={{0,16},{1,17},{2,18},{3,19},{4,5},{5,4},{6,7},{7,6},{8,24},{9,25},... | collective-permute-start | bytes 196616 | tf_op jit(solution)/shard_map/ppermute | solution.py:278
  17.9 7.4 %collective-permute-start.8 = (bf16[128,256]{1,0:T(8,128)(2,1)S(1)}, bf16[128,256]{1,0:T(8,128)(2,1)S(1)}, u32[]{:S(2)}, u32[]{:S(2)}) collective-permute-start(bf16[128,256]{1,0:T(8,128)(2,1)S(1)} %get-tuple-element.22), channel_id=1, source_target_pairs={{0,12},{4,8},{8,4},{12,0},{16,28},{20,24},{24,20},{28,16},{1,13},{... | collective-permute-start | bytes 196616 | tf_op jit(solution)/shard_map/ppermute | solution.py:254
  21.4 5.0 %collective-permute-start.16 = (bf16[128,256]{1,0:T(8,128)(2,1)S(1)}, bf16[128,256]{1,0:T(8,128)(2,1)S(1)}, u32[]{:S(2)}, u32[]{:S(2)}) collective-permute-start(bf16[128,256]{1,0:T(8,128)(2,1)S(1)} %shard_map.104), channel_id=1, source_target_pairs={{0,7},{1,6},{2,5},{3,4},{4,24},{5,25},{6,26},{7,27},{8,15},{9,14},... | collective-permute-start | bytes 196616 | tf_op jit(solution)/shard_map/ppermute | solution.py:265
  23.1 3.7 %collective-permute-start.15 = (bf16[128,256]{1,0:T(8,128)(2,1)S(1)}, bf16[128,256]{1,0:T(8,128)(2,1)S(1)}, u32[]{:S(2)}, u32[]{:S(2)}) collective-permute-start(bf16[128,256]{1,0:T(8,128)(2,1)S(1)} %shard_map.104), channel_id=1, source_target_pairs={{0,6},{1,7},{2,4},{3,5},{4,8},{5,9},{6,10},{7,11},{8,14},{9,15},{1... | collective-permute-start | bytes 196616 | tf_op jit(solution)/shard_map/ppermute | solution.py:265
  24.5 3.7 %collective-permute-start.14 = (bf16[128,256]{1,0:T(8,128)(2,1)S(1)}, bf16[128,256]{1,0:T(8,128)(2,1)S(1)}, u32[]{:S(2)}, u32[]{:S(2)}) collective-permute-start(bf16[128,256]{1,0:T(8,128)(2,1)S(1)} %shard_map.104), channel_id=1, source_target_pairs={{0,5},{1,4},{2,7},{3,6},{4,16},{5,17},{6,18},{7,19},{8,13},{9,12},... | collective-permute-start | bytes 196616 | tf_op jit(solution)/shard_map/ppermute | solution.py:265
  24.5 3.7 %collective-permute-start.13 = (bf16[128,256]{1,0:T(8,128)(2,1)S(1)}, bf16[128,256]{1,0:T(8,128)(2,1)S(1)}, u32[]{:S(2)}, u32[]{:S(2)}) collective-permute-start(bf16[128,256]{1,0:T(8,128)(2,1)S(1)} %shard_map.104), channel_id=1, source_target_pairs={{0,4},{4,0},{8,12},{12,8},{16,20},{20,16},{24,28},{28,24},{1,5},{5... | collective-permute-start | bytes 196616 | tf_op jit(solution)/shard_map/ppermute | solution.py:254
  25.3 3.6 %copy-start.2 = (bf16[256,256]{1,0:T(8,128)(2,1)S(1)}, bf16[256,256]{1,0:T(8,128)(2,1)}, u32[]{:S(2)}) copy-start(bf16[256,256]{1,0:T(8,128)(2,1)} %weight.1) | copy-start | bytes 393220
  25.3 3.6 %collective-permute-start.9 = (bf16[64,256]{1,0:T(8,128)(2,1)S(1)}, bf16[64,256]{1,0:T(8,128)(2,1)S(1)}, u32[]{:S(2)}, u32[]{:S(2)}) collective-permute-start(bf16[64,256]{1,0:T(8,128)(2,1)S(1)} %get-tuple-element.24), channel_id=1, source_target_pairs={{0,20},{4,16},{8,28},{12,24},{16,4},{20,0},{24,12},{28,8},{1,21},{... | collective-permute-start | bytes 98312 | tf_op jit(solution)/shard_map/ppermute | solution.py:254
  28.3 1.6 %collective-permute-start.17 = (f32[128,256]{1,0:T(8,128)S(1)}, f32[128,256]{1,0:T(8,128)S(1)}, u32[]{:S(2)}, u32[]{:S(2)}) collective-permute-start(f32[128,256]{1,0:T(8,128)S(1)} %shard_map.105.own), channel_id=1, source_target_pairs={{0,4},{4,0},{8,12},{12,8},{16,20},{20,16},{24,28},{28,24},{1,5},{5... | collective-permute-start | bytes 393224 | tf_op jit(solution)/shard_map/ppermute | solution.py:254

commit v10 on v8

--- a/solution.py
+++ b/solution.py
@@ -22,14 +22,18 @@
     return k & ~3 | (k & 1) << 1 | (k >> 1) & 1
 
 
-def call(body, outs, ins, spaces=None, limit=8 * 2**20, flops=0, scratch=(), out_space=VMEM):
+def call(
+    body, outs, ins, spaces=None, limit=8 * 2**20, flops=0, scratch=(), out_spaces=None, alias=None
+):
+    out_spaces = out_spaces or [VMEM] * len(outs)
     spaces = spaces or [VMEM] * len(ins)
     moved = sum(x.size * x.dtype.itemsize for x in list(ins) + list(outs))
     return pl.pallas_call(
         body,
         out_shape=outs,
         in_specs=[pl.BlockSpec(memory_space=s) for s in spaces],
-        out_specs=[pl.BlockSpec(memory_space=out_space) for _ in outs],
+        out_specs=[pl.BlockSpec(memory_space=s) for s in out_spaces],
+        input_output_aliases=alias or {},
         scratch_shapes=list(scratch),
         compiler_params=pltpu.CompilerParams(vmem_limit_bytes=limit),
         cost_estimate=pl.CostEstimate(flops=flops, bytes_accessed=moved, transcendentals=0),
@@ -192,8 +196,9 @@
     out[...] = tree([t[...].astype(jnp.float32) for t in terms]).astype(jnp.bfloat16)
 
 
-def finish_features(kept, received, scale, weight, out, token):
-    token[...] = jnp.zeros_like(token)
+def finish_features(kept, received, scale, weight, own_half, out, placed, sem):
+    copy = half_copy(0, own_half, placed, sem)
+    copy.start()
     total = (kept[...] + received[...].astype(jnp.float32)) * scale[...]
     high = total.astype(jnp.bfloat16)
     low = (total - high.astype(jnp.float32)).astype(jnp.bfloat16)
@@ -201,6 +206,7 @@
     w = weight[...]
     out[...] = lax.dot_general(high, w, last, preferred_element_type=jnp.float32)
     out[...] += lax.dot_general(low, w, last, preferred_element_type=jnp.float32)
+    copy.wait()
 
 
 def finish_weight(factor, *refs):
@@ -208,19 +214,17 @@
     out[...] = tree([t[...].astype(jnp.float32) for t in terms]) * factor
 
 
-def join(after, own, other, out, sems):
-    rows = own.shape[0]
-    core = positions()[1]
-    copies = [
-        pltpu.make_async_copy(
-            part, out.at[pl.ds(pl.multiple_of(at * rows, rows), rows)], sems.at[n]
-        )
-        for n, (at, part) in enumerate(((core, own), (1 - core, other)))
-    ]
-    for c in copies:
-        c.start()
-    for c in copies:
-        c.wait()
+def half_copy(whose, part, out, sem):
+    rows = part.shape[0]
+    core = positions()[1]
+    at = (1 - core if whose else core) * rows
+    return pltpu.make_async_copy(part, out.at[pl.ds(pl.multiple_of(at, rows), rows)], sem)
+
+
+def join(held, other, out, sem):
+    copy = half_copy(1, other, out, sem)
+    copy.start()
+    copy.wait()
 
 
 def local(features, grad_out, relu_mask, degree, weight, adjacency, block_slot, block_count):
@@ -319,12 +323,6 @@
             [kept, received],
         )
     received = swap(leaving, CORES * bit + 1)
-    grad_features, token = call(
-        finish_features,
-        [shape((nodes, width), f32), shape((8, 128), f32)],
-        [kept, received, scale, weight],
-        flops=HEAVY,
-    )
     (once,) = call(sum_parts, [shape((half, width), bf16)], [leave] + along(leave))
     factor = (nodes * rows * cols) ** (-0.5)
     (own_half,) = call(
@@ -332,9 +330,17 @@
         [shape((half, width), f32)],
         [partner(once)] + spread(once),
     )
+    sem = [pltpu.SemaphoreType.DMA]
+    full = shape((width, width), f32)
+    grad_features, placed = call(
+        finish_features,
+        [shape((nodes, width), f32), full],
+        [kept, received, scale, weight, own_half],
+        flops=HEAVY, scratch=sem, out_spaces=[VMEM, pl.ANY],
+    )
     (weight_grad,) = call(
-        join, [shape((width, width), f32)], [token, own_half, partner(own_half)],
-        scratch=[pltpu.SemaphoreType.DMA((2,))], out_space=pl.ANY,
+        join, [full], [placed, partner(own_half)], [pl.ANY, VMEM],
+        scratch=sem, out_spaces=[pl.ANY], alias={0: 0},
     )
     return grad_features, weight_grad
 

time: 30.6 us -> 31.1 us (1.016)
  transfers between devices with their start and end apart: 17 -> 17, of which waited for: 8 -> 8; matrix products, arithmetic and copies ran while one was open for 0% -> 0% of each run, Pallas kernels for 7% -> 8%
where the time goes in v10:
time: 31.1 us; the launch traced here: 31 us
  starting transfers between devices  17.6 us (57%)
  waiting for transfers between devices  7.44 us (24%)
  Pallas kernels  4.55 us (15%)
  between operations  1.39 us (4%)
    ppermute x6, starting transfers between devices, along(): out.append(lax.ppermute(x, ('row', 'col'), pairs))  8.06 us
    ppermute x8, starting transfers between devices, swap(): return lax.ppermute(x, 'row', [(d, d ^ k) for d in range(rows)])  6.07 us
    pallas_call x11, Pallas kernels, call(): pl.pallas_call(body, out_shape=outs, in_specs=[pl.BlockSpec(memory_space=...  4.55 us
    ppermute x6, waiting for transfers between devices, along(): out.append(lax.ppermute(x, ('row', 'col'), pairs))  3.96 us
    ppermute x3, starting transfers between devices, cross(): return lax.ppermute(x, ('row', 'col'), pairs)  3.47 us
    ppermute x3, waiting for transfers between devices, cross(): return lax.ppermute(x, ('row', 'col'), pairs)  1.84 us
    ppermute x8, waiting for transfers between devices, swap(): return lax.ppermute(x, 'row', [(d, d ^ k) for d in range(rows)])  1.64 us
  transfers between devices with their start and end apart: 17, of which 8 were waited for; matrix products, arithmetic and copies ran while one was open for 0% of the time, Pallas kernels for 8%

profile of v10, /device:TPU:0, one launch (start us, length us, event | category | flops | bytes accessed | tf_op | source)
XLA Modules:
  0.0 31.0 jit_solution(5443970598594647176)
XLA Ops:
  0.6 0.0 copy-start
  0.6 1.0 %shard_map.95 = (bf16[128,256]{1,0:T(8,128)(2,1)S(1)}, f32[64,1]{1,0:T(8,128)S(1)}) custom-call(bf16[64,256]{1,0:T(8,128)(2,1)} %features.1, bf16[64,256]{1,0:T(8,128)(2,1)} %grad_out.1, s32[64,256]{1,0:T(8,128)} %relu_mask.1, s32[1,64]{1,0:T(1,128)} %bitcast.1), custom_call_target="tpu_custom_call" | custom-call | bytes 197120 | tf_op jit(solution)/shard_map/pallas_call | solution.py:31
  1.6 0.5 %collective-permute-start = (bf16[128,256]{1,0:T(8,128)(2,1)S(1)}, bf16[128,256]{1,0:T(8,128)(2,1)S(1)}, u32[]{:S(2)}, u32[]{:S(2)}) collective-permute-start(bf16[128,256]{1,0:T(8,128)(2,1)S(1)} %get-tuple-element.12.scaled), channel_id=1, source_target_pairs={{0,4},{4,0},{8,12},{12,8},{16,20},{20,16},{24,28},{28,24},{1,5},{5... | collective-permute-start | bytes 196616 | tf_op jit(solution)/shard_map/ppermute | solution.py:241
  2.8 0.3 collective-permute-done.other
  3.1 0.0 copy-start.1
  3.1 3.9 %collective-permute-start.5 = (bf16[128,256]{1,0:T(8,128)(2,1)S(1)}, bf16[128,256]{1,0:T(8,128)(2,1)S(1)}, u32[]{:S(2)}, u32[]{:S(2)}) collective-permute-start(bf16[128,256]{1,0:T(8,128)(2,1)S(1)} %get-tuple-element.13.after.refs_2_), channel_id=1, source_target_pairs={{0,24},{1,25},{2,26},{3,27},{4,7},{5,6},{6,5},{7,4},{8,16},{9,17},... | collective-permute-start | bytes 196616 | tf_op jit(solution)/shard_map/ppermute | solution.py:265
  6.9 0.5 %collective-permute-start.4 = (bf16[128,256]{1,0:T(8,128)(2,1)S(1)}, bf16[128,256]{1,0:T(8,128)(2,1)S(1)}, u32[]{:S(2)}, u32[]{:S(2)}) collective-permute-start(bf16[128,256]{1,0:T(8,128)(2,1)S(1)} %get-tuple-element.13.after.refs_2_), channel_id=1, source_target_pairs={{0,8},{1,9},{2,10},{3,11},{4,6},{5,7},{6,4},{7,5},{8,0},{9,1},{10,... | collective-permute-start | bytes 196616 | tf_op jit(solution)/shard_map/ppermute | solution.py:265
  7.5 0.1 collective-permute-start.2
  7.6 0.0 copy-done
  7.6 0.0 copy-done.1
  7.6 0.6 %shard_map.97.refs_2_.refs_0_ = bf16[512,256]{1,0:T(8,128)(2,1)S(1)} custom-call(bf16[1,1,6,128,128]{4,3,2,1,0:T(8,128)(2,1)S(1)} %copy-done, s32[1,1,6]{2,1,0:T(1,128)S(1)} %copy-done.1, s32[1,1]{1,0:T(1,128)S(6)} %copy.12.count, bf16[128,256]{1,0:T(8,128)(2,1)S(1)} %get-tuple-element.13.after.refs_2_), custom_call_target="tpu_custom_call" | custom-call | bytes 524316 | tf_op jit(solution)/shard_map/pallas_call | solution.py:31
  8.2 1.1 %collective-permute-start.1 = (bf16[512,256]{1,0:T(8,128)(2,1)S(1)}, bf16[512,256]{1,0:T(8,128)(2,1)S(1)}, u32[]{:S(2)}, u32[]{:S(2)}) collective-permute-start(bf16[512,256]{1,0:T(8,128)(2,1)S(1)} %shard_map.97.refs_2_.refs_0_), channel_id=1, source_target_pairs={{0,4},{4,0},{8,12},{12,8},{16,20},{20,16},{24,28},{28,24},{1,5},{5... | collective-permute-start | bytes 786440 | tf_op jit(solution)/shard_map/ppermute | solution.py:241
  9.3 0.0 collective-permute-done.5.refs_1_.refs_8_
  9.3 1.9 %collective-permute-done.4.refs_0_.refs_7_ = bf16[128,256]{1,0:T(8,128)(2,1)S(1)} collective-permute-done((bf16[128,256]{1,0:T(8,128)(2,1)S(1)}, bf16[128,256]{1,0:T(8,128)(2,1)S(1)}, u32[]{:S(2)}, u32[]{:S(2)}) %collective-permute-start.4) | collective-permute-done | bytes 65568 | tf_op jit(solution)/shard_map/ppermute | solution.py:265
  11.2 0.8 %collective-permute-start.6 = (bf16[256,256]{1,0:T(8,128)(2,1)S(1)}, bf16[256,256]{1,0:T(8,128)(2,1)S(1)}, u32[]{:S(2)}, u32[]{:S(2)}) collective-permute-start(bf16[256,256]{1,0:T(8,128)(2,1)S(1)} %shard_map.98), channel_id=1, source_target_pairs={{0,4},{4,0},{8,12},{12,8},{16,20},{20,16},{24,28},{28,24},{1,5},{5... | collective-permute-start | bytes 393224 | tf_op jit(solution)/shard_map/ppermute | solution.py:241
  12.1 0.0 collective-permute-done.2.refs_6_
  12.1 0.1 collective-permute-start.3
  12.1 1.2 %collective-permute-done.3.refs_4_ = bf16[128,256]{1,0:T(8,128)(2,1)S(1)} collective-permute-done((bf16[128,256]{1,0:T(8,128)(2,1)S(1)}, bf16[128,256]{1,0:T(8,128)(2,1)S(1)}, u32[]{:S(2)}, u32[]{:S(2)}) %collective-permute-start.3) | collective-permute-done | bytes 65568 | tf_op jit(solution)/shard_map/ppermute | solution.py:241
  13.3 0.0 collective-permute-done.6.refs_5_
  13.3 0.0 collective-permute-done.1.refs_1_
  13.3 0.5 %shard_map.101.refs_0_ = bf16[128,256]{1,0:T(8,128)(2,1)S(1)} custom-call(bf16[512,256]{1,0:T(8,128)(2,1)S(1)} %shard_map.97.refs_2_.refs_0_, bf16[512,256]{1,0:T(8,128)(2,1)S(1)} %collective-permute-done.1.refs_1_, bf16[128,256]{1,0:T(8,128)(2,1)S(1)} %get-tuple-element.13.after.refs_2_, bf16[128,256]{1,0:T(8,128)(2,1)S(1)} %get-tuple-element.14.refs_3_, ...), custom_call_target="tpu_custom_call" | custom-call | flops 134217728 | bytes 1114112 | tf_op jit(solution)/shard_map/pallas_call | solution.py:31
  13.8 2.5 %collective-permute-start.11 = (bf16[128,256]{1,0:T(8,128)(2,1)S(1)}, bf16[128,256]{1,0:T(8,128)(2,1)S(1)}, u32[]{:S(2)}, u32[]{:S(2)}) collective-permute-start(bf16[128,256]{1,0:T(8,128)(2,1)S(1)} %shard_map.101.refs_0_), channel_id=1, source_target_pairs={{0,24},{1,25},{2,26},{3,27},{4,7},{5,6},{6,5},{7,4},{8,16},{9,17},... | collective-permute-start | bytes 196616 | tf_op jit(solution)/shard_map/ppermute | solution.py:265
  16.3 0.5 %collective-permute-start.10 = (bf16[128,256]{1,0:T(8,128)(2,1)S(1)}, bf16[128,256]{1,0:T(8,128)(2,1)S(1)}, u32[]{:S(2)}, u32[]{:S(2)}) collective-permute-start(bf16[128,256]{1,0:T(8,128)(2,1)S(1)} %shard_map.101.refs_0_), channel_id=1, source_target_pairs={{0,8},{1,9},{2,10},{3,11},{4,6},{5,7},{6,4},{7,5},{8,0},{9,1},{10,... | collective-permute-start | bytes 196616 | tf_op jit(solution)/shard_map/ppermute | solution.py:265
  16.8 0.5 %collective-permute-start.9 = (bf16[128,256]{1,0:T(8,128)(2,1)S(1)}, bf16[128,256]{1,0:T(8,128)(2,1)S(1)}, u32[]{:S(2)}, u32[]{:S(2)}) collective-permute-start(bf16[128,256]{1,0:T(8,128)(2,1)S(1)} %shard_map.101.refs_0_), channel_id=1, source_target_pairs={{0,16},{1,17},{2,18},{3,19},{4,5},{5,4},{6,7},{7,6},{8,24},{9,25},... | collective-permute-start | bytes 196616 | tf_op jit(solution)/shard_map/ppermute | solution.py:265
  17.4 0.3 shard_map.99
  17.7 1.4 %collective-permute-start.7 = (bf16[128,256]{1,0:T(8,128)(2,1)S(1)}, bf16[128,256]{1,0:T(8,128)(2,1)S(1)}, u32[]{:S(2)}, u32[]{:S(2)}) collective-permute-start(bf16[128,256]{1,0:T(8,128)(2,1)S(1)} %get-tuple-element.16), channel_id=1, source_target_pairs={{0,12},{4,8},{8,4},{12,0},{16,28},{20,24},{24,20},{28,16},{1,13},{... | collective-permute-start | bytes 196616 | tf_op jit(solution)/shard_map/ppermute | solution.py:241
  19.1 0.0 collective-permute-done.11.refs_3_
  19.1 1.5 %collective-permute-done.10.refs_2_ = bf16[128,256]{1,0:T(8,128)(2,1)S(1)} collective-permute-done((bf16[128,256]{1,0:T(8,128)(2,1)S(1)}, bf16[128,256]{1,0:T(8,128)(2,1)S(1)}, u32[]{:S(2)}, u32[]{:S(2)}) %collective-permute-start.10) | collective-permute-done | bytes 65568 | tf_op jit(solution)/shard_map/ppermute | solution.py:265
  20.6 0.5 %collective-permute-done.9.refs_1_ = bf16[128,256]{1,0:T(8,128)(2,1)S(1)} collective-permute-done((bf16[128,256]{1,0:T(8,128)(2,1)S(1)}, bf16[128,256]{1,0:T(8,128)(2,1)S(1)}, u32[]{:S(2)}, u32[]{:S(2)}) %collective-permute-start.9) | collective-permute-done | bytes 65568 | tf_op jit(solution)/shard_map/ppermute | solution.py:265
  21.1 1.9 %collective-permute-start.15 = (bf16[128,256]{1,0:T(8,128)(2,1)S(1)}, bf16[128,256]{1,0:T(8,128)(2,1)S(1)}, u32[]{:S(2)}, u32[]{:S(2)}) collective-permute-start(bf16[128,256]{1,0:T(8,128)(2,1)S(1)} %shard_map.102), channel_id=1, source_target_pairs={{0,7},{1,6},{2,5},{3,4},{4,24},{5,25},{6,26},{7,27},{8,15},{9,14},... | collective-permute-start | bytes 196616 | tf_op jit(solution)/shard_map/ppermute | solution.py:252
  23.0 1.6 %collective-permute-start.14 = (bf16[128,256]{1,0:T(8,128)(2,1)S(1)}, bf16[128,256]{1,0:T(8,128)(2,1)S(1)}, u32[]{:S(2)}, u32[]{:S(2)}) collective-permute-start(bf16[128,256]{1,0:T(8,128)(2,1)S(1)} %shard_map.102), channel_id=1, source_target_pairs={{0,6},{1,7},{2,4},{3,5},{4,8},{5,9},{6,10},{7,11},{8,14},{9,15},{1... | collective-permute-start | bytes 196616 | tf_op jit(solution)/shard_map/ppermute | solution.py:252
  24.6 0.0 collective-permute-start.13
  24.6 0.7 %collective-permute-start.12 = (bf16[128,256]{1,0:T(8,128)(2,1)S(1)}, bf16[128,256]{1,0:T(8,128)(2,1)S(1)}, u32[]{:S(2)}, u32[]{:S(2)}) collective-permute-start(bf16[128,256]{1,0:T(8,128)(2,1)S(1)} %shard_map.102), channel_id=1, source_target_pairs={{0,4},{4,0},{8,12},{12,8},{16,20},{20,16},{24,28},{28,24},{1,5},{5... | collective-permute-start | bytes 196616 | tf_op jit(solution)/shard_map/ppermute | solution.py:241
  25.3 0.0 collective-permute-done.7.received
  25.3 0.0 copy-start.2
  25.3 1.1 %collective-permute-start.8 = (bf16[64,256]{1,0:T(8,128)(2,1)S(1)}, bf16[64,256]{1,0:T(8,128)(2,1)S(1)}, u32[]{:S(2)}, u32[]{:S(2)}) collective-permute-start(bf16[64,256]{1,0:T(8,128)(2,1)S(1)} %get-tuple-element.18), channel_id=1, source_target_pairs={{0,20},{4,16},{8,28},{12,24},{16,4},{20,0},{24,12},{28,8},{1,21},{... | collective-permute-start | bytes 98312 | tf_op jit(solution)/shard_map/ppermute | solution.py:241
  26.5 0.0 collective-permute-done.15.refs_3_
  26.5 0.2 collective-permute-done.14.refs_2_
  26.7 1.6 %collective-permute-done.13.refs_1_ = bf16[128,256]{1,0:T(8,128)(2,1)S(1)} collective-permute-done((bf16[128,256]{1,0:T(8,128)(2,1)S(1)}, bf16[128,256]{1,0:T(8,128)(2,1)S(1)}, u32[]{:S(2)}, u32[]{:S(2)}) %collective-permute-start.13) | collective-permute-done | bytes 65568 | tf_op jit(solution)/shard_map/ppermute | solution.py:252
  28.3 0.0 collective-permute-done.12.refs_0_
  28.4 0.3 %collective-permute-start.16 = (f32[128,256]{1,0:T(8,128)S(1)}, f32[128,256]{1,0:T(8,128)S(1)}, u32[]{:S(2)}, u32[]{:S(2)}) collective-permute-start(f32[128,256]{1,0:T(8,128)S(1)} %shard_map.103.own_half), channel_id=1, source_target_pairs={{0,4},{4,0},{8,12},{12,8},{16,20},{20,16},{24,28},{28,24},{1,5},{5... | collective-permute-start | bytes 393224 | tf_op jit(solution)/shard_map/ppermute | solution.py:241
  28.7 0.2 collective-permute-done.8.received
  28.9 0.0 copy-done.2
  28.9 1.4 %shard_map.104 = (f32[64,256]{1,0:T(8,128)}, f32[256,256]{1,0:T(8,128)}) custom-call(f32[64,256]{1,0:T(8,128)S(1)} %get-tuple-element.17.kept, bf16[64,256]{1,0:T(8,128)(2,1)S(1)} %collective-permute-done.8.received, f32[64,1]{1,0:T(8,128)S(1)} %get-tuple-element.19.scale, bf16[256,256]{1,0:T(8,128)(2,1)S(1)} %copy-done.2, f32[128,256]{1,0:T(8,128)S(1)} %shard_map.103.own_half), custom_call_target="tpu_custom_call" | custom-call | flops 4000000000 | bytes 688384 | tf_op jit(solution)/shard_map/pallas_call | solution.py:31
  30.3 0.0 collective-permute-done.16.other
  30.3 0.7 %shard_map.105 = f32[256,256]{1,0:T(8,128)} custom-call(f32[256,256]{1,0:T(8,128)} %get-tuple-element.21.held, f32[128,256]{1,0:T(8,128)S(1)} %collective-permute-done.16.other), custom_call_target="tpu_custom_call", output_to_operand_aliasing={{}: (0, {})} | custom-call | bytes 655360 | tf_op jit(solution)/shard_map/pallas_call | solution.py:31
  (5 shorter events, 0.1 us)
Async XLA Ops:
  0.6 6.9 %copy-start = (bf16[1,1,6,128,128]{4,3,2,1,0:T(8,128)(2,1)S(1)}, bf16[1,1,6,128,128]{4,3,2,1,0:T(8,128)(2,1)}, u32[]{:S(2)}) copy-start(bf16[1,1,6,128,128]{4,3,2,1,0:T(8,128)(2,1)} %blocks.1) | copy-start | bytes 589828
  1.6 1.4 %collective-permute-start = (bf16[128,256]{1,0:T(8,128)(2,1)S(1)}, bf16[128,256]{1,0:T(8,128)(2,1)S(1)}, u32[]{:S(2)}, u32[]{:S(2)}) collective-permute-start(bf16[128,256]{1,0:T(8,128)(2,1)S(1)} %get-tuple-element.12.scaled), channel_id=1, source_target_pairs={{0,4},{4,0},{8,12},{12,8},{16,20},{20,16},{24,28},{28,24},{1,5},{5... | collective-permute-start | bytes 196616 | tf_op jit(solution)/shard_map/ppermute | solution.py:241
  3.1 4.5 %copy-start.1 = (s32[1,1,6]{2,1,0:T(1,128)S(1)}, s32[1,1,6]{2,1,0:T(1,128)}, u32[]{:S(2)}) copy-start(s32[1,1,6]{2,1,0:T(1,128)} %slots.1) | copy-start | bytes 76
  3.1 6.2 %collective-permute-start.5 = (bf16[128,256]{1,0:T(8,128)(2,1)S(1)}, bf16[128,256]{1,0:T(8,128)(2,1)S(1)}, u32[]{:S(2)}, u32[]{:S(2)}) collective-permute-start(bf16[128,256]{1,0:T(8,128)(2,1)S(1)} %get-tuple-element.13.after.refs_2_), channel_id=1, source_target_pairs={{0,24},{1,25},{2,26},{3,27},{4,7},{5,6},{6,5},{7,4},{8,16},{9,17},... | collective-permute-start | bytes 196616 | tf_op jit(solution)/shard_map/ppermute | solution.py:265
  6.9 4.3 %collective-permute-start.4 = (bf16[128,256]{1,0:T(8,128)(2,1)S(1)}, bf16[128,256]{1,0:T(8,128)(2,1)S(1)}, u32[]{:S(2)}, u32[]{:S(2)}) collective-permute-start(bf16[128,256]{1,0:T(8,128)(2,1)S(1)} %get-tuple-element.13.after.refs_2_), channel_id=1, source_target_pairs={{0,8},{1,9},{2,10},{3,11},{4,6},{5,7},{6,4},{7,5},{8,0},{9,1},{10,... | collective-permute-start | bytes 196616 | tf_op jit(solution)/shard_map/ppermute | solution.py:265
  7.5 4.6 %collective-permute-start.2 = (bf16[128,256]{1,0:T(8,128)(2,1)S(1)}, bf16[128,256]{1,0:T(8,128)(2,1)S(1)}, u32[]{:S(2)}, u32[]{:S(2)}) collective-permute-start(bf16[128,256]{1,0:T(8,128)(2,1)S(1)} %get-tuple-element.13.after.refs_2_), channel_id=1, source_target_pairs={{0,16},{1,17},{2,18},{3,19},{4,5},{5,4},{6,7},{7,6},{8,24},{9,25},... | collective-permute-start | bytes 196616 | tf_op jit(solution)/shard_map/ppermute | solution.py:265
  8.2 5.1 %collective-permute-start.1 = (bf16[512,256]{1,0:T(8,128)(2,1)S(1)}, bf16[512,256]{1,0:T(8,128)(2,1)S(1)}, u32[]{:S(2)}, u32[]{:S(2)}) collective-permute-start(bf16[512,256]{1,0:T(8,128)(2,1)S(1)} %shard_map.97.refs_2_.refs_0_), channel_id=1, source_target_pairs={{0,4},{4,0},{8,12},{12,8},{16,20},{20,16},{24,28},{28,24},{1,5},{5... | collective-permute-start | bytes 786440 | tf_op jit(solution)/shard_map/ppermute | solution.py:241
  11.2 2.1 %collective-permute-start.6 = (bf16[256,256]{1,0:T(8,128)(2,1)S(1)}, bf16[256,256]{1,0:T(8,128)(2,1)S(1)}, u32[]{:S(2)}, u32[]{:S(2)}) collective-permute-start(bf16[256,256]{1,0:T(8,128)(2,1)S(1)} %shard_map.98), channel_id=1, source_target_pairs={{0,4},{4,0},{8,12},{12,8},{16,20},{20,16},{24,28},{28,24},{1,5},{5... | collective-permute-start | bytes 393224 | tf_op jit(solution)/shard_map/ppermute | solution.py:241
  12.1 1.3 %collective-permute-start.3 = (bf16[128,256]{1,0:T(8,128)(2,1)S(1)}, bf16[128,256]{1,0:T(8,128)(2,1)S(1)}, u32[]{:S(2)}, u32[]{:S(2)}) collective-permute-start(bf16[128,256]{1,0:T(8,128)(2,1)S(1)} %collective-permute-done.2.refs_6_), channel_id=1, source_target_pairs={{0,4},{4,0},{8,12},{12,8},{16,20},{20,16},{24,28},{28,24},{1,5},{5... | collective-permute-start | bytes 196616 | tf_op jit(solution)/shard_map/ppermute | solution.py:241
  13.8 5.3 %collective-permute-start.11 = (bf16[128,256]{1,0:T(8,128)(2,1)S(1)}, bf16[128,256]{1,0:T(8,128)(2,1)S(1)}, u32[]{:S(2)}, u32[]{:S(2)}) collective-permute-start(bf16[128,256]{1,0:T(8,128)(2,1)S(1)} %shard_map.101.refs_0_), channel_id=1, source_target_pairs={{0,24},{1,25},{2,26},{3,27},{4,7},{5,6},{6,5},{7,4},{8,16},{9,17},... | collective-permute-start | bytes 196616 | tf_op jit(solution)/shard_map/ppermute | solution.py:265
  16.3 4.3 %collective-permute-start.10 = (bf16[128,256]{1,0:T(8,128)(2,1)S(1)}, bf16[128,256]{1,0:T(8,128)(2,1)S(1)}, u32[]{:S(2)}, u32[]{:S(2)}) collective-permute-start(bf16[128,256]{1,0:T(8,128)(2,1)S(1)} %shard_map.101.refs_0_), channel_id=1, source_target_pairs={{0,8},{1,9},{2,10},{3,11},{4,6},{5,7},{6,4},{7,5},{8,0},{9,1},{10,... | collective-permute-start | bytes 196616 | tf_op jit(solution)/shard_map/ppermute | solution.py:265
  16.8 4.3 %collective-permute-start.9 = (bf16[128,256]{1,0:T(8,128)(2,1)S(1)}, bf16[128,256]{1,0:T(8,128)(2,1)S(1)}, u32[]{:S(2)}, u32[]{:S(2)}) collective-permute-start(bf16[128,256]{1,0:T(8,128)(2,1)S(1)} %shard_map.101.refs_0_), channel_id=1, source_target_pairs={{0,16},{1,17},{2,18},{3,19},{4,5},{5,4},{6,7},{7,6},{8,24},{9,25},... | collective-permute-start | bytes 196616 | tf_op jit(solution)/shard_map/ppermute | solution.py:265
  17.7 7.6 %collective-permute-start.7 = (bf16[128,256]{1,0:T(8,128)(2,1)S(1)}, bf16[128,256]{1,0:T(8,128)(2,1)S(1)}, u32[]{:S(2)}, u32[]{:S(2)}) collective-permute-start(bf16[128,256]{1,0:T(8,128)(2,1)S(1)} %get-tuple-element.16), channel_id=1, source_target_pairs={{0,12},{4,8},{8,4},{12,0},{16,28},{20,24},{24,20},{28,16},{1,13},{... | collective-permute-start | bytes 196616 | tf_op jit(solution)/shard_map/ppermute | solution.py:241
  21.1 5.3 %collective-permute-start.15 = (bf16[128,256]{1,0:T(8,128)(2,1)S(1)}, bf16[128,256]{1,0:T(8,128)(2,1)S(1)}, u32[]{:S(2)}, u32[]{:S(2)}) collective-permute-start(bf16[128,256]{1,0:T(8,128)(2,1)S(1)} %shard_map.102), channel_id=1, source_target_pairs={{0,7},{1,6},{2,5},{3,4},{4,24},{5,25},{6,26},{7,27},{8,15},{9,14},... | collective-permute-start | bytes 196616 | tf_op jit(solution)/shard_map/ppermute | solution.py:252
  23.0 3.7 %collective-permute-start.14 = (bf16[128,256]{1,0:T(8,128)(2,1)S(1)}, bf16[128,256]{1,0:T(8,128)(2,1)S(1)}, u32[]{:S(2)}, u32[]{:S(2)}) collective-permute-start(bf16[128,256]{1,0:T(8,128)(2,1)S(1)} %shard_map.102), channel_id=1, source_target_pairs={{0,6},{1,7},{2,4},{3,5},{4,8},{5,9},{6,10},{7,11},{8,14},{9,15},{1... | collective-permute-start | bytes 196616 | tf_op jit(solution)/shard_map/ppermute | solution.py:252
  24.6 3.7 %collective-permute-start.13 = (bf16[128,256]{1,0:T(8,128)(2,1)S(1)}, bf16[128,256]{1,0:T(8,128)(2,1)S(1)}, u32[]{:S(2)}, u32[]{:S(2)}) collective-permute-start(bf16[128,256]{1,0:T(8,128)(2,1)S(1)} %shard_map.102), channel_id=1, source_target_pairs={{0,5},{1,4},{2,7},{3,6},{4,16},{5,17},{6,18},{7,19},{8,13},{9,12},... | collective-permute-start | bytes 196616 | tf_op jit(solution)/shard_map/ppermute | solution.py:252
  24.6 3.7 %collective-permute-start.12 = (bf16[128,256]{1,0:T(8,128)(2,1)S(1)}, bf16[128,256]{1,0:T(8,128)(2,1)S(1)}, u32[]{:S(2)}, u32[]{:S(2)}) collective-permute-start(bf16[128,256]{1,0:T(8,128)(2,1)S(1)} %shard_map.102), channel_id=1, source_target_pairs={{0,4},{4,0},{8,12},{12,8},{16,20},{20,16},{24,28},{28,24},{1,5},{5... | collective-permute-start | bytes 196616 | tf_op jit(solution)/shard_map/ppermute | solution.py:241
  25.3 3.6 %copy-start.2 = (bf16[256,256]{1,0:T(8,128)(2,1)S(1)}, bf16[256,256]{1,0:T(8,128)(2,1)}, u32[]{:S(2)}) copy-start(bf16[256,256]{1,0:T(8,128)(2,1)} %weight.1) | copy-start | bytes 393220
  25.3 3.6 %collective-permute-start.8 = (bf16[64,256]{1,0:T(8,128)(2,1)S(1)}, bf16[64,256]{1,0:T(8,128)(2,1)S(1)}, u32[]{:S(2)}, u32[]{:S(2)}) collective-permute-start(bf16[64,256]{1,0:T(8,128)(2,1)S(1)} %get-tuple-element.18), channel_id=1, source_target_pairs={{0,20},{4,16},{8,28},{12,24},{16,4},{20,0},{24,12},{28,8},{1,21},{... | collective-permute-start | bytes 98312 | tf_op jit(solution)/shard_map/ppermute | solution.py:241
  28.4 1.9 %collective-permute-start.16 = (f32[128,256]{1,0:T(8,128)S(1)}, f32[128,256]{1,0:T(8,128)S(1)}, u32[]{:S(2)}, u32[]{:S(2)}) collective-permute-start(f32[128,256]{1,0:T(8,128)S(1)} %shard_map.103.own_half), channel_id=1, source_target_pairs={{0,4},{4,0},{8,12},{12,8},{16,20},{20,16},{24,28},{28,24},{1,5},{5... | collective-permute-start | bytes 393224 | tf_op jit(solution)/shard_map/ppermute | solution.py:241
